TPU v7x, 256 devices: a whole 4x4x8 slice. The times are simulated.
256 devices in a mesh: ctx: 16 (over z, x_hi), tp: 4 (over y), dp: 4 (over x_lo, core).
Axes of the slice: x: 4 (x_hi: 2, x_lo: 2; x = x_hi * 2 + x_lo), y: 4, z: 8, core: 2. Of those that a mesh axis runs over, the one named last changes fastest.
Arguments:
- q_raw: bfloat16 [4, 4096, 4096], P('dp', 'ctx', 'tp'), may hold values from -6 to 6
- k_raw: bfloat16 [4, 4096, 4096], P('dp', 'ctx', 'tp'), may hold values from -6 to 6
- values: bfloat16 [4, 4096, 4096], P('dp', 'ctx', 'tp'), may hold values from -6 to 6
- d_out: bfloat16 [4, 4096, 4096], P('dp', 'ctx', 'tp'), may hold values from -6 to 6
- q_gain: float32 [32, 128], P('tp'), may hold values from 0.5 to 6
- k_gain: float32 [32, 128], P('tp'), may hold values from 0.5 to 6
- q_weight: bfloat16 [4096, 4096], P(None, 'tp'), may hold values from -0.09375 to 0.09375
- doc_lengths: int32 [4, 8], P('dp'), may hold values from 1 to 3840, as said below
Outputs:
- input_grad: bfloat16 [4, 4096, 4096], P('dp', 'ctx', 'tp')
- key_grad: bfloat16 [4, 4096, 4096], P('dp', 'ctx', 'tp')
- value_grad: bfloat16 [4, 4096, 4096], P('dp', 'ctx', 'tp')
- q_gain_grad: float32 [32, 128], P('tp')
- k_gain_grad: float32 [32, 128], P('tp')
Inputs may be any that keep to these rules, and one draw needn't show every extreme that they name: `doc_lengths`: each sequence's lengths sum to 4096.
All inputs are finite; a program needn't handle non-finite values.
Results may differ from a plain program's by a relative error of at most 0.02.
The roundings to bfloat16 on the way count: a program that leaves them out, or rounds other values in their place, can miss the bound.
Values may be sent and summed in bfloat16 or wider, within the bound.
No kernel may reach another device: no remote copies, remote signals or barrier semaphores. Data moves between devices by JAX's collectives and lax.ppermute only.
A program may use at most 128 MiB of HBM per device.

v0:
```python
import jax
import jax.numpy as jnp
from jax import lax
from jax.sharding import PartitionSpec as P

NORM_EPSILON = 1e-05
MASKED_SCORE = -1e30


def joined(part, axis, combine):
    gathered = jax.tree.map(lambda a: lax.all_gather(a, axis), part)

    def take(source):
        return jax.tree.map(lambda a: lax.dynamic_index_in_dim(a, source, 0, False), gathered)

    return lax.fori_loop(
        1, lax.axis_size(axis), lambda source, state: combine(state, take(source)), take(0)
    )


def norm_forward(raw_rows, gain):
    row_count = raw_rows.shape[0]
    head_count, head_width = gain.shape
    widened = raw_rows.astype(jnp.float32).reshape(row_count, head_count, head_width)
    centered = widened - jnp.mean(widened, axis=2, keepdims=True)
    inverse = lax.rsqrt(jnp.mean(centered * centered, axis=2, keepdims=True) + NORM_EPSILON)
    unit_rows = centered * inverse
    scaled = (unit_rows * gain[None]).astype(jnp.bfloat16)
    return (unit_rows, inverse, scaled.reshape(row_count, head_count * head_width))


def norm_backward(grad_norm, unit_rows, inverse, gain):
    scaled = grad_norm * gain[None]
    mean_grad = jnp.mean(scaled, axis=2, keepdims=True)
    mean_cross = jnp.mean(scaled * unit_rows, axis=2, keepdims=True)
    raw_grad = (scaled - mean_grad - unit_rows * mean_cross) * inverse
    return (raw_grad, jnp.sum(grad_norm * unit_rows, axis=0))


def doc_index(positions, starts):
    return jnp.sum((positions[:, None] >= starts[None, :]).astype(jnp.int32), axis=1) - 1


def allowed_pairs(query_pos, key_pos, starts):
    same_doc = doc_index(query_pos, starts)[:, None] == doc_index(key_pos, starts)[None, :]
    return same_doc & (key_pos[None, :] <= query_pos[:, None])


def split_heads(rows, head_count):
    return rows.reshape(rows.shape[0], head_count, rows.shape[1] // head_count)


def shard_sum(pieces):
    rounded = lax.optimization_barrier(pieces.astype(jnp.bfloat16))
    return jnp.sum(rounded.astype(jnp.float32), axis=0)


def block_scores(query_rows, key_rows, pair_mask, head_count):
    head_width = query_rows.shape[1] // head_count
    raw_scores = jnp.einsum(
        "qhd,khd->hqk",
        split_heads(query_rows, head_count),
        split_heads(key_rows, head_count),
        preferred_element_type=jnp.float32,
    )
    return jnp.where(pair_mask[None], raw_scores * head_width ** (-0.5), MASKED_SCORE)


def value_dots(grad_rows, value_rows, head_count):
    return jnp.einsum(
        "qhd,khd->hqk",
        split_heads(grad_rows, head_count),
        split_heads(value_rows, head_count),
        preferred_element_type=jnp.float32,
    )


def block_stats(query_rows, grad_rows, key_rows, value_rows, pair_mask, head_count):
    scores = block_scores(query_rows, key_rows, pair_mask, head_count)
    row_peak = jnp.max(scores, axis=2)
    shifted = jnp.where(pair_mask[None], jnp.exp(scores - row_peak[:, :, None]), 0.0)
    dot_terms = value_dots(grad_rows, value_rows, head_count)
    return (row_peak, jnp.sum(shifted, axis=2), jnp.sum(shifted * dot_terms, axis=2))


def combine_stats(earlier, later):
    row_peak = jnp.maximum(earlier[0], later[0])
    scale_early = jnp.exp(earlier[0] - row_peak)
    scale_late = jnp.exp(later[0] - row_peak)
    return (
        row_peak,
        earlier[1] * scale_early + later[1] * scale_late,
        earlier[2] * scale_early + later[2] * scale_late,
    )


def block_grads(
    query_rows, grad_rows, key_rows, value_rows, pair_mask, log_total, row_delta, head_count
):
    head_width = query_rows.shape[1] // head_count
    scores = block_scores(query_rows, key_rows, pair_mask, head_count)
    chances = jnp.where(pair_mask[None], jnp.exp(scores - log_total[:, :, None]), 0.0)
    dot_terms = value_dots(grad_rows, value_rows, head_count)
    score_grad = (chances * (dot_terms - row_delta[:, :, None]) * head_width ** (-0.5)).astype(
        jnp.bfloat16
    )
    return (chances.astype(jnp.bfloat16), score_grad)


def local(q_raw, k_raw, values, d_out, q_gain, k_gain, q_weight, doc_lengths):
    head_count, head_width = q_gain.shape
    row_count = q_raw.shape[1]
    seq_rows = row_count * lax.axis_size("ctx")
    block_rows = min(seq_rows, max(512, row_count))
    per_block = block_rows // row_count
    block_count = seq_rows // block_rows
    lengths = doc_lengths[0]
    starts = jnp.cumsum(lengths) - lengths
    local_pos = lax.axis_index("ctx") * row_count + jnp.arange(row_count, dtype=jnp.int32)
    q_unit, q_inverse, q_norm = norm_forward(q_raw[0], q_gain)
    k_unit, k_inverse, k_norm = norm_forward(k_raw[0], k_gain)
    value_rows = values[0]
    grad_rows = d_out[0]
    empty_acc = jnp.zeros((row_count, head_count, head_width), jnp.float32)
    gathered_q, gathered_grad = (
        lax.all_gather(q_norm, "ctx", axis=0, tiled=True),
        lax.all_gather(grad_rows, "ctx", axis=0, tiled=True),
    )

    def query_block(block_index):
        row_start = block_index * block_rows
        rows_q = lax.dynamic_slice_in_dim(gathered_q, row_start, block_rows, 0)
        rows_grad = lax.dynamic_slice_in_dim(gathered_grad, row_start, block_rows, 0)
        block_pos = row_start + jnp.arange(block_rows, dtype=jnp.int32)
        return (rows_q, rows_grad, allowed_pairs(block_pos, local_pos, starts))

    def stats_step(block_index):
        rows_q, rows_grad, pair_mask = query_block(block_index)
        return block_stats(rows_q, rows_grad, k_norm, value_rows, pair_mask, head_count)

    stacked = lax.map(stats_step, jnp.arange(block_count))
    partial_stats = tuple(
        (jnp.moveaxis(piece, 0, 1).reshape(head_count, seq_rows) for piece in stacked)
    )
    row_peak, row_total, row_weighted = joined(partial_stats, "ctx", combine_stats)
    log_total = row_peak + jnp.log(row_total)
    row_delta = row_weighted / row_total

    def grad_step(totals, block_index):
        rows_q, rows_grad, pair_mask = query_block(block_index)
        row_start = block_index * block_rows
        block_log = lax.dynamic_slice_in_dim(log_total, row_start, block_rows, 1)
        block_delta = lax.dynamic_slice_in_dim(row_delta, row_start, block_rows, 1)
        chances, score_grad = block_grads(
            rows_q, rows_grad, k_norm, value_rows, pair_mask, block_log, block_delta, head_count
        )
        key_part = shard_sum(
            jnp.einsum(
                "hsqk,sqhd->skhd",
                score_grad.reshape(head_count, per_block, row_count, row_count),
                rows_q.reshape(per_block, row_count, head_count, head_width),
                preferred_element_type=jnp.float32,
            )
        )
        value_part = shard_sum(
            jnp.einsum(
                "hsqk,sqhd->skhd",
                chances.reshape(head_count, per_block, row_count, row_count),
                rows_grad.reshape(per_block, row_count, head_count, head_width),
                preferred_element_type=jnp.float32,
            )
        )
        query_part = jnp.einsum(
            "hqk,khd->qhd",
            score_grad,
            split_heads(k_norm, head_count),
            preferred_element_type=jnp.float32,
        )
        key_part, value_part, query_part = (key_part, value_part, query_part)
        return ((totals[0] + key_part, totals[1] + value_part), query_part)

    (key_norm_grad, value_sum), query_blocks = lax.scan(
        grad_step, (empty_acc, empty_acc), jnp.arange(block_count)
    )
    query_term = query_blocks.reshape(seq_rows, head_count * head_width)
    query_norm_grad = (
        lax.psum_scatter(query_term.astype(jnp.bfloat16), "ctx", scatter_dimension=0, tiled=True)
        .astype(jnp.float32)
        .reshape(row_count, head_count, head_width)
    )
    q_raw_grad, q_gain_part = norm_backward(query_norm_grad, q_unit, q_inverse, q_gain)
    k_raw_grad, k_gain_part = norm_backward(key_norm_grad, k_unit, k_inverse, k_gain)
    q_gain_grad, k_gain_grad = lax.psum((q_gain_part, k_gain_part), ("ctx", "dp"))
    q_grad_rows = q_raw_grad.reshape(row_count, head_count * head_width).astype(jnp.bfloat16)
    partial_input = jnp.einsum(
        "th,dh->td", q_grad_rows, q_weight, preferred_element_type=jnp.float32
    )
    input_grad = lax.psum_scatter(
        partial_input.astype(jnp.bfloat16), "tp", scatter_dimension=1, tiled=True
    )
    key_grad = k_raw_grad.reshape(row_count, head_count * head_width).astype(jnp.bfloat16)
    value_grad = value_sum.reshape(row_count, head_count * head_width).astype(jnp.bfloat16)
    return (input_grad[None], key_grad[None], value_grad[None], q_gain_grad, k_gain_grad)


def solution(mesh):
    return jax.shard_map(
        local,
        mesh=mesh,
        in_specs=(
            P("dp", "ctx", "tp"),
            P("dp", "ctx", "tp"),
            P("dp", "ctx", "tp"),
            P("dp", "ctx", "tp"),
            P("tp", None),
            P("tp", None),
            P(None, "tp"),
            P("dp", None),
        ),
        out_specs=(
            P("dp", "ctx", "tp"),
            P("dp", "ctx", "tp"),
            P("dp", "ctx", "tp"),
            P("tp", None),
            P("tp", None),
        ),
        check_vma=False,
    )
```

profile of v0, /device:TPU:32, one launch (start us, length us, event | category | flops | bytes accessed | tf_op | source)
XLA Modules:
  0.0 1241.9 jit_solution(3021370318078079397)
XLA Ops:
  16.6 133.3 %all-gather.7.cloned.1.call-done = bf16[4096,1024]{1,0:T(8,128)(2,1)} async-done(((bf16[256,1024]{1,0:T(8,128)(2,1)}), bf16[4096,1024]{1,0:T(8,128)(2,1)}) %all-gather.7.cloned.1.call-update) | async-done | bytes 8388624 | tf_op jit(solution)/shard_map/all_gather | solution.py:126
  149.9 11.3 copy.159
  161.2 138.0 %all-gather.15.cloned.1.call-done = bf16[1,4096,1024]{1,2,0:T(8,128)(2,1)} async-done(((bf16[1,256,1024]{1,2,0:T(8,128)(2,1)}), bf16[1,4096,1024]{1,2,0:T(8,128)(2,1)}) %all-gather.15.cloned.1.call-update) | async-done | bytes 8388624 | tf_op jit(solution)/shard_map/all_gather | solution.py:127
  299.2 76.0 %while.56 = (s32[]{:T(128)}, f32[8,8,512]{2,1,0:T(8,128)S(1)}, f32[8,8,512]{2,1,0:T(8,128)}, f32[8,8,512]{2,1,0:T(8,128)}, s32[8]{0:T(128)S(1)}, /*index=5*/s32[...) while((s32[]{:T(128)}, f32[8,8,512]{2,1,0:T(8,128)S(1)}, ...), condition=%wide.region_11.12_spmd.clone, body=%wide.region_5.11_spmd.clone.sunk | while | flops 551951104 | bytes 21697832 | solution.py:141
  377.3 80.5 %all-gather.9.cloned.1.call-done = f32[16,8,4096]{2,1,0:T(8,128)} async-done(((f32[1,8,4096]{2,1,0:T(8,128)}), f32[16,8,4096]{2,1,0:T(8,128)}) %all-gather.9.cloned.1.call-update) | async-done | bytes 2097168 | tf_op jit(solution)/shard_map/all_gather | solution.py:11
  458.8 84.4 %all-gather.11.cloned.1.call-done = f32[16,8,4096]{2,1,0:T(8,128)} async-done(((f32[1,8,4096]{2,1,0:T(8,128)}), f32[16,8,4096]{2,1,0:T(8,128)}) %all-gather.11.cloned.1.call-update) | async-done | bytes 2097168 | tf_op jit(solution)/shard_map/all_gather | solution.py:11
  544.0 83.8 %all-gather.13.cloned.1.call-done = f32[16,8,4096]{2,1,0:T(8,128)} async-done(((f32[1,8,4096]{2,1,0:T(8,128)}), f32[16,8,4096]{2,1,0:T(8,128)}) %all-gather.13.cloned.1.call-update) | async-done | bytes 2097168 | tf_op jit(solution)/shard_map/all_gather | solution.py:11
  628.7 32.7 %while.55 = (s32[]{:T(128)}, f32[8,4096]{1,0:T(8,128)S(1)}, f32[8,4096]{1,0:T(8,128)S(1)}, f32[8,4096]{1,0:T(8,128)S(1)}, f32[16,8,4096]{2,1,0:T(8,128)}, /*inde...) while((s32[]{:T(128)}, f32[8,4096]{1,0:T(8,128)S(1)}, ...), condition=%wide.region_13.14_spmd, body=%wide.region_12.13_spmd.sunk | while | flops 360453 | bytes 1835159 | solution.py:16
  662.1 203.3 %while.57 = (s32[]{:T(128)}, f32[256,8,128]{0,2,1:T(8,128)}, f32[256,8,128]{0,2,1:T(8,128)}, bf16[8,512,8,128]{3,1,2,0:T(8,128)(2,1)}, s32[8]{0:T(128)S(1)}, /*i...) while((s32[]{:T(128)}, f32[256,8,128]{0,2,1:T(8,128)}, ...), condition=%wide.region_19.20_spmd.clone, body=%wide.region_14.19_spmd.clone.sunk | while | flops 1359891200 | bytes 79698120 | solution.py:182
  665.2 3.5 fusion.89
  674.4 4.7 multiply_convert_fusion.5
  690.6 3.5 fusion.89
  699.8 4.7 multiply_convert_fusion.5
  709.7 3.1 bitcast_dynamic-update-slice_fusion.9
  716.0 3.5 fusion.89
  725.2 4.7 multiply_convert_fusion.5
  741.4 3.5 fusion.89
  750.6 4.7 multiply_convert_fusion.5
  766.8 3.5 fusion.89
  776.0 4.7 multiply_convert_fusion.5
  792.1 3.5 fusion.89
  801.4 4.7 multiply_convert_fusion.5
  811.3 3.1 bitcast_dynamic-update-slice_fusion.9
  817.5 3.5 fusion.89
  826.7 4.7 multiply_convert_fusion.5
  842.9 3.5 fusion.89
  852.1 4.7 multiply_convert_fusion.5
  865.4 12.0 copy.161
  877.4 8.8 copy.230
  886.3 219.5 %reduce-scatter.3.cloned.1.call-done = bf16[256,1024]{1,0:T(8,128)(2,1)} async-done(((bf16[4096,1024]{1,0:T(8,128)(2,1)}), bf16[256,1024]{1,0:T(8,128)(2,1)}) %reduce-scatter.3.cloned.1.call-update) | async-done | bytes 524304 | tf_op jit(solution)/shard_map/reduce_scatter | solution.py:187
  1110.1 8.4 convolution_convert_fusion
  1125.7 109.3 %all-reduce = (f32[8,128]{1,0:T(8,128)}, f32[8,128]{1,0:T(8,128)}) all-reduce(f32[8,128]{1,0:T(8,128)S(1)} %bitcast.233, f32[8,128]{1,0:T(8,128)S(1)} %get-tuple-element.792), channel_id=1, replica_groups=mesh['ctx'=16,'tp'=4,'dp'=4] {'ctx','dp'}, use_global_device_ids=true, to_apply=%region_27.28 | all-reduce | flops 2048 | bytes 16384 | tf_op jit(solution)/shard_map/psum | solution.py:193
  (659 shorter events, 253.5 us)
Async XLA Ops:
  7.2 4.6 copy-start.16
  7.2 142.7 %all-gather.7.cloned.1.call-start = ((), (), s32[]{:S(2)}) async-start(), calls=%async_computation.2 | async-start | bytes 8912896 | tf_op jit(solution)/shard_map/all_gather | solution.py:126
  13.1 286.1 %all-gather.15.cloned.1.call-start = ((), (), s32[]{:S(2)}) async-start(), calls=%async_computation.8 | async-start | bytes 8912896 | tf_op jit(solution)/shard_map/all_gather | solution.py:127
  14.2 443.7 %all-gather.9.cloned.1.call-start = ((), (), s32[]{:S(2)}) async-start(), calls=%async_computation.3 | async-start | bytes 2228224 | tf_op jit(solution)/shard_map/all_gather | solution.py:11
  14.7 146.6 %copy-start.9 = (f32[1,256,1024]{1,2,0:T(8,128)}, f32[1,256,1024]{1,2,0:T(8,128)S(1)}, u32[]{:S(2)}) copy-start(f32[1,256,1024]{1,2,0:T(8,128)S(1)} %copy.155) | copy-start | bytes 3145732
  375.9 167.2 %all-gather.11.cloned.1.call-start = ((), (), s32[]{:S(2)}) async-start(), calls=%async_computation.4 | async-start | bytes 2228224 | tf_op jit(solution)/shard_map/all_gather | solution.py:11
  376.5 251.3 %all-gather.13.cloned.1.call-start = ((), (), s32[]{:S(2)}) async-start(), calls=%async_computation.5 | async-start | bytes 2228224 | tf_op jit(solution)/shard_map/all_gather | solution.py:11
  377.1 728.6 %reduce-scatter.3.cloned.1.call-start = ((), (), s32[]{:S(2)}) async-start(), calls=%async_computation.6 | async-start | bytes 8912896 | tf_op jit(solution)/shard_map/reduce_scatter | solution.py:187
  662.1 6.6 copy-start
  662.1 6.6 copy-start.23
  687.5 6.6 copy-start
  687.5 6.6 copy-start.23
  712.9 6.6 copy-start
  712.9 6.6 copy-start.23
  738.3 6.6 copy-start
  738.3 6.6 copy-start.23
  763.7 6.6 copy-start
  763.7 6.6 copy-start.23
  789.0 6.6 copy-start
  789.1 6.6 copy-start.23
  814.4 6.6 copy-start
  814.5 6.6 copy-start.23
  839.8 6.6 copy-start
  839.8 6.6 copy-start.23
  886.2 220.9 %copy-start.12 = (f32[32,8,8,128]{3,2,1,0:T(8,128)S(1)}, f32[32,8,8,128]{3,2,1,0:T(8,128)}, u32[]{:S(2)}) copy-start(f32[32,8,8,128]{3,2,1,0:T(8,128)} %copy-done.11) | copy-start | bytes 3145732
  886.2 220.9 %copy-start.31 = (f32[8,128]{1,0:T(8,128)S(1)}, f32[8,128]{1,0:T(8,128)}, u32[]{:S(2)}) copy-start(f32[8,128]{1,0:T(8,128)} %param.18) | copy-start | bytes 12292
  886.2 348.8 %reduce-scatter.5.cloned.1.call-start = ((), (), s32[]{:S(2)}) async-start(), calls=%async_computation.7 | async-start | bytes 2621440 | tf_op jit(solution)/shard_map/reduce_scatter | solution.py:198
  1110.1 8.5 copy-start.5
  1110.1 8.5 copy-start.10
  1110.1 8.5 copy-start.22
  1110.1 8.5 copy-start.26
  1110.1 8.5 copy-start.29
  (101 other events, 311.3 us)
Sparse Core Ops, SparseCore 0:
  13.2 136.6 all-gather.6
  153.0 146.2 all-gather.14
  376.0 81.7 all-gather.8
  460.9 82.2 all-gather.10
  545.6 82.2 all-gather.12
  886.3 219.3 reduce-scatter.2
  1118.7 31.2 reduce-scatter.4
where the time goes:
time: 1270 us; the launch traced here: 1240 us
  waiting for transfers between devices  741 us (58%)
  matrix products  154 us (12%)
  local copies, waits for them, and re-layouts  142 us (11%)
  blocking collectives  109 us (9%)
  other arithmetic  67.4 us (5%)
  between operations  14.6 us (1%)
  loops' own time  13 us (1%)
    all_gather x3, waiting for transfers between devices, joined(): gathered = jax.tree.map(lambda a: lax.all_gather(a, axis), part)  249 us
    reduce_scatter x1, waiting for transfers between devices, local(): lax.psum_scatter(query_term.astype(jnp.bfloat16), 'ctx', scatter_dimensio...  219 us
    all_gather x1, waiting for transfers between devices, local(): lax.all_gather(grad_rows, 'ctx', axis=0, tiled=True)  138 us
    all_gather x1, waiting for transfers between devices, local(): lax.all_gather(q_norm, 'ctx', axis=0, tiled=True)  133 us
    psum x1, blocking collectives, local(): lax.psum((q_gain_part, k_gain_part), ('ctx', 'dp'))  109 us
    dot_general x16, matrix products, value_dots(): jnp.einsum('qhd,khd->hqk', split_heads(grad_rows, head_count), split_head...  49.7 us
    dot_general x16, matrix products, block_scores(): jnp.einsum('qhd,khd->hqk', split_heads(query_rows, head_count), split_hea...  35.1 us
  transfers between devices with their start and end apart: 7, of which 6 were waited for; matrix products, arithmetic and copies ran while one was open for 2% of the time, Pallas kernels for 0%

commit v1 on v0

v1 whole, which is shorter than its diff:
```python
import functools

import jax
import jax.numpy as jnp
from jax import lax
from jax.experimental import pallas as pl
from jax.experimental.pallas import tpu as pltpu
from jax.sharding import PartitionSpec as P

NORM_EPSILON = 1e-05
MASKED_SCORE = -1e30
HEADS_LOCAL = 8
HD = 128
ROWS = 256
LANES = 256
CHUNKS = 2
FACTOR = HD ** (-0.5)
EXP2_FACTOR = FACTOR * 1.4426950408889634
VMEM_LIMIT = 40 * 1024 * 1024

Z_GROUPS = [[2 * z + half for z in range(8)] for half in range(2)]
HALF_SWAP = [(index, index ^ 1) for index in range(16)]


def nt_dot(a, b):
    return lax.dot_general(a, b, (((1,), (1,)), ((), ())), preferred_element_type=jnp.float32)


def nn_dot(a, b):
    return lax.dot_general(a, b, (((1,), (0,)), ((), ())), preferred_element_type=jnp.float32)


def unit_norm(raw):
    widened = raw.astype(jnp.float32)
    centered = widened - jnp.mean(widened, axis=1, keepdims=True)
    inverse = lax.rsqrt(jnp.mean(centered * centered, axis=1, keepdims=True) + NORM_EPSILON)
    return centered * inverse, inverse


def unit_norm_backward(grad_norm, unit_rows, inverse, gain):
    scaled = grad_norm * gain
    mean_grad = jnp.mean(scaled, axis=1, keepdims=True)
    mean_cross = jnp.mean(scaled * unit_rows, axis=1, keepdims=True)
    return (scaled - mean_grad - unit_rows * mean_cross) * inverse


def key_prep_kernel(raw_ref, gain_ref, norm_ref, norm_t_ref):
    unit_rows, _ = unit_norm(raw_ref[0])
    scaled = unit_rows * gain_ref[...]
    norm_ref[0] = scaled.astype(jnp.bfloat16)
    norm_t_ref[0] = scaled.T.astype(jnp.bfloat16)


def key_prep(raw, gain):
    count = raw.shape[0]
    return pl.pallas_call(
        key_prep_kernel,
        grid=(count,),
        in_specs=[
            pl.BlockSpec((1, ROWS, HD), lambda i: (i, 0, 0)),
            pl.BlockSpec((1, HD), lambda i: (0, 0)),
        ],
        out_specs=[
            pl.BlockSpec((1, ROWS, HD), lambda i: (i, 0, 0)),
            pl.BlockSpec((1, HD, ROWS), lambda i: (i, 0, 0)),
        ],
        out_shape=[
            jax.ShapeDtypeStruct((count, ROWS, HD), jnp.bfloat16),
            jax.ShapeDtypeStruct((count, HD, ROWS), jnp.bfloat16),
        ],
        cost_estimate=pl.CostEstimate(flops=0, bytes_accessed=3 * 2**19, transcendentals=0),
        name="key_prep",
    )(raw, gain)


def fold(tile):
    return tile.reshape(tile.shape[0] // 8, 8, tile.shape[1])


def attention_kernel(
    has_prior,
    bounds_ref,
    half_ref,
    pos_ref,
    low_ref,
    query_ref,
    grad_ref,
    norm_own,
    norm_other,
    norm_t_own,
    norm_t_other,
    value_own,
    value_other,
    gain_ref,
    *rest,
):
    if has_prior:
        prior, rest = rest[:4], rest[4:]
    dq_ref, gain_grad_ref, dk_own, dk_other, dv_own, dv_other, score_ref, dot_ref, dqt_ref = rest
    blocks = query_ref.shape[0] // LANES
    half = half_ref[0]
    if has_prior:
        for target, source in zip((dk_own, dk_other, dv_own, dv_other), prior):
            target[...] = source[...]
    else:
        for target in (dk_own, dk_other, dv_own, dv_other):
            target[...] = jnp.zeros_like(target)
    gain_grad_ref[...] = jnp.zeros_like(gain_grad_ref)
    sides = (
        (norm_own, norm_t_own, value_own, dk_own, dv_own),
        (norm_other, norm_t_other, value_other, dk_other, dv_other),
    )

    def block_body(block, carry):
        rows = pl.ds(pl.multiple_of(block * LANES, LANES), LANES)
        unit_rows, inverse = unit_norm(query_ref[rows, :])
        query = (unit_rows * gain_ref[...]).astype(jnp.bfloat16)
        grad = grad_ref[rows, :]
        pos = pos_ref[pl.ds(block, 1), :]
        low = low_ref[pl.ds(block, 1), :]
        first, inner, diagonal, last = (bounds_ref[block, i] for i in range(4))

        def scores_body(masked, tile, peak):
            for side, (norm, _, value, _, _) in enumerate(sides):
                scores = nt_dot(norm[tile], query)
                if masked:
                    which = half if side == 0 else 1 - half
                    key_pos = (2 * tile + which) * ROWS + lax.broadcasted_iota(
                        jnp.int32, (ROWS, LANES), 0
                    )
                    scores = jnp.where(
                        (key_pos >= low) & (key_pos <= pos), scores, MASKED_SCORE
                    )
                score_ref[2 * tile + side] = scores
                peak = jnp.maximum(peak, jnp.max(fold(scores), axis=0))
                dot_ref[2 * tile + side] = nt_dot(value[tile], grad)
            return peak

        peak = jnp.full((8, LANES), MASKED_SCORE, jnp.float32)
        peak = lax.fori_loop(first, inner, functools.partial(scores_body, True), peak)
        peak = lax.fori_loop(inner, diagonal, functools.partial(scores_body, False), peak)
        peak = lax.fori_loop(diagonal, last, functools.partial(scores_body, True), peak)
        peak = jnp.max(peak, axis=0, keepdims=True) * EXP2_FACTOR

        def exp_body(tile, sums):
            total, weighted = sums
            for side in range(2):
                shifted = jnp.exp2(score_ref[2 * tile + side] * EXP2_FACTOR - peak)
                score_ref[2 * tile + side] = shifted
                total = total + jnp.sum(fold(shifted), axis=0)
                weighted = weighted + jnp.sum(fold(shifted * dot_ref[2 * tile + side]), axis=0)
            return total, weighted

        empty = jnp.zeros((8, LANES), jnp.float32)
        total, weighted = lax.fori_loop(first, last, exp_body, (empty, empty))
        share = 1.0 / jnp.sum(total, axis=0, keepdims=True)
        delta = jnp.sum(weighted, axis=0, keepdims=True) * share
        dqt_ref[...] = jnp.zeros_like(dqt_ref)

        def grads_body(tile, carry):
            for side, (_, norm_t, _, dk, dv) in enumerate(sides):
                chance = score_ref[2 * tile + side] * share
                score_grad = (chance * (dot_ref[2 * tile + side] - delta)).astype(jnp.bfloat16)
                dv[tile] += nn_dot(chance.astype(jnp.bfloat16), grad)
                dk[tile] += nn_dot(score_grad, query)
                dqt_ref[...] += nn_dot(norm_t[tile], score_grad)
            return carry

        lax.fori_loop(first, last, grads_body, 0)
        query_grad = dqt_ref[...].T * FACTOR
        dq_ref[rows, :] = unit_norm_backward(
            query_grad, unit_rows, inverse, gain_ref[...]
        ).astype(jnp.bfloat16)
        gain_grad_ref[...] += jnp.sum(query_grad * unit_rows, axis=0, keepdims=True)
        return carry

    lax.fori_loop(0, blocks, block_body, 0)


def attention(bounds, half, pos, low, query, grad, keys, values, gain, prior):
    rows = query.shape[0]
    tiles = keys[0][0].shape[0]
    smem = pl.BlockSpec(memory_space=pltpu.SMEM)
    vmem = pl.BlockSpec(memory_space=pltpu.VMEM)
    wide = jax.ShapeDtypeStruct((tiles, ROWS, HD), jnp.float32)
    operands = [
        bounds, half, pos, low, query, grad,
        keys[0][0], keys[1][0], keys[0][1], keys[1][1], values[0], values[1], gain,
    ]
    if prior is not None:
        operands += list(prior)
    flops = 5 * 2 * rows * tiles * ROWS * HD
    return pl.pallas_call(
        functools.partial(attention_kernel, prior is not None),
        in_specs=[smem, smem] + [vmem] * (len(operands) - 2),
        out_specs=[vmem] * 6,
        out_shape=[
            jax.ShapeDtypeStruct((rows, HD), jnp.bfloat16),
            jax.ShapeDtypeStruct((1, HD), jnp.float32),
            wide, wide, wide, wide,
        ],
        scratch_shapes=[
            pltpu.VMEM((2 * tiles, ROWS, LANES), jnp.float32),
            pltpu.VMEM((2 * tiles, ROWS, LANES), jnp.float32),
            pltpu.VMEM((HD, LANES), jnp.float32),
        ],
        compiler_params=pltpu.CompilerParams(vmem_limit_bytes=VMEM_LIMIT),
        cost_estimate=pl.CostEstimate(
            flops=2 * flops, bytes_accessed=2**24, transcendentals=rows * tiles * ROWS
        ),
        name="attention",
    )(*operands)


def key_finish_kernel(own_ref, other_ref, raw_ref, gain_ref, out_ref, gain_grad_ref):
    @pl.when(pl.program_id(0) == 0)
    def _():
        gain_grad_ref[...] = jnp.zeros_like(gain_grad_ref)

    grad_norm = (own_ref[0] + other_ref[0].astype(jnp.float32)) * FACTOR
    unit_rows, inverse = unit_norm(raw_ref[0])
    out_ref[0] = unit_norm_backward(grad_norm, unit_rows, inverse, gain_ref[...]).astype(
        jnp.bfloat16
    )
    gain_grad_ref[...] += jnp.sum(grad_norm * unit_rows, axis=0, keepdims=True)


def key_finish(own, other, raw, gain):
    count = raw.shape[0]
    block = pl.BlockSpec((1, ROWS, HD), lambda i: (i, 0, 0))
    row = pl.BlockSpec((1, HD), lambda i: (0, 0))
    return pl.pallas_call(
        key_finish_kernel,
        grid=(count,),
        in_specs=[block, block, block, row],
        out_specs=[block, row],
        out_shape=[
            jax.ShapeDtypeStruct((count, ROWS, HD), jnp.bfloat16),
            jax.ShapeDtypeStruct((1, HD), jnp.float32),
        ],
        cost_estimate=pl.CostEstimate(flops=0, bytes_accessed=5 * 2**19, transcendentals=0),
        name="key_finish",
    )(own, other, raw, gain)


def project_kernel(rows_ref, weight_ref, out_ref, joined_ref):
    @pl.when(pl.program_id(0) == 0)
    def _():
        for head in range(rows_ref.shape[0]):
            joined_ref[:, head * HD : (head + 1) * HD] = rows_ref[head]

    out_ref[0] = nt_dot(joined_ref[...], weight_ref[...]).astype(jnp.bfloat16)


def project(rows, weight, parts):
    heads, count, _ = rows.shape
    model, inner = weight.shape
    width = model // parts
    block = 512
    per_part = width // block
    return pl.pallas_call(
        project_kernel,
        grid=(model // block,),
        in_specs=[
            pl.BlockSpec((heads, count, HD), lambda i: (0, 0, 0)),
            pl.BlockSpec((block, inner), lambda i: (i, 0)),
        ],
        out_specs=pl.BlockSpec((1, count, block), lambda i: (i // per_part, 0, i % per_part)),
        out_shape=jax.ShapeDtypeStruct((parts, count, width), jnp.bfloat16),
        scratch_shapes=[pltpu.VMEM((count, inner), jnp.bfloat16)],
        cost_estimate=pl.CostEstimate(
            flops=2 * count * model * inner, bytes_accessed=2 * model * inner, transcendentals=0
        ),
        name="project",
    )(rows, weight)


def along_z(pieces):
    return lax.all_to_all(pieces, "ctx", 0, 0, axis_index_groups=Z_GROUPS)


def swap_half(piece):
    return lax.ppermute(piece, "ctx", HALF_SWAP)


def by_head(rows):
    return rows.reshape(rows.shape[0], HEADS_LOCAL, HD).transpose(1, 0, 2)


def by_row(pieces):
    return pieces.transpose(1, 0, 2).reshape(pieces.shape[1], HEADS_LOCAL * HD)


def reduce_tp(parts):
    count = parts.shape[0]
    me = lax.axis_index("tp")

    def part(step):
        return lax.dynamic_index_in_dim(parts, lax.rem(me + step, count), 0, False)

    total = part(0).astype(jnp.float32)
    for step in range(1, count):
        moved = lax.ppermute(part(step), "tp", [(i, (i + step) % count) for i in range(count)])
        total = total + moved.astype(jnp.float32)
    return total.astype(jnp.bfloat16)


def spread_gains(gains, z):
    mine = jnp.arange(HEADS_LOCAL, dtype=jnp.int32)[:, None, None] == z
    total = jnp.where(mine, gains[None], 0.0)
    for distance in (1, 2):
        total = total + lax.ppermute(total, "dp", [(i, i ^ distance) for i in range(4)])
    for distance in (1, 2, 4, 8):
        total = total + lax.ppermute(total, "ctx", [(i, i ^ distance) for i in range(16)])
    return total


def local(q_raw, k_raw, values, d_out, q_gain, k_gain, q_weight, doc_lengths):
    ctx = lax.axis_index("ctx")
    z = ctx // 2
    half = lax.rem(ctx, 2)
    lengths = doc_lengths[0]
    starts = jnp.cumsum(lengths) - lengths
    q_gain_row = lax.dynamic_slice_in_dim(q_gain, z, 1, 0)
    k_gain_row = lax.dynamic_slice_in_dim(k_gain, z, 1, 0)

    key_own = along_z(by_head(k_raw[0]))
    value_own = along_z(by_head(values[0]))
    key_other = swap_half(key_own)
    value_other = swap_half(value_own)
    keys = (key_prep(key_own, k_gain_row), key_prep(key_other, k_gain_row))

    count = ROWS // CHUNKS
    prior = None
    query_gain_sum = jnp.zeros((1, HD), jnp.float32)
    input_parts = []
    for chunk in range(CHUNKS):
        rows = slice(chunk * count, (chunk + 1) * count)
        sent = jnp.stack([by_head(q_raw[0, rows]), by_head(d_out[0, rows])], axis=1)
        moved = along_z(sent)
        query = moved[:, 0].reshape(8 * count, HD)
        grad = moved[:, 1].reshape(8 * count, HD)
        pos = (
            (2 * jnp.arange(8, dtype=jnp.int32) + half)[:, None] * ROWS
            + chunk * count
            + jnp.arange(count, dtype=jnp.int32)[None, :]
        ).reshape(8 * count // LANES, LANES)
        low = jnp.max(
            jnp.where(starts[None, None, :] <= pos[:, :, None], starts[None, None, :], 0), axis=2
        )
        first = low[:, 0] // (2 * ROWS)
        last = pos[:, -1] // (2 * ROWS) + 1
        inner = jnp.clip((low[:, -1] + 2 * ROWS - 1) // (2 * ROWS), first, last)
        diagonal = jnp.clip(pos[:, 0] // (2 * ROWS), inner, last)
        bounds = jnp.stack([first, inner, diagonal, last], axis=1).astype(jnp.int32)
        dq, gain_part, *prior = attention(
            bounds,
            half.reshape(1),
            pos,
            low,
            query,
            grad,
            keys,
            (value_own, value_other),
            q_gain_row,
            prior,
        )
        query_gain_sum = query_gain_sum + gain_part
        returned = along_z(dq.reshape(8, count, HD))
        input_parts.append(reduce_tp(project(returned, q_weight, 4)))
    dk_own, dk_other, dv_own, dv_other = prior

    dv_moved = swap_half(dv_other.astype(jnp.bfloat16))
    dk_moved = swap_half(dk_other.astype(jnp.bfloat16))
    value_sum = (dv_own + dv_moved.astype(jnp.float32)).astype(jnp.bfloat16)
    value_grad = by_row(along_z(value_sum))
    dk_raw, key_gain_sum = key_finish(dk_own, dk_moved, key_own, k_gain_row)
    key_grad = by_row(along_z(dk_raw))
    gains = spread_gains(jnp.concatenate([query_gain_sum, key_gain_sum], axis=0), z)
    input_grad = jnp.concatenate(input_parts, axis=0)
    return (input_grad[None], key_grad[None], value_grad[None], gains[:, 0], gains[:, 1])


def solution(mesh):
    return jax.shard_map(
        local,
        mesh=mesh,
        in_specs=(
            P("dp", "ctx", "tp"),
            P("dp", "ctx", "tp"),
            P("dp", "ctx", "tp"),
            P("dp", "ctx", "tp"),
            P("tp", None),
            P("tp", None),
            P(None, "tp"),
            P("dp", None),
        ),
        out_specs=(
            P("dp", "ctx", "tp"),
            P("dp", "ctx", "tp"),
            P("dp", "ctx", "tp"),
            P("tp", None),
            P("tp", None),
        ),
        check_vma=False,
    )
```

time: 1270 us -> 262 us (0.21); the launches traced: 1240 us -> 259 us
  waiting for transfers between devices: 741 us -> 66.4 us
  matrix products: 154 us -> 0 us
  blocking collectives: 109 us -> 0 us
  local copies, waits for them, and re-layouts: 142 us -> 35.1 us
  starting transfers between devices: 0.46 us -> 78.3 us
  Pallas kernels: 0 us -> 71.8 us
  other arithmetic: 67.4 us -> 6.73 us
  between operations: 14.6 us -> 0.87 us
  loops' own time: 13 us -> 0 us
    all_gather x5 -> x0, waiting for transfers between devices: 520 us -> none  [the longest x3 249 us: joined(): gathered = jax.tree.map(lambda a: lax.all_gather(a, axis), part)]
    reduce_scatter x2 -> x0, waiting for transfers between devices: 219 us -> none  [the longest x1 219 us: local(): lax.psum_scatter(query_term.astype(jnp.bfloat16), 'ctx', scatter_dimensio...]
    dot_general x57 -> x0, matrix products: 154 us -> none  [the longest x16 49.7 us: value_dots(): jnp.einsum('qhd,khd->hqk', split_heads(grad_rows, head_count), split_head...]
    psum x1 -> x0, blocking collectives: 109 us -> none  [local(): lax.psum((q_gain_part, k_gain_part), ('ctx', 'dp'))]
    pallas_call x0 -> x7, Pallas kernels: none -> 71.8 us  [the longest x2 36.6 us: attention(): pl.pallas_call(functools.partial(attention_kernel, prior is not None), in...]
    dynamic_slice x64 -> x1, local copies, waits for them, and re-layouts: 57.7 us -> 1.22 us  [local(): q_gain_row = lax.dynamic_slice_in_dim(q_gain, z, 1, 0)]
    all_to_all x0 -> x8, starting transfers between devices: none -> 50.5 us  [along_z(): return lax.all_to_all(pieces, 'ctx', 0, 0, axis_index_groups=Z_GROUPS)]
    all_to_all x0 -> x8, waiting for transfers between devices: none -> 47.2 us  [along_z(): return lax.all_to_all(pieces, 'ctx', 0, 0, axis_index_groups=Z_GROUPS)]
  transfers between devices with their start and end apart: 7 -> 24, of which waited for: 6 -> 10; matrix products, arithmetic and copies ran while one was open for 2% -> 8% of each run, Pallas kernels for 0% -> 21%
where the time goes in v1:
time: 262 us; the launch traced here: 259 us
  starting transfers between devices  78.3 us (30%)
  Pallas kernels  71.8 us (27%)
  waiting for transfers between devices  66.4 us (25%)
  local copies, waits for them, and re-layouts  35.1 us (13%)
  other arithmetic  6.73 us (3%)
    all_to_all x8, starting transfers between devices, along_z(): return lax.all_to_all(pieces, 'ctx', 0, 0, axis_index_groups=Z_GROUPS)  50.5 us
    all_to_all x8, waiting for transfers between devices, along_z(): return lax.all_to_all(pieces, 'ctx', 0, 0, axis_index_groups=Z_GROUPS)  47.2 us
    pallas_call x2, Pallas kernels, attention(): pl.pallas_call(functools.partial(attention_kernel, prior is not None), in...  36.6 us
    unnamed x54, local copies, waits for them, and re-layouts  23.3 us
    pallas_call x2, Pallas kernels, project(): pl.pallas_call(project_kernel, grid=(model // block,), in_specs=[pl.Block...  17.3 us
    pallas_call x2, Pallas kernels, key_prep(): pl.pallas_call(key_prep_kernel, grid=(count,), in_specs=[pl.BlockSpec((1,...  11.6 us
    ppermute x6, starting transfers between devices, reduce_tp(): lax.ppermute(part(step), 'tp', [(i, (i + step) % count) for i in range(co...  9.64 us
    ppermute x4, waiting for transfers between devices, swap_half(): return lax.ppermute(piece, 'ctx', HALF_SWAP)  9.5 us
  transfers between devices with their start and end apart: 24, of which 10 were waited for; matrix products, arithmetic and copies ran while one was open for 8% of the time, Pallas kernels for 21%

profile of v1, /device:TPU:32, one launch (start us, length us, event | category | flops | bytes accessed | tf_op | source)
XLA Modules:
  0.0 259.1 jit_solution(1249603791194821449)
XLA Ops:
  2.9 8.6 %all-to-all-start.1 = ((bf16[8,256,128]{2,1,0:T(8,128)(2,1)}), bf16[8,256,128]{2,1,0:T(8,128)(2,1)S(1)}, u32[]{:S(2)}, u32[]{:S(2)}) async-start(bf16[8,256,128]{2,1,0:T(8,128)(2,1)} %bitcast.15), calls=%async_computation.1 | async-start | bytes 1048576 | tf_op jit(solution)/shard_map/all_to_all | solution.py:279
  15.0 12.5 %all-to-all-done.1.raw_ref = bf16[8,256,128]{2,1,0:T(8,128)(2,1)S(1)} async-done(((bf16[8,256,128]{2,1,0:T(8,128)(2,1)}), bf16[8,256,128]{2,1,0:T(8,128)(2,1)S(1)}, u32[]{:S(2)}, u32[]{:S(2)}) %all-to-all-start.1) | async-done | bytes 524320 | tf_op jit(solution)/shard_map/all_to_all | solution.py:279
  27.5 4.9 %all-to-all-start = ((bf16[8,2,128,128]{3,2,1,0:T(8,128)(2,1)}), bf16[8,2,128,128]{3,2,1,0:T(8,128)(2,1)S(1)}, u32[]{:S(2)}, u32[]{:S(2)}) async-start(bf16[8,2,128,128]{3,2,1,0:T(8,128)(2,1)} %copy.53), calls=%async_computation | async-start | bytes 1048576 | tf_op jit(solution)/shard_map/all_to_all | solution.py:279
  35.1 13.8 %all-to-all-done = bf16[8,2,128,128]{3,2,1,0:T(8,128)(2,1)S(1)} async-done(((bf16[8,2,128,128]{3,2,1,0:T(8,128)(2,1)}), bf16[8,2,128,128]{3,2,1,0:T(8,128)(2,1)S(1)}, u32[]{:S(2)}, u32[]{:S(2)}) %all-to-all-start) | async-done | bytes 524320 | tf_op jit(solution)/shard_map/all_to_all | solution.py:279
  48.9 4.8 %all-to-all-start.2 = ((bf16[8,256,128]{2,1,0:T(8,128)(2,1)}), bf16[8,256,128]{2,1,0:T(8,128)(2,1)S(1)}, u32[]{:S(2)}, u32[]{:S(2)}) async-start(bf16[8,256,128]{2,1,0:T(8,128)(2,1)} %bitcast.17), calls=%async_computation.2 | async-start | bytes 1048576 | tf_op jit(solution)/shard_map/all_to_all | solution.py:279
  55.1 15.2 %all-to-all-done.2.value_own = bf16[8,256,128]{2,1,0:T(8,128)(2,1)S(1)} async-done(((bf16[8,256,128]{2,1,0:T(8,128)(2,1)}), bf16[8,256,128]{2,1,0:T(8,128)(2,1)S(1)}, u32[]{:S(2)}, u32[]{:S(2)}) %all-to-all-start.2) | async-done | bytes 524320 | tf_op jit(solution)/shard_map/all_to_all | solution.py:279
  70.3 5.5 %all-to-all-start.4 = ((bf16[8,2,128,128]{3,2,1,0:T(8,128)(2,1)}), bf16[8,2,128,128]{3,2,1,0:T(8,128)(2,1)}, u32[]{:S(2)}, u32[]{:S(2)}) async-start(bf16[8,2,128,128]{3,2,1,0:T(8,128)(2,1)} %copy.60), calls=%async_computation.4 | async-start | bytes 1048576 | tf_op jit(solution)/shard_map/all_to_all | solution.py:279
  76.1 3.0 %collective-permute-start = (bf16[8,256,128]{2,1,0:T(8,128)(2,1)S(1)}, bf16[8,256,128]{2,1,0:T(8,128)(2,1)}, u32[]{:S(2)}, u32[]{:S(2)}) collective-permute-start(bf16[8,256,128]{2,1,0:T(8,128)(2,1)S(1)} %all-to-all-done.1.raw_ref), channel_id=1, source_target_pairs={{0,16},{16,0},{32,48},{48,32},{64,80},{80,64},{96,112},{112,96},{1... | collective-permute-start | bytes 1572872 | tf_op jit(solution)/shard_map/ppermute | solution.py:283
  80.9 5.8 %key_prep.2 = (bf16[8,256,128]{2,1,0:T(8,128)(2,1)}, bf16[8,128,256]{2,1,0:T(8,128)(2,1)}) custom-call(bf16[8,256,128]{2,1,0:T(8,128)(2,1)} %copy-done.17, f32[1,128]{1,0:T(1,128)} %get-tuple-element.98.gain_ref), custom_call_target="tpu_custom_call" | custom-call | bytes 1572864 | tf_op jit(solution)/shard_map/key_prep/pallas_call | solution.py:56
  86.7 5.7 %all-to-all-done.4 = bf16[8,2,128,128]{3,2,1,0:T(8,128)(2,1)} async-done(((bf16[8,2,128,128]{3,2,1,0:T(8,128)(2,1)}), bf16[8,2,128,128]{3,2,1,0:T(8,128)(2,1)}, u32[]{:S(2)}, u32[]{:S(2)}) %all-to-all-start.4) | async-done | bytes 524320 | tf_op jit(solution)/shard_map/all_to_all | solution.py:279
  93.5 5.8 %key_prep.3 = (bf16[8,256,128]{2,1,0:T(8,128)(2,1)}, bf16[8,128,256]{2,1,0:T(8,128)(2,1)}) custom-call(bf16[8,256,128]{2,1,0:T(8,128)(2,1)} %collective-permute-done.raw_ref, f32[1,128]{1,0:T(1,128)} %get-tuple-element.98.gain_ref), custom_call_target="tpu_custom_call" | custom-call | bytes 1572864 | tf_op jit(solution)/shard_map/key_prep/pallas_call | solution.py:56
  99.2 3.2 %collective-permute-done.1.value_other = bf16[8,256,128]{2,1,0:T(8,128)(2,1)S(1)} collective-permute-done((bf16[8,256,128]{2,1,0:T(8,128)(2,1)S(1)}, bf16[8,256,128]{2,1,0:T(8,128)(2,1)S(1)}, u32[]{:S(2)}, u32[]{:S(2)}) %collective-permute-start.1) | collective-permute-done | bytes 524320 | tf_op jit(solution)/shard_map/ppermute | solution.py:283
  106.6 18.3 %attention.2 = (bf16[1024,128]{1,0:T(8,128)(2,1)}, f32[1,128]{1,0:T(1,128)S(1)}, f32[8,256,128]{2,1,0:T(8,128)S(1)}, f32[8,256,128]{2,1,0:T(8,128)S(1)}, f32[8,2...) custom-call(s32[4,4]{1,0:T(4,128)S(1)} %pad_add_fusion.bounds_ref, s32[1]{0:T(128)} %bitcast.5.half_ref, ...), custom_call_target="tpu_custom_call" | custom-call | flops 5368709120 | bytes 16777216 | tf_op jit(solution)/shard_map/attention/pallas_call | solution.py:193
  128.9 7.2 %all-to-all-start.3 = ((bf16[8,128,128]{2,1,0:T(8,128)(2,1)}), bf16[8,128,128]{2,1,0:T(8,128)(2,1)S(1)}, u32[]{:S(2)}, u32[]{:S(2)}) async-start(bf16[8,128,128]{2,1,0:T(8,128)(2,1)} %bitcast.18), calls=%async_computation.3 | async-start | bytes 524288 | tf_op jit(solution)/shard_map/all_to_all | solution.py:279
  144.1 18.3 %attention.3 = (bf16[1024,128]{1,0:T(8,128)(2,1)}, f32[1,128]{1,0:T(1,128)S(1)}, f32[8,256,128]{2,1,0:T(8,128)S(1)}, f32[8,256,128]{2,1,0:T(8,128)S(1)}, f32[8,2...) custom-call(s32[4,4]{1,0:T(4,128)S(1)} %pad_add_fusion.1.bounds_ref, s32[1]{0:T(128)} %bitcast.5.half_ref, ...), custom_call_target="tpu_custom_call" | custom-call | flops 5368709120 | bytes 16777216 | tf_op jit(solution)/shard_map/attention/pallas_call | solution.py:193
  163.5 3.1 %collective-permute-start.8 = (bf16[8,256,128]{2,1,0:T(8,128)(2,1)S(1)}, bf16[8,256,128]{2,1,0:T(8,128)(2,1)S(1)}, u32[]{:S(2)}, u32[]{:S(2)}) collective-permute-start(bf16[8,256,128]{2,1,0:T(8,128)(2,1)S(1)} %convert_element_type.60), channel_id=1, source_target_pairs={{0,16},{16,0},{32,48},{48,32},{64,80},{80,64},{96,112},{112,96},{1... | collective-permute-start | bytes 1572872 | tf_op jit(solution)/shard_map/ppermute | solution.py:283
  167.3 7.2 %all-to-all-start.5 = ((bf16[8,128,128]{2,1,0:T(8,128)(2,1)}), bf16[8,128,128]{2,1,0:T(8,128)(2,1)S(1)}, u32[]{:S(2)}, u32[]{:S(2)}) async-start(bf16[8,128,128]{2,1,0:T(8,128)(2,1)} %bitcast.31), calls=%async_computation.5 | async-start | bytes 524288 | tf_op jit(solution)/shard_map/all_to_all | solution.py:279
  174.5 5.4 %collective-permute-done.8.other_ref = bf16[8,256,128]{2,1,0:T(8,128)(2,1)S(1)} collective-permute-done((bf16[8,256,128]{2,1,0:T(8,128)(2,1)S(1)}, bf16[8,256,128]{2,1,0:T(8,128)(2,1)S(1)}, u32[]{:S(2)}, u32[]{:S(2)}) %collective-permute-start.8) | collective-permute-done | bytes 524320 | tf_op jit(solution)/shard_map/ppermute | solution.py:283
  180.8 6.3 %key_finish.1 = (bf16[8,256,128]{2,1,0:T(8,128)(2,1)}, f32[1,128]{1,0:T(1,128)}) custom-call(f32[8,256,128]{2,1,0:T(8,128)} %copy-done, bf16[8,256,128]{2,1,0:T(8,128)(2,1)} %copy-done.20, bf16[8,256,128]{2,1,0:T(8,128)(2,1)} %copy-done.17, f32[1,128]{1,0:T(1,128)} %get-tuple-element.98.gain_ref), custom_call_target="tpu_custom_call" | custom-call | bytes 2621440 | tf_op jit(solution)/shard_map/key_finish/pallas_call | solution.py:232
  188.6 1.9 add_convert_fusion
  190.5 7.2 %all-to-all-start.7 = ((bf16[8,256,128]{2,1,0:T(8,128)(2,1)}), bf16[8,256,128]{2,1,0:T(8,128)(2,1)S(1)}, u32[]{:S(2)}, u32[]{:S(2)}) async-start(bf16[8,256,128]{2,1,0:T(8,128)(2,1)} %add_convert_fusion), calls=%async_computation.7 | async-start | bytes 1048576 | tf_op jit(solution)/shard_map/all_to_all | solution.py:279
  197.9 8.7 %project.2 = bf16[4,128,1024]{2,1,0:T(8,128)(2,1)} custom-call(bf16[8,128,128]{2,1,0:T(8,128)(2,1)} %copy-done.18, bf16[4096,1024]{1,0:T(8,128)(2,1)} %weight_ref.3), custom_call_target="tpu_custom_call" | custom-call | flops 1073741824 | bytes 8388608 | tf_op jit(solution)/shard_map/project/pallas_call | solution.py:261
  209.3 1.8 collective-permute-start.2
  211.2 2.8 %collective-permute-start.12 = (f32[8,2,128]{2,0,1:T(8,128)S(1)}, f32[8,2,128]{2,0,1:T(8,128)S(1)}, u32[]{:S(2)}, u32[]{:S(2)}) collective-permute-start(f32[8,2,128]{2,0,1:T(8,128)S(1)} %fusion.41), channel_id=1, source_target_pairs={{0,16},{16,0},{32,48},{48,32},{64,80},{80,64},{96,112},{112,96},{1... | collective-permute-start | bytes 24584 | tf_op jit(solution)/shard_map/ppermute | solution.py:314
  214.0 2.4 collective-permute-done.12
  216.4 2.9 %collective-permute-start.3 = (bf16[128,1024]{1,0:T(8,128)(2,1)S(1)}, bf16[128,1024]{1,0:T(8,128)(2,1)S(1)}, u32[]{:S(2)}, u32[]{:S(2)}) collective-permute-start(bf16[128,1024]{1,0:T(8,128)(2,1)S(1)} %get-tuple-element.71), channel_id=1, source_target_pairs={{0,8},{4,12},{8,0},{12,4},{1,9},{5,13},{9,1},{13,5},{2,10},{6,14},... | collective-permute-start | bytes 786440 | tf_op jit(solution)/shard_map/ppermute | solution.py:303
  220.7 2.9 %collective-permute-start.14 = (f32[8,2,128]{2,0,1:T(8,128)S(1)}, f32[8,2,128]{2,0,1:T(8,128)S(1)}, u32[]{:S(2)}, u32[]{:S(2)}) collective-permute-start(f32[8,2,128]{2,0,1:T(8,128)S(1)} %add.257), channel_id=1, source_target_pairs={{0,64},{16,80},{32,96},{48,112},{64,0},{80,16},{96,32},{112,48},{1... | collective-permute-start | bytes 24584 | tf_op jit(solution)/shard_map/ppermute | solution.py:314
  223.6 8.6 %project.3 = bf16[4,128,1024]{2,1,0:T(8,128)(2,1)} custom-call(bf16[8,128,128]{2,1,0:T(8,128)(2,1)} %copy-done.19, bf16[4096,1024]{1,0:T(8,128)(2,1)} %weight_ref.3), custom_call_target="tpu_custom_call" | custom-call | flops 1073741824 | bytes 8388608 | tf_op jit(solution)/shard_map/project/pallas_call | solution.py:261
  232.2 3.7 %collective-permute-start.15 = (f32[8,2,128]{2,0,1:T(8,128)S(1)}, f32[8,2,128]{2,0,1:T(8,128)S(1)}, u32[]{:S(2)}, u32[]{:S(2)}) collective-permute-start(f32[8,2,128]{2,0,1:T(8,128)S(1)} %add.258), channel_id=1, source_target_pairs={{0,128},{16,144},{32,160},{48,176},{64,192},{80,208},{96,224},{112... | collective-permute-start | bytes 24584 | tf_op jit(solution)/shard_map/ppermute | solution.py:314
  235.9 5.1 %all-to-all-start.6 = ((bf16[8,256,128]{2,1,0:T(8,128)(2,1)}), bf16[8,256,128]{2,1,0:T(8,128)(2,1)S(1)}, u32[]{:S(2)}, u32[]{:S(2)}) async-start(bf16[8,256,128]{2,1,0:T(8,128)(2,1)} %get-tuple-element.35), calls=%async_computation.6 | async-start | bytes 1048576 | tf_op jit(solution)/shard_map/all_to_all | solution.py:279
  243.8 1.9 collective-permute-start.7
  247.5 6.6 %collective-permute-done.5 = bf16[128,1024]{1,0:T(8,128)(2,1)S(1)} collective-permute-done((bf16[128,1024]{1,0:T(8,128)(2,1)S(1)}, bf16[128,1024]{1,0:T(8,128)(2,1)S(1)}, u32[]{:S(2)}, u32[]{:S(2)}) %collective-permute-start.5) | collective-permute-done | bytes 262176 | tf_op jit(solution)/shard_map/ppermute | solution.py:303
  (120 shorter events, 47.1 us)
Async XLA Ops:
  0.6 53.1 %copy-start.21 = (s32[1,8]{1,0:T(1,128)S(1)}, s32[1,8]{1,0:T(1,128)}, u32[]{:S(2)}) copy-start(s32[1,8]{1,0:T(1,128)} %param.15) | copy-start | bytes 100
  2.9 24.6 %all-to-all-start.1 = ((bf16[8,256,128]{2,1,0:T(8,128)(2,1)}), bf16[8,256,128]{2,1,0:T(8,128)(2,1)S(1)}, u32[]{:S(2)}, u32[]{:S(2)}) async-start(bf16[8,256,128]{2,1,0:T(8,128)(2,1)} %bitcast.15), calls=%async_computation.1 | async-start | bytes 1048576 | tf_op jit(solution)/shard_map/all_to_all | solution.py:279
  27.5 53.4 %copy-start.17 = (bf16[8,256,128]{2,1,0:T(8,128)(2,1)}, bf16[8,256,128]{2,1,0:T(8,128)(2,1)S(1)}, u32[]{:S(2)}) copy-start(bf16[8,256,128]{2,1,0:T(8,128)(2,1)S(1)} %all-to-all-done.1.raw_ref) | copy-start | bytes 1572868
  27.5 21.4 %all-to-all-start = ((bf16[8,2,128,128]{3,2,1,0:T(8,128)(2,1)}), bf16[8,2,128,128]{3,2,1,0:T(8,128)(2,1)S(1)}, u32[]{:S(2)}, u32[]{:S(2)}) async-start(bf16[8,2,128,128]{3,2,1,0:T(8,128)(2,1)} %copy.53), calls=%async_computation | async-start | bytes 1048576 | tf_op jit(solution)/shard_map/all_to_all | solution.py:279
  48.9 21.4 %all-to-all-start.2 = ((bf16[8,256,128]{2,1,0:T(8,128)(2,1)}), bf16[8,256,128]{2,1,0:T(8,128)(2,1)S(1)}, u32[]{:S(2)}, u32[]{:S(2)}) async-start(bf16[8,256,128]{2,1,0:T(8,128)(2,1)} %bitcast.17), calls=%async_computation.2 | async-start | bytes 1048576 | tf_op jit(solution)/shard_map/all_to_all | solution.py:279
  70.3 22.1 %all-to-all-start.4 = ((bf16[8,2,128,128]{3,2,1,0:T(8,128)(2,1)}), bf16[8,2,128,128]{3,2,1,0:T(8,128)(2,1)}, u32[]{:S(2)}, u32[]{:S(2)}) async-start(bf16[8,2,128,128]{3,2,1,0:T(8,128)(2,1)} %copy.60), calls=%async_computation.4 | async-start | bytes 1048576 | tf_op jit(solution)/shard_map/all_to_all | solution.py:279
  76.1 17.4 %collective-permute-start = (bf16[8,256,128]{2,1,0:T(8,128)(2,1)S(1)}, bf16[8,256,128]{2,1,0:T(8,128)(2,1)}, u32[]{:S(2)}, u32[]{:S(2)}) collective-permute-start(bf16[8,256,128]{2,1,0:T(8,128)(2,1)S(1)} %all-to-all-done.1.raw_ref), channel_id=1, source_target_pairs={{0,16},{16,0},{32,48},{48,32},{64,80},{80,64},{96,112},{112,96},{1... | collective-permute-start | bytes 1572872 | tf_op jit(solution)/shard_map/ppermute | solution.py:283
  79.1 23.3 %collective-permute-start.1 = (bf16[8,256,128]{2,1,0:T(8,128)(2,1)S(1)}, bf16[8,256,128]{2,1,0:T(8,128)(2,1)S(1)}, u32[]{:S(2)}, u32[]{:S(2)}) collective-permute-start(bf16[8,256,128]{2,1,0:T(8,128)(2,1)S(1)} %all-to-all-done.2.value_own), channel_id=1, source_target_pairs={{0,16},{16,0},{32,48},{48,32},{64,80},{80,64},{96,112},{112,96},{1... | collective-permute-start | bytes 1572872 | tf_op jit(solution)/shard_map/ppermute | solution.py:283
  106.6 29.5 %copy-start.2 = (bf16[8,256,128]{2,1,0:T(8,128)(2,1)S(1)}, bf16[8,256,128]{2,1,0:T(8,128)(2,1)}, u32[]{:S(2)}) copy-start(bf16[8,256,128]{2,1,0:T(8,128)(2,1)} %get-tuple-element.23.norm_own) | copy-start | bytes 1572868
  128.9 38.4 %all-to-all-start.3 = ((bf16[8,128,128]{2,1,0:T(8,128)(2,1)}), bf16[8,128,128]{2,1,0:T(8,128)(2,1)S(1)}, u32[]{:S(2)}, u32[]{:S(2)}) async-start(bf16[8,128,128]{2,1,0:T(8,128)(2,1)} %bitcast.18), calls=%async_computation.3 | async-start | bytes 524288 | tf_op jit(solution)/shard_map/all_to_all | solution.py:279
  139.2 1.2 copy-start.10
  140.5 1.2 copy-start.12
  142.9 1.2 copy-start.16
  163.5 16.5 %collective-permute-start.8 = (bf16[8,256,128]{2,1,0:T(8,128)(2,1)S(1)}, bf16[8,256,128]{2,1,0:T(8,128)(2,1)S(1)}, u32[]{:S(2)}, u32[]{:S(2)}) collective-permute-start(bf16[8,256,128]{2,1,0:T(8,128)(2,1)S(1)} %convert_element_type.60), channel_id=1, source_target_pairs={{0,16},{16,0},{32,48},{48,32},{64,80},{80,64},{96,112},{112,96},{1... | collective-permute-start | bytes 1572872 | tf_op jit(solution)/shard_map/ppermute | solution.py:283
  166.7 21.9 %collective-permute-start.9 = (bf16[8,256,128]{2,1,0:T(8,128)(2,1)S(1)}, bf16[8,256,128]{2,1,0:T(8,128)(2,1)}, u32[]{:S(2)}, u32[]{:S(2)}) collective-permute-start(bf16[8,256,128]{2,1,0:T(8,128)(2,1)S(1)} %convert_element_type.61), channel_id=1, source_target_pairs={{0,16},{16,0},{32,48},{48,32},{64,80},{80,64},{96,112},{112,96},{1... | collective-permute-start | bytes 1572872 | tf_op jit(solution)/shard_map/ppermute | solution.py:283
  167.3 30.5 %copy-start.18 = (bf16[8,128,128]{2,1,0:T(8,128)(2,1)}, bf16[8,128,128]{2,1,0:T(8,128)(2,1)S(1)}, u32[]{:S(2)}) copy-start(bf16[8,128,128]{2,1,0:T(8,128)(2,1)S(1)} %all-to-all-done.3.rows_ref) | copy-start | bytes 786436
  167.3 23.2 %all-to-all-start.5 = ((bf16[8,128,128]{2,1,0:T(8,128)(2,1)}), bf16[8,128,128]{2,1,0:T(8,128)(2,1)S(1)}, u32[]{:S(2)}, u32[]{:S(2)}) async-start(bf16[8,128,128]{2,1,0:T(8,128)(2,1)} %bitcast.31), calls=%async_computation.5 | async-start | bytes 524288 | tf_op jit(solution)/shard_map/all_to_all | solution.py:279
  190.5 33.1 %copy-start.19 = (bf16[8,128,128]{2,1,0:T(8,128)(2,1)}, bf16[8,128,128]{2,1,0:T(8,128)(2,1)S(1)}, u32[]{:S(2)}) copy-start(bf16[8,128,128]{2,1,0:T(8,128)(2,1)S(1)} %all-to-all-done.5.rows_ref) | copy-start | bytes 786436
  190.5 45.4 %all-to-all-start.7 = ((bf16[8,256,128]{2,1,0:T(8,128)(2,1)}), bf16[8,256,128]{2,1,0:T(8,128)(2,1)S(1)}, u32[]{:S(2)}, u32[]{:S(2)}) async-start(bf16[8,256,128]{2,1,0:T(8,128)(2,1)} %add_convert_fusion), calls=%async_computation.7 | async-start | bytes 1048576 | tf_op jit(solution)/shard_map/all_to_all | solution.py:279
  197.8 8.8 %collective-permute-start.10 = (f32[8,2,128]{2,0,1:T(8,128)S(1)}, f32[8,2,128]{2,0,1:T(8,128)S(1)}, u32[]{:S(2)}, u32[]{:S(2)}) collective-permute-start(f32[8,2,128]{2,0,1:T(8,128)S(1)} %broadcast_select_fusion), channel_id=1, source_target_pairs={{0,1},{1,0},{2,3},{3,2},{4,5},{5,4},{6,7},{7,6},{8,9},{9,8},{10,11... | collective-permute-start | bytes 24584 | tf_op jit(solution)/shard_map/ppermute | solution.py:312
  206.6 4.5 %collective-permute-start.11 = (f32[8,2,128]{2,0,1:T(8,128)S(1)}, f32[8,2,128]{2,0,1:T(8,128)S(1)}, u32[]{:S(2)}, u32[]{:S(2)}) collective-permute-start(f32[8,2,128]{2,0,1:T(8,128)S(1)} %fusion.32), channel_id=1, source_target_pairs={{0,2},{1,3},{2,0},{3,1},{4,6},{5,7},{6,4},{7,5},{8,10},{9,11},{10,... | collective-permute-start | bytes 24584 | tf_op jit(solution)/shard_map/ppermute | solution.py:312
  209.3 34.5 %collective-permute-start.2 = (bf16[128,1024]{1,0:T(8,128)(2,1)S(1)}, bf16[128,1024]{1,0:T(8,128)(2,1)S(1)}, u32[]{:S(2)}, u32[]{:S(2)}) collective-permute-start(bf16[128,1024]{1,0:T(8,128)(2,1)S(1)} %get-tuple-element.69), channel_id=1, source_target_pairs={{0,4},{4,8},{8,12},{12,0},{1,5},{5,9},{9,13},{13,1},{2,6},{6,10},{... | collective-permute-start | bytes 786440 | tf_op jit(solution)/shard_map/ppermute | solution.py:303
  211.2 5.2 %collective-permute-start.12 = (f32[8,2,128]{2,0,1:T(8,128)S(1)}, f32[8,2,128]{2,0,1:T(8,128)S(1)}, u32[]{:S(2)}, u32[]{:S(2)}) collective-permute-start(f32[8,2,128]{2,0,1:T(8,128)S(1)} %fusion.41), channel_id=1, source_target_pairs={{0,16},{16,0},{32,48},{48,32},{64,80},{80,64},{96,112},{112,96},{1... | collective-permute-start | bytes 24584 | tf_op jit(solution)/shard_map/ppermute | solution.py:314
  216.4 4.3 %collective-permute-start.13 = (f32[8,2,128]{2,0,1:T(8,128)S(1)}, f32[8,2,128]{2,0,1:T(8,128)S(1)}, u32[]{:S(2)}, u32[]{:S(2)}) collective-permute-start(f32[8,2,128]{2,0,1:T(8,128)S(1)} %add.256), channel_id=1, source_target_pairs={{0,32},{16,48},{32,0},{48,16},{64,96},{80,112},{96,64},{112,80},{1... | collective-permute-start | bytes 24584 | tf_op jit(solution)/shard_map/ppermute | solution.py:314
  216.4 29.9 %collective-permute-start.3 = (bf16[128,1024]{1,0:T(8,128)(2,1)S(1)}, bf16[128,1024]{1,0:T(8,128)(2,1)S(1)}, u32[]{:S(2)}, u32[]{:S(2)}) collective-permute-start(bf16[128,1024]{1,0:T(8,128)(2,1)S(1)} %get-tuple-element.71), channel_id=1, source_target_pairs={{0,8},{4,12},{8,0},{12,4},{1,9},{5,13},{9,1},{13,5},{2,10},{6,14},... | collective-permute-start | bytes 786440 | tf_op jit(solution)/shard_map/ppermute | solution.py:303
  219.3 27.0 %collective-permute-start.4 = (bf16[128,1024]{1,0:T(8,128)(2,1)S(1)}, bf16[128,1024]{1,0:T(8,128)(2,1)S(1)}, u32[]{:S(2)}, u32[]{:S(2)}) collective-permute-start(bf16[128,1024]{1,0:T(8,128)(2,1)S(1)} %get-tuple-element.70), channel_id=1, source_target_pairs={{0,12},{4,0},{8,4},{12,8},{1,13},{5,1},{9,5},{13,9},{2,14},{6,2},{... | collective-permute-start | bytes 786440 | tf_op jit(solution)/shard_map/ppermute | solution.py:303
  220.7 11.5 %collective-permute-start.14 = (f32[8,2,128]{2,0,1:T(8,128)S(1)}, f32[8,2,128]{2,0,1:T(8,128)S(1)}, u32[]{:S(2)}, u32[]{:S(2)}) collective-permute-start(f32[8,2,128]{2,0,1:T(8,128)S(1)} %add.257), channel_id=1, source_target_pairs={{0,64},{16,80},{32,96},{48,112},{64,0},{80,16},{96,32},{112,48},{1... | collective-permute-start | bytes 24584 | tf_op jit(solution)/shard_map/ppermute | solution.py:314
  232.2 10.7 %collective-permute-start.15 = (f32[8,2,128]{2,0,1:T(8,128)S(1)}, f32[8,2,128]{2,0,1:T(8,128)S(1)}, u32[]{:S(2)}, u32[]{:S(2)}) collective-permute-start(f32[8,2,128]{2,0,1:T(8,128)S(1)} %add.258), channel_id=1, source_target_pairs={{0,128},{16,144},{32,160},{48,176},{64,192},{80,208},{96,224},{112... | collective-permute-start | bytes 24584 | tf_op jit(solution)/shard_map/ppermute | solution.py:314
  235.9 22.0 %all-to-all-start.6 = ((bf16[8,256,128]{2,1,0:T(8,128)(2,1)}), bf16[8,256,128]{2,1,0:T(8,128)(2,1)S(1)}, u32[]{:S(2)}, u32[]{:S(2)}) async-start(bf16[8,256,128]{2,1,0:T(8,128)(2,1)} %get-tuple-element.35), calls=%async_computation.6 | async-start | bytes 1048576 | tf_op jit(solution)/shard_map/all_to_all | solution.py:279
  242.2 11.9 %collective-permute-start.5 = (bf16[128,1024]{1,0:T(8,128)(2,1)S(1)}, bf16[128,1024]{1,0:T(8,128)(2,1)S(1)}, u32[]{:S(2)}, u32[]{:S(2)}) collective-permute-start(bf16[128,1024]{1,0:T(8,128)(2,1)S(1)} %get-tuple-element.72), channel_id=1, source_target_pairs={{0,4},{4,8},{8,12},{12,0},{1,5},{5,9},{9,13},{13,1},{2,6},{6,10},{... | collective-permute-start | bytes 786440 | tf_op jit(solution)/shard_map/ppermute | solution.py:303
  242.9 11.2 %collective-permute-start.6 = (bf16[128,1024]{1,0:T(8,128)(2,1)S(1)}, bf16[128,1024]{1,0:T(8,128)(2,1)S(1)}, u32[]{:S(2)}, u32[]{:S(2)}) collective-permute-start(bf16[128,1024]{1,0:T(8,128)(2,1)S(1)} %get-tuple-element.74), channel_id=1, source_target_pairs={{0,8},{4,12},{8,0},{12,4},{1,9},{5,13},{9,1},{13,5},{2,10},{6,14},... | collective-permute-start | bytes 786440 | tf_op jit(solution)/shard_map/ppermute | solution.py:303
  243.8 10.9 %collective-permute-start.7 = (bf16[128,1024]{1,0:T(8,128)(2,1)S(1)}, bf16[128,1024]{1,0:T(8,128)(2,1)S(1)}, u32[]{:S(2)}, u32[]{:S(2)}) collective-permute-start(bf16[128,1024]{1,0:T(8,128)(2,1)S(1)} %get-tuple-element.73), channel_id=1, source_target_pairs={{0,12},{4,0},{8,4},{12,8},{1,13},{5,1},{9,5},{13,9},{2,14},{6,2},{... | collective-permute-start | bytes 786440 | tf_op jit(solution)/shard_map/ppermute | solution.py:303
  (14 other events, 14.3 us)

commit v2 on v1

v2 whole, which is shorter than its diff:
```python
import functools

import jax
import jax.numpy as jnp
from jax import lax
from jax.experimental import pallas as pl
from jax.experimental.pallas import tpu as pltpu
from jax.sharding import PartitionSpec as P

NORM_EPSILON = 1e-05
MASKED_SCORE = -1e30
HEADS_LOCAL = 8
HD = 128
ROWS = 256
LANES = 256
PAIRS = 2
FACTOR = HD ** (-0.5)
EXP2_FACTOR = FACTOR * 1.4426950408889634
VMEM_LIMIT = 60 * 1024 * 1024

DEPTH = 8
Z_GROUPS = [[2 * z + half for z in range(8)] for half in range(2)]
HALF_SWAP = [(index, index ^ 1) for index in range(16)]


def nt_dot(a, b):
    return lax.dot_general(a, b, (((1,), (1,)), ((), ())), preferred_element_type=jnp.float32)


def nn_dot(a, b):
    return lax.dot_general(a, b, (((1,), (0,)), ((), ())), preferred_element_type=jnp.float32)


def unit_norm(raw):
    widened = raw.astype(jnp.float32)
    centered = widened - jnp.mean(widened, axis=1, keepdims=True)
    inverse = lax.rsqrt(jnp.mean(centered * centered, axis=1, keepdims=True) + NORM_EPSILON)
    return centered * inverse, inverse


def unit_norm_backward(grad_norm, unit_rows, inverse, gain):
    scaled = grad_norm * gain
    mean_grad = jnp.mean(scaled, axis=1, keepdims=True)
    mean_cross = jnp.mean(scaled * unit_rows, axis=1, keepdims=True)
    return (scaled - mean_grad - unit_rows * mean_cross) * inverse


VMEM_SPEC = pl.BlockSpec(memory_space=pltpu.VMEM)
SMEM_SPEC = pl.BlockSpec(memory_space=pltpu.SMEM)
ANY_SPEC = pl.BlockSpec(memory_space=pltpu.HBM)


def pack_kernel(first_ref, second_ref, out_ref, held_ref, in_sem, out_sem):
    def inward(head, which):
        return pltpu.make_async_copy(
            (first_ref, second_ref)[which].at[:, head * HD : (head + 1) * HD],
            held_ref.at[head, which],
            in_sem.at[head, which],
        )

    def outward(head):
        return pltpu.make_async_copy(held_ref.at[head], out_ref.at[head], out_sem.at[head])

    for head in range(HEADS_LOCAL):
        for which in range(2):
            inward(head, which).start()
    for head in range(HEADS_LOCAL):
        for which in range(2):
            inward(head, which).wait()
        outward(head).start()
    for head in range(HEADS_LOCAL):
        outward(head).wait()


def pack(first, second):
    shape = (HEADS_LOCAL, 2, ROWS, HD)
    return pl.pallas_call(
        pack_kernel,
        in_specs=[ANY_SPEC, ANY_SPEC],
        out_specs=ANY_SPEC,
        out_shape=jax.ShapeDtypeStruct(shape, jnp.bfloat16),
        scratch_shapes=[
            pltpu.VMEM(shape, jnp.bfloat16),
            pltpu.SemaphoreType.DMA((HEADS_LOCAL, 2)),
            pltpu.SemaphoreType.DMA((HEADS_LOCAL,)),
        ],
        cost_estimate=pl.CostEstimate(flops=0, bytes_accessed=2**22, transcendentals=0),
        name="pack",
    )(first, second)


def unpack_kernel(pieces_ref, *refs):
    outs, (held_ref, in_sem, out_sem) = refs[:2], refs[2:]

    def inward(head):
        return pltpu.make_async_copy(pieces_ref.at[head], held_ref.at[head], in_sem.at[head])

    def outward(head, which):
        return pltpu.make_async_copy(
            held_ref.at[head, which * ROWS : (which + 1) * ROWS],
            outs[which].at[:, head * HD : (head + 1) * HD],
            out_sem.at[head, which],
        )

    for head in range(HEADS_LOCAL):
        inward(head).start()
    for head in range(HEADS_LOCAL):
        inward(head).wait()
        for which in range(2):
            outward(head, which).start()
    for head in range(HEADS_LOCAL):
        for which in range(2):
            outward(head, which).wait()


def unpack(pieces):
    rows = jax.ShapeDtypeStruct((ROWS, HEADS_LOCAL * HD), jnp.bfloat16)
    return pl.pallas_call(
        unpack_kernel,
        in_specs=[ANY_SPEC],
        out_specs=[ANY_SPEC, ANY_SPEC],
        out_shape=[rows, rows],
        scratch_shapes=[
            pltpu.VMEM(pieces.shape, jnp.bfloat16),
            pltpu.SemaphoreType.DMA((HEADS_LOCAL,)),
            pltpu.SemaphoreType.DMA((HEADS_LOCAL, 2)),
        ],
        cost_estimate=pl.CostEstimate(flops=0, bytes_accessed=2**22, transcendentals=0),
        name="unpack",
    )(pieces)


def whole(*shape):
    return pl.BlockSpec(shape, lambda i: (0,) * len(shape))


def key_prep_kernel(gain_ref, raw_ref, norm_ref, turned_ref, held_raw, held_norm, held_turned, in_sem, out_sem):
    inward = [
        pltpu.make_async_copy(raw_ref.at[tile, 0], held_raw.at[tile], in_sem.at[tile])
        for tile in range(DEPTH)
    ]
    outward = [
        pltpu.make_async_copy(held_norm, norm_ref, out_sem.at[0]),
        pltpu.make_async_copy(held_turned, turned_ref, out_sem.at[1]),
    ]
    for copy in inward:
        copy.start()
    for tile in range(DEPTH):
        inward[tile].wait()
        unit_rows, _ = unit_norm(held_raw[tile])
        scaled = unit_rows * gain_ref[...]
        held_norm[tile] = scaled.astype(jnp.bfloat16)
        held_turned[tile] = scaled.T.astype(jnp.bfloat16)
    for copy in outward:
        copy.start()
    for copy in outward:
        copy.wait()


def key_prep(gain, keys_values):
    shapes = [(DEPTH, ROWS, HD), (DEPTH, HD, ROWS)]
    return pl.pallas_call(
        key_prep_kernel,
        in_specs=[VMEM_SPEC, ANY_SPEC],
        out_specs=[ANY_SPEC] * 2,
        out_shape=[jax.ShapeDtypeStruct(shape, jnp.bfloat16) for shape in shapes],
        scratch_shapes=[
            pltpu.VMEM(shapes[0], jnp.bfloat16),
            pltpu.VMEM(shapes[0], jnp.bfloat16),
            pltpu.VMEM(shapes[1], jnp.bfloat16),
            pltpu.SemaphoreType.DMA((DEPTH,)),
            pltpu.SemaphoreType.DMA((2,)),
        ],
        cost_estimate=pl.CostEstimate(flops=0, bytes_accessed=2**22, transcendentals=0),
        name="key_prep",
    )(gain, keys_values)


def fold(tile):
    return tile.reshape(tile.shape[0] // 8, 8, tile.shape[1])


def attention_kernel(bounds_ref, half_ref, pos_ref, low_ref, gain_ref, *refs):
    queries_grads_ref, refs = refs[0], refs[1:]
    norms, turned, raws = refs[0:2], refs[2:4], refs[4:6]
    refs = refs[6:]
    dq_ref, gain_grad_ref, own_ref, other_ref = refs[:4]
    (
        chance_ref,
        dot_ref,
        peak_ref,
        dk_ref,
        dv_ref,
        dqt_ref,
        held_norm,
        held_turned,
        held_value,
        held_query,
        held_dq,
        cast_ref,
        in_sem,
        out_sem,
    ) = refs[4:]
    half = half_ref[0]
    moves = [(queries_grads_ref, held_query)]
    for side in range(2):
        moves.append((norms[side], held_norm.at[side]))
        moves.append((turned[side], held_turned.at[side]))
        moves.append((raws[side].at[:, 1], held_value.at[side]))
    loads = [
        pltpu.make_async_copy(source, target, in_sem.at[index])
        for index, (source, target) in enumerate(moves)
    ]
    for copy in loads:
        copy.start()
    dk_ref[...] = jnp.zeros_like(dk_ref)
    dv_ref[...] = jnp.zeros_like(dv_ref)
    gain_grad_ref[...] = jnp.zeros_like(gain_grad_ref)
    for copy in loads:
        copy.wait()

    def block_body(block, carry):
        unit_rows, inverse = unit_norm(held_query[block, 0])
        query = (unit_rows * gain_ref[...]).astype(jnp.bfloat16)
        grad = held_query[block, 1]
        pos = pos_ref[pl.ds(block, 1), :]
        low = low_ref[pl.ds(block, 1), :]
        first, inner, diagonal, last = (bounds_ref[block, i] for i in range(4))

        def scores_body(masked, step, sums):
            best, total, weighted = sums
            parts = []
            peak = jnp.full((8, LANES), MASKED_SCORE, jnp.float32)
            for pair in range(PAIRS):
                tile = step * PAIRS + pair
                for side in range(2):
                    scores = nt_dot(held_norm[side, tile], query)
                    mask = None
                    if masked:
                        which = half if side == 0 else 1 - half
                        key_pos = (2 * tile + which) * ROWS + lax.broadcasted_iota(
                            jnp.int32, (ROWS, LANES), 0
                        )
                        mask = (key_pos >= low) & (key_pos <= pos)
                        scores = jnp.where(mask, scores, MASKED_SCORE)
                    parts.append((tile, side, scores, mask))
                    peak = jnp.maximum(peak, jnp.max(fold(scores), axis=0))
            new_best = jnp.maximum(best, jnp.max(peak, axis=0, keepdims=True) * EXP2_FACTOR)
            scale = jnp.exp2(best - new_best)
            total, weighted = total * scale, weighted * scale
            for tile, side, scores, mask in parts:
                shifted = jnp.exp2(scores * EXP2_FACTOR - new_best)
                if masked:
                    shifted = jnp.where(mask, shifted, 0.0)
                dots = nt_dot(held_value[side, tile], grad)
                chance_ref[tile, side * ROWS : (side + 1) * ROWS] = shifted
                dot_ref[tile, side * ROWS : (side + 1) * ROWS] = dots
                total = total + jnp.sum(fold(shifted), axis=0)
                weighted = weighted + jnp.sum(fold(shifted * dots), axis=0)
            peak_ref[pl.ds(step, 1), :] = new_best
            return new_best, total, weighted

        empty = jnp.zeros((8, LANES), jnp.float32)
        sums = (jnp.full((1, LANES), MASKED_SCORE, jnp.float32), empty, empty)
        sums = lax.fori_loop(first, inner, functools.partial(scores_body, True), sums)
        sums = lax.fori_loop(inner, diagonal, functools.partial(scores_body, False), sums)
        best, total, weighted = lax.fori_loop(
            diagonal, last, functools.partial(scores_body, True), sums
        )
        share = 1.0 / jnp.sum(total, axis=0, keepdims=True)
        delta = jnp.sum(weighted, axis=0, keepdims=True) * share
        dqt_ref[...] = jnp.zeros_like(dqt_ref)

        def grads_body(step, carry):
            step_share = share * jnp.exp2(peak_ref[pl.ds(step, 1), :] - best)
            score_grads, norms_t = [], []
            for pair in range(PAIRS):
                tile = step * PAIRS + pair
                chance = chance_ref[tile] * step_share
                score_grad = (chance * (dot_ref[tile] - delta)).astype(jnp.bfloat16)
                dv_ref[tile] += nn_dot(chance.astype(jnp.bfloat16), grad)
                dk_ref[tile] += nn_dot(score_grad, query)
                score_grads.append(score_grad)
                norms_t += [held_turned[0, tile], held_turned[1, tile]]
            dqt_ref[...] += nn_dot(
                jnp.concatenate(norms_t, axis=1), jnp.concatenate(score_grads, axis=0)
            )
            return carry

        lax.fori_loop(first, last, grads_body, 0)
        query_grad = dqt_ref[...].T * FACTOR
        held_dq[block] = unit_norm_backward(
            query_grad, unit_rows, inverse, gain_ref[...]
        ).astype(jnp.bfloat16)
        gain_grad_ref[...] += jnp.sum(query_grad * unit_rows, axis=0, keepdims=True)
        return carry

    lax.fori_loop(0, DEPTH, block_body, 0)
    cast_ref[:, 0] = dv_ref[:, ROWS:].astype(jnp.bfloat16)
    cast_ref[:, 1] = dk_ref[:, ROWS:].astype(jnp.bfloat16)
    moves = [
        (held_dq, dq_ref),
        (cast_ref, other_ref),
        (dv_ref.at[:, :ROWS], own_ref.at[0]),
        (dk_ref.at[:, :ROWS], own_ref.at[1]),
    ]
    copies = [
        pltpu.make_async_copy(source, target, out_sem.at[index])
        for index, (source, target) in enumerate(moves)
    ]
    for copy in copies:
        copy.start()
    for copy in copies:
        copy.wait()


def attention(bounds, half, pos, low, gain, queries_grads, keys, raws):
    tiles = DEPTH
    pairs = DEPTH * tiles * ROWS * 2 * ROWS
    wide = pltpu.VMEM((tiles, 2 * ROWS, LANES), jnp.float32)
    total = pltpu.VMEM((tiles, 2 * ROWS, HD), jnp.float32)
    rows = pltpu.VMEM((tiles, ROWS, HD), jnp.bfloat16)
    outs = [
        jax.ShapeDtypeStruct((DEPTH, ROWS, HD), jnp.bfloat16),
        jax.ShapeDtypeStruct((1, HD), jnp.float32),
        jax.ShapeDtypeStruct((2, DEPTH, ROWS, HD), jnp.float32),
        jax.ShapeDtypeStruct((DEPTH, 2, ROWS, HD), jnp.bfloat16),
    ]
    return pl.pallas_call(
        attention_kernel,
        in_specs=[SMEM_SPEC, SMEM_SPEC, VMEM_SPEC, VMEM_SPEC, VMEM_SPEC] + [ANY_SPEC] * 7,
        out_specs=[ANY_SPEC, VMEM_SPEC, ANY_SPEC, ANY_SPEC],
        out_shape=outs,
        scratch_shapes=[
            wide, wide, pltpu.VMEM((tiles, LANES), jnp.float32), total, total,
            pltpu.VMEM((HD, LANES), jnp.float32),
            pltpu.VMEM((2, tiles, ROWS, HD), jnp.bfloat16),
            pltpu.VMEM((2, tiles, HD, ROWS), jnp.bfloat16),
            pltpu.VMEM((2, tiles, ROWS, HD), jnp.bfloat16),
            pltpu.VMEM((DEPTH, 2, ROWS, HD), jnp.bfloat16),
            rows, pltpu.VMEM((DEPTH, 2, ROWS, HD), jnp.bfloat16),
            pltpu.SemaphoreType.DMA((7,)),
            pltpu.SemaphoreType.DMA((4,)),
        ],
        compiler_params=pltpu.CompilerParams(vmem_limit_bytes=VMEM_LIMIT),
        cost_estimate=pl.CostEstimate(
            flops=12 * pairs * HD, bytes_accessed=2**23, transcendentals=pairs
        ),
        name="attention",
    )(
        bounds, half, pos, low, gain, queries_grads,
        *[key[0] for key in keys], *[key[1] for key in keys], *raws,
    )


def key_gain_kernel(own_ref, other_ref, raw_own, raw_other, out_ref):
    total = jnp.zeros((ROWS, HD), jnp.float32)
    for tile in range(DEPTH):
        for grad, raw_ref in ((own_ref[0, tile], raw_own), (other_ref[tile, 0], raw_other)):
            total += grad.astype(jnp.float32) * unit_norm(raw_ref[tile, 0])[0]
    out_ref[...] = jnp.sum(total, axis=0, keepdims=True) * FACTOR


def keys_of_pair():
    return pl.BlockSpec((DEPTH, 1, ROWS, HD), lambda i: (0, 0, 0, 0))


def key_gain(own, other, raws):
    return pl.pallas_call(
        key_gain_kernel,
        grid=(1,),
        in_specs=[
            pl.BlockSpec((1, DEPTH, ROWS, HD), lambda i: (1, 0, 0, 0)),
            pl.BlockSpec((DEPTH, 1, ROWS, HD), lambda i: (0, 1, 0, 0)),
            keys_of_pair(),
            keys_of_pair(),
        ],
        out_specs=whole(1, HD),
        out_shape=jax.ShapeDtypeStruct((1, HD), jnp.float32),
        cost_estimate=pl.CostEstimate(flops=0, bytes_accessed=5 * 2**19, transcendentals=0),
        name="key_gain",
    )(own, other, *raws)


def finish_kernel(
    own_ref, other_ref, raw_ref, gain_ref, out_ref
):
    for tile in range(DEPTH):
        value_sum = own_ref[0, tile] + other_ref[tile, 0].astype(jnp.float32)
        out_ref[tile, :ROWS] = value_sum.astype(jnp.bfloat16)
        grad_norm = (own_ref[1, tile] + other_ref[tile, 1].astype(jnp.float32)) * FACTOR
        unit_rows, inverse = unit_norm(raw_ref[tile, 0])
        out_ref[tile, ROWS : 2 * ROWS] = unit_norm_backward(
            grad_norm, unit_rows, inverse, gain_ref[...]
        ).astype(jnp.bfloat16)


def finish(own, other, raw, gain):
    rows = 2 * ROWS
    return pl.pallas_call(
        finish_kernel,
        grid=(1,),
        in_specs=[whole(2, DEPTH, ROWS, HD), whole(DEPTH, 2, ROWS, HD)]
        + [keys_of_pair(), whole(1, HD)],
        out_specs=whole(DEPTH, rows, HD),
        out_shape=jax.ShapeDtypeStruct((DEPTH, rows, HD), jnp.bfloat16),
        cost_estimate=pl.CostEstimate(flops=0, bytes_accessed=2**23, transcendentals=0),
        name="finish",
    )(own, other, raw, gain)


def project_kernel(part_ref, rows_ref, weight_ref, *refs):
    outs, joined_ref = refs[:-1], refs[-1]
    width = outs[0].shape[1]
    for head in range(rows_ref.shape[0]):
        joined_ref[:, head * HD : (head + 1) * HD] = rows_ref[head]
    for step, out_ref in enumerate(outs):
        base = lax.rem(part_ref[0] + step, len(outs)) * width
        for start in range(0, width, LANES):
            rows = pl.ds(pl.multiple_of(base + start, LANES), LANES)
            out_ref[:, start : start + LANES] = nt_dot(
                joined_ref[...], weight_ref[rows, :]
            ).astype(jnp.bfloat16)


def project(part, weight, rows, parts):
    heads, count, _ = rows.shape
    model, inner = weight.shape
    return pl.pallas_call(
        project_kernel,
        in_specs=[SMEM_SPEC, VMEM_SPEC, VMEM_SPEC],
        out_specs=[VMEM_SPEC] * parts,
        out_shape=[jax.ShapeDtypeStruct((count, model // parts), jnp.bfloat16)] * parts,
        scratch_shapes=[pltpu.VMEM((count, inner), jnp.bfloat16)],
        compiler_params=pltpu.CompilerParams(vmem_limit_bytes=20 * 1024 * 1024),
        cost_estimate=pl.CostEstimate(
            flops=2 * count * model * inner, bytes_accessed=2 * model * inner, transcendentals=0
        ),
        name="project",
    )(part, rows, weight)


def along_z(pieces):
    return lax.all_to_all(pieces, "ctx", 0, 0, axis_index_groups=Z_GROUPS)


def swap_half(piece):
    return lax.ppermute(piece, "ctx", HALF_SWAP)


def sum_tp(parts):
    count = len(parts)
    total = parts[0].astype(jnp.float32)
    for step in range(1, count):
        pairs = [(index, (index + step) % count) for index in range(count)]
        total = total + lax.ppermute(parts[step], "tp", pairs).astype(jnp.float32)
    return total.astype(jnp.bfloat16)


def spread_gains(gains, z):
    moved = [
        lax.ppermute(gains, "dp", [(i, (i + step) % 4) for i in range(4)]) for step in (1, 2, 3)
    ]
    total = (gains + moved[1]) + (moved[0] + moved[2])
    mine = jnp.arange(HEADS_LOCAL, dtype=jnp.int32)[:, None, None] == z
    total = jnp.where(mine, total[None], 0.0)
    for distance in (1, 2, 4, 8):
        total = total + lax.ppermute(total, "ctx", [(i, i ^ distance) for i in range(16)])
    return total


def local(q_raw, k_raw, values, d_out, q_gain, k_gain, q_weight, doc_lengths):
    ctx = lax.axis_index("ctx")
    z = ctx // 2
    half = lax.rem(ctx, 2)
    lengths = doc_lengths[0]
    starts = jnp.cumsum(lengths) - lengths
    q_gain_row = lax.dynamic_slice_in_dim(q_gain, z, 1, 0)
    k_gain_row = lax.dynamic_slice_in_dim(k_gain, z, 1, 0)

    pos = (2 * jnp.arange(8, dtype=jnp.int32)[:, None] + half) * ROWS + jnp.arange(
        ROWS, dtype=jnp.int32
    )
    low = jnp.max(
        jnp.where(starts[None, None, :] <= pos[:, :, None], starts[None, None, :], 0), axis=2
    )
    wide = 2 * ROWS * PAIRS
    first = low[:, 0] // wide
    last = pos[:, -1] // wide + 1
    inner = jnp.clip((low[:, -1] + wide - 1) // wide, first, last)
    diagonal = jnp.clip(pos[:, 0] // wide, inner, last)
    bounds = jnp.stack([first, inner, diagonal, last], axis=1).astype(jnp.int32)

    own = along_z(pack(k_raw[0], values[0]))
    sent, own = lax.optimization_barrier((pack(q_raw[0], d_out[0]), own))
    queries_grads = along_z(sent)
    other = swap_half(own)
    (norm_own, turned_own), (norm_other, turned_other) = (
        key_prep(k_gain_row, own),
        key_prep(k_gain_row, other),
    )
    dq, query_gain_sum, sums, other_sums = attention(
        bounds,
        half.reshape(1),
        pos,
        low,
        q_gain_row,
        queries_grads,
        ((norm_own, turned_own), (norm_other, turned_other)),
        (own, other),
    )

    returned = along_z(dq)
    moved = swap_half(other_sums)
    key_gain_sum = key_gain(sums, other_sums, (own, other))
    gains = spread_gains(jnp.concatenate([query_gain_sum, key_gain_sum], axis=0), z)
    key_gain_sum, returned = lax.optimization_barrier((key_gain_sum, returned))
    parts = project(lax.axis_index("tp").reshape(1), q_weight, returned, 4)
    moved, *parts = lax.optimization_barrier((moved, *parts))
    input_grad = sum_tp(parts)
    pieces_back = along_z(finish(sums, moved, own, k_gain_row))
    value_grad, key_grad = unpack(pieces_back)
    return (input_grad[None], key_grad[None], value_grad[None], gains[:, 0], gains[:, 1])


def solution(mesh):
    return jax.shard_map(
        local,
        mesh=mesh,
        in_specs=(
            P("dp", "ctx", "tp"),
            P("dp", "ctx", "tp"),
            P("dp", "ctx", "tp"),
            P("dp", "ctx", "tp"),
            P("tp", None),
            P("tp", None),
            P(None, "tp"),
            P("dp", None),
        ),
        out_specs=(
            P("dp", "ctx", "tp"),
            P("dp", "ctx", "tp"),
            P("dp", "ctx", "tp"),
            P("tp", None),
            P("tp", None),
        ),
        check_vma=False,
    )
```

time: 262 us -> 193 us (0.74)
  local copies, waits for them, and re-layouts: 35.1 us -> 7.22 us
  starting transfers between devices: 78.3 us -> 56.6 us
  Pallas kernels: 71.8 us -> 59.6 us
  other arithmetic: 6.73 us -> 2.51 us
    all_to_all x8 -> x4, starting transfers between devices: 50.5 us -> 27.9 us  [along_z(): return lax.all_to_all(pieces, 'ctx', 0, 0, axis_index_groups=Z_GROUPS)]
    unnamed x54 -> x18, local copies, waits for them, and re-layouts: 23.3 us -> 5.33 us
    all_to_all x8 -> x4, waiting for transfers between devices: 47.2 us -> 32.8 us  [along_z(): return lax.all_to_all(pieces, 'ctx', 0, 0, axis_index_groups=Z_GROUPS)]
    pallas_call x7 -> x9, Pallas kernels: 71.8 us -> 59.6 us  [the longest x1 33.1 us: attention(): pl.pallas_call(attention_kernel, in_specs=[SMEM_SPEC, SMEM_SPEC, VMEM_SPE...]
    ppermute x4 -> x2, waiting for transfers between devices: 9.5 us -> 20.7 us  [swap_half(): return lax.ppermute(piece, 'ctx', HALF_SWAP)]
    ppermute x4, waiting for transfers between devices: 2.42 us -> 8.22 us  [spread_gains(): lax.ppermute(total, 'ctx', [(i, i ^ distance) for i in range(16)])]
    convert_element_type x5 -> x0, other arithmetic: 4.33 us -> none  [the longest x2 2.24 us: reduce_tp(): return total.astype(jnp.bfloat16)]
    another operation x4 -> x0, local copies, waits for them, and re-layouts: 4.04 us -> none  [the longest x2 2.04 us: local(): sent = jnp.stack([by_head(q_raw[0, rows]), by_head(d_out[0, rows])], axis=1)]
  transfers between devices with their start and end apart: 24 -> 16, of which waited for: 10 -> 9; matrix products, arithmetic and copies ran while one was open for 8% -> 2% of each run, Pallas kernels for 21% -> 9%
where the time goes in v2:
time: 193 us
  waiting for transfers between devices  65.8 us (34%)
  Pallas kernels  59.6 us (31%)
  starting transfers between devices  56.6 us (29%)
  local copies, waits for them, and re-layouts  7.22 us (4%)
  other arithmetic  2.51 us (1%)
    pallas_call x1, Pallas kernels, attention(): pl.pallas_call(attention_kernel, in_specs=[SMEM_SPEC, SMEM_SPEC, VMEM_SPE...  33.1 us
    all_to_all x4, waiting for transfers between devices, along_z(): return lax.all_to_all(pieces, 'ctx', 0, 0, axis_index_groups=Z_GROUPS)  32.8 us
    all_to_all x4, starting transfers between devices, along_z(): return lax.all_to_all(pieces, 'ctx', 0, 0, axis_index_groups=Z_GROUPS)  27.9 us
    ppermute x2, waiting for transfers between devices, swap_half(): return lax.ppermute(piece, 'ctx', HALF_SWAP)  20.7 us
    ppermute x4, starting transfers between devices, spread_gains(): lax.ppermute(total, 'ctx', [(i, i ^ distance) for i in range(16)])  13.2 us
    pallas_call x2, Pallas kernels, key_prep(): pl.pallas_call(key_prep_kernel, in_specs=[VMEM_SPEC, ANY_SPEC], out_specs...  9.09 us
    ppermute x4, waiting for transfers between devices, spread_gains(): lax.ppermute(total, 'ctx', [(i, i ^ distance) for i in range(16)])  8.22 us
    ppermute x2, starting transfers between devices, swap_half(): return lax.ppermute(piece, 'ctx', HALF_SWAP)  6.36 us
  transfers between devices with their start and end apart: 16, of which 9 were waited for; matrix products, arithmetic and copies ran while one was open for 2% of the time, Pallas kernels for 9%

profile of v2, /device:TPU:32, one launch (start us, length us, event | category | flops | bytes accessed | tf_op | source)
XLA Modules:
  0.0 192.7 jit_solution(15479811702507166754)
XLA Ops:
  0.6 2.1 %pack.3 = bf16[8,2,256,128]{3,2,1,0:T(8,128)(2,1)} custom-call(bf16[256,1024]{1,0:T(8,128)(2,1)} %bitcast.19, bf16[256,1024]{1,0:T(8,128)(2,1)} %bitcast.20), custom_call_target="tpu_custom_call" | custom-call | bytes 4194304 | tf_op jit(solution)/shard_map/pack/pallas_call | solution.py:77
  2.8 8.6 %all-to-all-start = ((bf16[8,2,256,128]{3,2,1,0:T(8,128)(2,1)}), bf16[8,2,256,128]{3,2,1,0:T(8,128)(2,1)S(1)}, u32[]{:S(2)}, u32[]{:S(2)}) async-start(bf16[8,2,256,128]{3,2,1,0:T(8,128)(2,1)} %pack.3), calls=%async_computation | async-start | bytes 2097152 | tf_op jit(solution)/shard_map/all_to_all | solution.py:444
  11.4 2.2 %pack.2 = bf16[8,2,256,128]{3,2,1,0:T(8,128)(2,1)} custom-call(bf16[256,1024]{1,0:T(8,128)(2,1)} %bitcast.21, bf16[256,1024]{1,0:T(8,128)(2,1)} %bitcast.22), custom_call_target="tpu_custom_call" | custom-call | bytes 4194304 | tf_op jit(solution)/shard_map/pack/pallas_call | solution.py:77
  13.5 25.1 %all-to-all-done.raw_ref.refs_5_.raw_own = bf16[8,2,256,128]{3,2,1,0:T(8,128)(2,1)S(1)} async-done(((bf16[8,2,256,128]{3,2,1,0:T(8,128)(2,1)}), bf16[8,2,256,128]{3,2,1,0:T(8,128)(2,1)S(1)}, u32[]{:S(2)}, u32[]{:S(2)}) %all-to-all-start) | async-done | bytes 1048608 | tf_op jit(solution)/shard_map/all_to_all | solution.py:444
  38.7 4.9 %all-to-all-start.1 = ((bf16[8,2,256,128]{3,2,1,0:T(8,128)(2,1)}), bf16[8,2,256,128]{3,2,1,0:T(8,128)(2,1)S(1)}, u32[]{:S(2)}, u32[]{:S(2)}) async-start(bf16[8,2,256,128]{3,2,1,0:T(8,128)(2,1)} %pack.2), calls=%async_computation.1 | async-start | bytes 2097152 | tf_op jit(solution)/shard_map/all_to_all | solution.py:444
  43.6 3.0 %collective-permute-start = (bf16[8,2,256,128]{3,2,1,0:T(8,128)(2,1)S(1)}, bf16[8,2,256,128]{3,2,1,0:T(8,128)(2,1)S(1)}, u32[]{:S(2)}, u32[]{:S(2)}) collective-permute-start(bf16[8,2,256,128]{3,2,1,0:T(8,128)(2,1)S(1)} %all-to-all-done.raw_ref.refs_5_.raw_own), channel_id=1, source_target_pairs={{0,16},{16,0},{32,48},{48,32},{64,80},{80,64},{96,112},{112,96},{1... | collective-permute-start | bytes 3145736 | tf_op jit(solution)/shard_map/ppermute | solution.py:448
  49.0 4.6 %key_prep.2 = (bf16[8,256,128]{2,1,0:T(8,128)(2,1)}, bf16[8,128,256]{2,1,0:T(8,128)(2,1)}) custom-call(f32[1,128]{1,0:T(1,128)} %get-tuple-element.55.gain_ref, bf16[8,2,256,128]{3,2,1,0:T(8,128)(2,1)} %copy-done.1), custom_call_target="tpu_custom_call" | custom-call | bytes 4194304 | tf_op jit(solution)/shard_map/key_prep/pallas_call | solution.py:162
  53.6 16.3 %collective-permute-done.raw_ref.refs_6_.raw_other = bf16[8,2,256,128]{3,2,1,0:T(8,128)(2,1)S(1)} collective-permute-done((bf16[8,2,256,128]{3,2,1,0:T(8,128)(2,1)S(1)}, bf16[8,2,256,128]{3,2,1,0:T(8,128)(2,1)S(1)}, u32[]{:S(2)}, u32[]{:S(2)}) %collective-permute-start) | collective-permute-done | bytes 1048608 | tf_op jit(solution)/shard_map/ppermute | solution.py:448
  70.8 4.5 %key_prep.3 = (bf16[8,256,128]{2,1,0:T(8,128)(2,1)}, bf16[8,128,256]{2,1,0:T(8,128)(2,1)}) custom-call(f32[1,128]{1,0:T(1,128)} %get-tuple-element.55.gain_ref, bf16[8,2,256,128]{3,2,1,0:T(8,128)(2,1)} %copy-done.2), custom_call_target="tpu_custom_call" | custom-call | bytes 4194304 | tf_op jit(solution)/shard_map/key_prep/pallas_call | solution.py:162
  76.4 33.1 %attention.1 = (bf16[8,256,128]{2,1,0:T(8,128)(2,1)}, f32[1,128]{1,0:T(1,128)}, f32[2,8,256,128]{3,2,1,0:T(8,128)}, bf16[8,2,256,128]{3,2,1,0:T(8,128)(2,1)}) custom-call(s32[8,4]{1,0:T(8,128)} %pad_add_fusion.bounds_ref, s32[1]{0:T(128)} %bitcast.3.half_ref, s32[8,256]{1,0:T(8,128)} %copy-done.4, s32[8,256]{1,0:T(8,128)} %copy-done.5, ...), custom_call_target="tpu_custom_call" | custom-call | flops 12884901888 | bytes 8388608 | tf_op jit(solution)/shard_map/attention/pallas_call | solution.py:329
  109.5 7.2 %all-to-all-start.2 = ((bf16[8,256,128]{2,1,0:T(8,128)(2,1)}), bf16[8,256,128]{2,1,0:T(8,128)(2,1)S(1)}, u32[]{:S(2)}, u32[]{:S(2)}) async-start(bf16[8,256,128]{2,1,0:T(8,128)(2,1)} %get-tuple-element.35), calls=%async_computation.2 | async-start | bytes 1048576 | tf_op jit(solution)/shard_map/all_to_all | solution.py:444
  116.8 3.3 %collective-permute-start.1 = (bf16[8,2,256,128]{3,2,1,0:T(8,128)(2,1)}, bf16[8,2,256,128]{3,2,1,0:T(8,128)(2,1)}, u32[]{:S(2)}, u32[]{:S(2)}) collective-permute-start(bf16[8,2,256,128]{3,2,1,0:T(8,128)(2,1)} %get-tuple-element.33.other_ref), channel_id=1, source_target_pairs={{0,16},{16,0},{32,48},{48,32},{64,80},{80,64},{96,112},{112,96},{1... | collective-permute-start | bytes 3145736 | tf_op jit(solution)/shard_map/ppermute | solution.py:448
  120.1 4.0 %key_gain.1 = f32[1,128]{1,0:T(1,128)} custom-call(f32[2,8,256,128]{3,2,1,0:T(8,128)} %get-tuple-element.34.own_ref, bf16[8,2,256,128]{3,2,1,0:T(8,128)(2,1)} %get-tuple-element.33.other_ref, bf16[8,2,256,128]{3,2,1,0:T(8,128)(2,1)} %copy-done.1, bf16[8,2,256,128]{3,2,1,0:T(8,128)(2,1)} %copy-done.2), custom_call_target="tpu_custom_call" | custom-call | bytes 2621440 | tf_op jit(solution)/shard_map/key_gain/pallas_call | solution.py:369
  124.1 7.7 %all-to-all-done.2.rows_ref = bf16[8,256,128]{2,1,0:T(8,128)(2,1)S(1)} async-done(((bf16[8,256,128]{2,1,0:T(8,128)(2,1)}), bf16[8,256,128]{2,1,0:T(8,128)(2,1)S(1)}, u32[]{:S(2)}, u32[]{:S(2)}) %all-to-all-start.2) | async-done | bytes 524320 | tf_op jit(solution)/shard_map/all_to_all | solution.py:444
  131.8 3.4 %copy-done = bf16[4096,1024]{1,0:T(8,128)(2,1)S(1)} copy-done((bf16[4096,1024]{1,0:T(8,128)(2,1)S(1)}, bf16[4096,1024]{1,0:T(8,128)(2,1)}, u32[]{:S(2)}) %copy-start) | copy-done | bytes 8388632
  135.2 2.4 %project.1 = (bf16[256,1024]{1,0:T(8,128)(2,1)S(1)}, bf16[256,1024]{1,0:T(8,128)(2,1)S(1)}, bf16[256,1024]{1,0:T(8,128)(2,1)S(1)}, bf16[256,1024]{1,0:T(8,128)(2,1)S(1)}) custom-call(s32[1]{0:T(128)} %bitcast.8.part_ref, bf16[8,256,128]{2,1,0:T(8,128)(2,1)S(1)} %all-to-all-done.2.rows_ref, bf16[4096,1024]{1,0:T(8,128)(2,1)S(1)} %copy-done), custom_call_target="tpu_custom_call" | custom-call | flops 2147483648 | bytes 8388608 | tf_op jit(solution)/shard_map/project/pallas_call | solution.py:429
  137.6 4.5 %collective-permute-done.1.other_ref = bf16[8,2,256,128]{3,2,1,0:T(8,128)(2,1)} collective-permute-done((bf16[8,2,256,128]{3,2,1,0:T(8,128)(2,1)}, bf16[8,2,256,128]{3,2,1,0:T(8,128)(2,1)}, u32[]{:S(2)}, u32[]{:S(2)}) %collective-permute-start.1) | collective-permute-done | bytes 1048608 | tf_op jit(solution)/shard_map/ppermute | solution.py:448
  142.0 4.6 %finish.1 = bf16[8,512,128]{2,1,0:T(8,128)(2,1)} custom-call(f32[2,8,256,128]{3,2,1,0:T(8,128)} %get-tuple-element.34.own_ref, bf16[8,2,256,128]{3,2,1,0:T(8,128)(2,1)} %collective-permute-done.1.other_ref, bf16[8,2,256,128]{3,2,1,0:T(8,128)(2,1)} %copy-done.1, f32[1,128]{1,0:T(1,128)} %get-tuple-element.55.gain_ref), custom_call_target="tpu_custom_call" | custom-call | bytes 8388608 | tf_op jit(solution)/shard_map/finish/pallas_call | solution.py:400
  146.6 7.2 %all-to-all-start.3 = ((bf16[8,512,128]{2,1,0:T(8,128)(2,1)}), bf16[8,512,128]{2,1,0:T(8,128)(2,1)}, u32[]{:S(2)}, u32[]{:S(2)}) async-start(bf16[8,512,128]{2,1,0:T(8,128)(2,1)} %finish.1), calls=%async_computation.3 | async-start | bytes 2097152 | tf_op jit(solution)/shard_map/all_to_all | solution.py:444
  153.9 1.7 collective-permute-start.7
  155.7 1.4 collective-permute-start.5
  157.1 2.2 %collective-permute-done.5 = f32[2,128]{1,0:T(2,128)S(1)} collective-permute-done((f32[2,128]{1,0:T(2,128)S(1)}, f32[2,128]{1,0:T(2,128)S(1)}, u32[]{:S(2)}, u32[]{:S(2)}) %collective-permute-start.5) | collective-permute-done | bytes 1056 | tf_op jit(solution)/shard_map/ppermute | solution.py:462
  159.3 3.3 %collective-permute-start.8 = (f32[8,2,128]{2,0,1:T(8,128)S(1)}, f32[8,2,128]{2,0,1:T(8,128)S(1)}, u32[]{:S(2)}, u32[]{:S(2)}) collective-permute-start(f32[8,2,128]{2,0,1:T(8,128)S(1)} %broadcast_select_fusion), channel_id=1, source_target_pairs={{0,16},{16,0},{32,48},{48,32},{64,80},{80,64},{96,112},{112,96},{1... | collective-permute-start | bytes 24584 | tf_op jit(solution)/shard_map/ppermute | solution.py:468
  162.6 1.6 collective-permute-start.2
  164.2 2.9 %collective-permute-start.3 = (bf16[256,1024]{1,0:T(8,128)(2,1)S(1)}, bf16[256,1024]{1,0:T(8,128)(2,1)S(1)}, u32[]{:S(2)}, u32[]{:S(2)}) collective-permute-start(bf16[256,1024]{1,0:T(8,128)(2,1)S(1)} %get-tuple-element.43), channel_id=1, source_target_pairs={{0,8},{4,12},{8,0},{12,4},{1,9},{5,13},{9,1},{13,5},{2,10},{6,14},... | collective-permute-start | bytes 1572872 | tf_op jit(solution)/shard_map/ppermute | solution.py:456
  168.5 4.8 %collective-permute-done.9 = f32[8,2,128]{2,0,1:T(8,128)S(1)} collective-permute-done((f32[8,2,128]{2,0,1:T(8,128)S(1)}, f32[8,2,128]{2,0,1:T(8,128)S(1)}, u32[]{:S(2)}, u32[]{:S(2)}) %collective-permute-start.9) | collective-permute-done | bytes 8224 | tf_op jit(solution)/shard_map/ppermute | solution.py:468
  173.4 3.7 %collective-permute-start.10 = (f32[8,2,128]{2,0,1:T(8,128)S(1)}, f32[8,2,128]{2,0,1:T(8,128)S(1)}, u32[]{:S(2)}, u32[]{:S(2)}) collective-permute-start(f32[8,2,128]{2,0,1:T(8,128)S(1)} %fusion.16), channel_id=1, source_target_pairs={{0,64},{16,80},{32,96},{48,112},{64,0},{80,16},{96,32},{112,48},{1... | collective-permute-start | bytes 24584 | tf_op jit(solution)/shard_map/ppermute | solution.py:468
  177.1 1.8 collective-permute-done.10
  178.9 6.2 %collective-permute-start.11 = (f32[8,2,128]{2,0,1:T(8,128)S(1)}, f32[8,2,128]{2,0,1:T(8,128)S(1)}, u32[]{:S(2)}, u32[]{:S(2)}) collective-permute-start(f32[8,2,128]{2,0,1:T(8,128)S(1)} %add.101), channel_id=1, source_target_pairs={{0,128},{16,144},{32,160},{48,176},{64,192},{80,208},{96,224},{112... | collective-permute-start | bytes 24584 | tf_op jit(solution)/shard_map/ppermute | solution.py:468
  185.1 1.6 collective-permute-done.11
  187.4 1.9 collective-permute-done.3
  190.4 2.1 %unpack.1 = (bf16[256,1024]{1,0:T(8,128)(2,1)}, bf16[256,1024]{1,0:T(8,128)(2,1)}) custom-call(bf16[8,512,128]{2,1,0:T(8,128)(2,1)} %all-to-all-done.3.pieces_ref), custom_call_target="tpu_custom_call" | custom-call | bytes 4194304 | tf_op jit(solution)/shard_map/unpack/pallas_call | solution.py:118
  (45 shorter events, 7.8 us)
Async XLA Ops:
  0.6 46.0 %copy-start.8 = (s32[1,8]{1,0:T(1,128)S(1)}, s32[1,8]{1,0:T(1,128)}, u32[]{:S(2)}) copy-start(s32[1,8]{1,0:T(1,128)} %param.15) | copy-start | bytes 100
  2.8 35.9 %all-to-all-start = ((bf16[8,2,256,128]{3,2,1,0:T(8,128)(2,1)}), bf16[8,2,256,128]{3,2,1,0:T(8,128)(2,1)S(1)}, u32[]{:S(2)}, u32[]{:S(2)}) async-start(bf16[8,2,256,128]{3,2,1,0:T(8,128)(2,1)} %pack.3), calls=%async_computation | async-start | bytes 2097152 | tf_op jit(solution)/shard_map/all_to_all | solution.py:444
  38.7 10.4 %copy-start.1 = (bf16[8,2,256,128]{3,2,1,0:T(8,128)(2,1)}, bf16[8,2,256,128]{3,2,1,0:T(8,128)(2,1)S(1)}, u32[]{:S(2)}) copy-start(bf16[8,2,256,128]{3,2,1,0:T(8,128)(2,1)S(1)} %all-to-all-done.raw_ref.refs_5_.raw_own) | copy-start | bytes 3145732
  38.7 36.7 %all-to-all-start.1 = ((bf16[8,2,256,128]{3,2,1,0:T(8,128)(2,1)}), bf16[8,2,256,128]{3,2,1,0:T(8,128)(2,1)S(1)}, u32[]{:S(2)}, u32[]{:S(2)}) async-start(bf16[8,2,256,128]{3,2,1,0:T(8,128)(2,1)} %pack.2), calls=%async_computation.1 | async-start | bytes 2097152 | tf_op jit(solution)/shard_map/all_to_all | solution.py:444
  43.6 26.3 %collective-permute-start = (bf16[8,2,256,128]{3,2,1,0:T(8,128)(2,1)S(1)}, bf16[8,2,256,128]{3,2,1,0:T(8,128)(2,1)S(1)}, u32[]{:S(2)}, u32[]{:S(2)}) collective-permute-start(bf16[8,2,256,128]{3,2,1,0:T(8,128)(2,1)S(1)} %all-to-all-done.raw_ref.refs_5_.raw_own), channel_id=1, source_target_pairs={{0,16},{16,0},{32,48},{48,32},{64,80},{80,64},{96,112},{112,96},{1... | collective-permute-start | bytes 3145736 | tf_op jit(solution)/shard_map/ppermute | solution.py:448
  48.2 27.3 %copy-start.4 = (s32[8,256]{1,0:T(8,128)}, s32[8,256]{1,0:T(8,128)S(1)}, u32[]{:S(2)}) copy-start(s32[8,256]{1,0:T(8,128)S(1)} %iota_add_fusion.pos_ref) | copy-start | bytes 24580
  48.3 27.2 %copy-start.5 = (s32[8,256]{1,0:T(8,128)}, s32[8,256]{1,0:T(8,128)S(1)}, u32[]{:S(2)}) copy-start(s32[8,256]{1,0:T(8,128)S(1)} %select_reduce_fusion.low_ref) | copy-start | bytes 24580
  69.9 1.0 copy-start.2
  75.4 1.0 copy-start.3
  109.5 22.3 %all-to-all-start.2 = ((bf16[8,256,128]{2,1,0:T(8,128)(2,1)}), bf16[8,256,128]{2,1,0:T(8,128)(2,1)S(1)}, u32[]{:S(2)}, u32[]{:S(2)}) async-start(bf16[8,256,128]{2,1,0:T(8,128)(2,1)} %get-tuple-element.35), calls=%async_computation.2 | async-start | bytes 1048576 | tf_op jit(solution)/shard_map/all_to_all | solution.py:444
  116.8 25.3 %collective-permute-start.1 = (bf16[8,2,256,128]{3,2,1,0:T(8,128)(2,1)}, bf16[8,2,256,128]{3,2,1,0:T(8,128)(2,1)}, u32[]{:S(2)}, u32[]{:S(2)}) collective-permute-start(bf16[8,2,256,128]{3,2,1,0:T(8,128)(2,1)} %get-tuple-element.33.other_ref), channel_id=1, source_target_pairs={{0,16},{16,0},{32,48},{48,32},{64,80},{80,64},{96,112},{112,96},{1... | collective-permute-start | bytes 3145736 | tf_op jit(solution)/shard_map/ppermute | solution.py:448
  124.1 29.7 %copy-start.6 = (f32[1,128]{1,0:T(1,128)S(1)}, f32[1,128]{1,0:T(1,128)}, u32[]{:S(2)}) copy-start(f32[1,128]{1,0:T(1,128)} %key_gain.1) | copy-start | bytes 1540
  124.1 29.7 %copy-start.7 = (f32[1,128]{1,0:T(1,128)S(1)}, f32[1,128]{1,0:T(1,128)}, u32[]{:S(2)}) copy-start(f32[1,128]{1,0:T(1,128)} %get-tuple-element.48) | copy-start | bytes 1540
  131.8 3.4 %copy-start = (bf16[4096,1024]{1,0:T(8,128)(2,1)S(1)}, bf16[4096,1024]{1,0:T(8,128)(2,1)}, u32[]{:S(2)}) copy-start(bf16[4096,1024]{1,0:T(8,128)(2,1)} %weight_ref.1) | copy-start | bytes 25165828
  146.6 43.8 %all-to-all-start.3 = ((bf16[8,512,128]{2,1,0:T(8,128)(2,1)}), bf16[8,512,128]{2,1,0:T(8,128)(2,1)}, u32[]{:S(2)}, u32[]{:S(2)}) async-start(bf16[8,512,128]{2,1,0:T(8,128)(2,1)} %finish.1), calls=%async_computation.3 | async-start | bytes 2097152 | tf_op jit(solution)/shard_map/all_to_all | solution.py:444
  153.8 3.2 %collective-permute-start.6 = (f32[2,128]{1,0:T(2,128)S(1)}, f32[2,128]{1,0:T(2,128)S(1)}, u32[]{:S(2)}, u32[]{:S(2)}) collective-permute-start(f32[2,128]{1,0:T(2,128)S(1)} %pad_maximum_fusion), channel_id=1, source_target_pairs={{0,1},{1,2},{2,3},{3,0},{4,5},{5,6},{6,7},{7,4},{8,9},{9,10},{10,1... | collective-permute-start | bytes 3080 | tf_op jit(solution)/shard_map/ppermute | solution.py:462
  153.9 3.1 %collective-permute-start.7 = (f32[2,128]{1,0:T(2,128)S(1)}, f32[2,128]{1,0:T(2,128)S(1)}, u32[]{:S(2)}, u32[]{:S(2)}) collective-permute-start(f32[2,128]{1,0:T(2,128)S(1)} %pad_maximum_fusion), channel_id=1, source_target_pairs={{0,3},{1,0},{2,1},{3,2},{4,7},{5,4},{6,5},{7,6},{8,11},{9,8},{10,9... | collective-permute-start | bytes 3080 | tf_op jit(solution)/shard_map/ppermute | solution.py:462
  155.7 3.6 %collective-permute-start.5 = (f32[2,128]{1,0:T(2,128)S(1)}, f32[2,128]{1,0:T(2,128)S(1)}, u32[]{:S(2)}, u32[]{:S(2)}) collective-permute-start(f32[2,128]{1,0:T(2,128)S(1)} %pad_maximum_fusion), channel_id=1, source_target_pairs={{0,2},{1,3},{2,0},{3,1},{4,6},{5,7},{6,4},{7,5},{8,10},{9,11},{10,... | collective-permute-start | bytes 3080 | tf_op jit(solution)/shard_map/ppermute | solution.py:462
  159.3 9.1 %collective-permute-start.8 = (f32[8,2,128]{2,0,1:T(8,128)S(1)}, f32[8,2,128]{2,0,1:T(8,128)S(1)}, u32[]{:S(2)}, u32[]{:S(2)}) collective-permute-start(f32[8,2,128]{2,0,1:T(8,128)S(1)} %broadcast_select_fusion), channel_id=1, source_target_pairs={{0,16},{16,0},{32,48},{48,32},{64,80},{80,64},{96,112},{112,96},{1... | collective-permute-start | bytes 24584 | tf_op jit(solution)/shard_map/ppermute | solution.py:468
  162.6 24.8 %collective-permute-start.2 = (bf16[256,1024]{1,0:T(8,128)(2,1)S(1)}, bf16[256,1024]{1,0:T(8,128)(2,1)S(1)}, u32[]{:S(2)}, u32[]{:S(2)}) collective-permute-start(bf16[256,1024]{1,0:T(8,128)(2,1)S(1)} %get-tuple-element.42), channel_id=1, source_target_pairs={{0,4},{4,8},{8,12},{12,0},{1,5},{5,9},{9,13},{13,1},{2,6},{6,10},{... | collective-permute-start | bytes 1572872 | tf_op jit(solution)/shard_map/ppermute | solution.py:456
  164.2 25.1 %collective-permute-start.3 = (bf16[256,1024]{1,0:T(8,128)(2,1)S(1)}, bf16[256,1024]{1,0:T(8,128)(2,1)S(1)}, u32[]{:S(2)}, u32[]{:S(2)}) collective-permute-start(bf16[256,1024]{1,0:T(8,128)(2,1)S(1)} %get-tuple-element.43), channel_id=1, source_target_pairs={{0,8},{4,12},{8,0},{12,4},{1,9},{5,13},{9,1},{13,5},{2,10},{6,14},... | collective-permute-start | bytes 1572872 | tf_op jit(solution)/shard_map/ppermute | solution.py:456
  167.1 22.2 %collective-permute-start.4 = (bf16[256,1024]{1,0:T(8,128)(2,1)S(1)}, bf16[256,1024]{1,0:T(8,128)(2,1)S(1)}, u32[]{:S(2)}, u32[]{:S(2)}) collective-permute-start(bf16[256,1024]{1,0:T(8,128)(2,1)S(1)} %get-tuple-element.44), channel_id=1, source_target_pairs={{0,12},{4,0},{8,4},{12,8},{1,13},{5,1},{9,5},{13,9},{2,14},{6,2},{... | collective-permute-start | bytes 1572872 | tf_op jit(solution)/shard_map/ppermute | solution.py:456
  168.5 4.8 %collective-permute-start.9 = (f32[8,2,128]{2,0,1:T(8,128)S(1)}, f32[8,2,128]{2,0,1:T(8,128)S(1)}, u32[]{:S(2)}, u32[]{:S(2)}) collective-permute-start(f32[8,2,128]{2,0,1:T(8,128)S(1)} %fusion.14), channel_id=1, source_target_pairs={{0,32},{16,48},{32,0},{48,16},{64,96},{80,112},{96,64},{112,80},{1... | collective-permute-start | bytes 24584 | tf_op jit(solution)/shard_map/ppermute | solution.py:468
  173.4 5.5 %collective-permute-start.10 = (f32[8,2,128]{2,0,1:T(8,128)S(1)}, f32[8,2,128]{2,0,1:T(8,128)S(1)}, u32[]{:S(2)}, u32[]{:S(2)}) collective-permute-start(f32[8,2,128]{2,0,1:T(8,128)S(1)} %fusion.16), channel_id=1, source_target_pairs={{0,64},{16,80},{32,96},{48,112},{64,0},{80,16},{96,32},{112,48},{1... | collective-permute-start | bytes 24584 | tf_op jit(solution)/shard_map/ppermute | solution.py:468
  178.9 7.8 %collective-permute-start.11 = (f32[8,2,128]{2,0,1:T(8,128)S(1)}, f32[8,2,128]{2,0,1:T(8,128)S(1)}, u32[]{:S(2)}, u32[]{:S(2)}) collective-permute-start(f32[8,2,128]{2,0,1:T(8,128)S(1)} %add.101), channel_id=1, source_target_pairs={{0,128},{16,144},{32,160},{48,176},{64,192},{80,208},{96,224},{112... | collective-permute-start | bytes 24584 | tf_op jit(solution)/shard_map/ppermute | solution.py:468

commit v3 on v2

--- a/solution.py
+++ b/solution.py
@@ -9,11 +9,14 @@
 
 NORM_EPSILON = 1e-05
 MASKED_SCORE = -1e30
+LEAST_PEAK = -1e20
 HEADS_LOCAL = 8
 HD = 128
 ROWS = 256
 LANES = 256
 PAIRS = 2
+WIDE = 2 * PAIRS * ROWS
+EXTRA = 16
 FACTOR = HD ** (-0.5)
 EXP2_FACTOR = FACTOR * 1.4426950408889634
 VMEM_LIMIT = 60 * 1024 * 1024
@@ -180,11 +183,11 @@
     return tile.reshape(tile.shape[0] // 8, 8, tile.shape[1])
 
 
-def attention_kernel(bounds_ref, half_ref, pos_ref, low_ref, gain_ref, *refs):
+def attention_kernel(bounds_ref, half_ref, pos_ref, low_ref, gain_ref, key_gain_ref, *refs):
     queries_grads_ref, refs = refs[0], refs[1:]
     norms, turned, raws = refs[0:2], refs[2:4], refs[4:6]
     refs = refs[6:]
-    dq_ref, gain_grad_ref, own_ref, other_ref = refs[:4]
+    dq_ref, own_ref, other_ref = refs[:3]
     (
         chance_ref,
         dot_ref,
@@ -198,33 +201,45 @@
         held_query,
         held_dq,
         cast_ref,
+        gain_grad_ref,
         in_sem,
+        dq_sem,
         out_sem,
-    ) = refs[4:]
+    ) = refs[3:]
     half = half_ref[0]
-    moves = [(queries_grads_ref, held_query)]
-    for side in range(2):
-        moves.append((norms[side], held_norm.at[side]))
-        moves.append((turned[side], held_turned.at[side]))
-        moves.append((raws[side].at[:, 1], held_value.at[side]))
-    loads = [
-        pltpu.make_async_copy(source, target, in_sem.at[index])
-        for index, (source, target) in enumerate(moves)
-    ]
-    for copy in loads:
-        copy.start()
+
+    def loads(step):
+        tiles = pl.ds(step * PAIRS, PAIRS)
+        moves = [(queries_grads_ref.at[tiles], held_query.at[tiles])]
+        for side in range(2):
+            lanes = pl.ds(side * ROWS, ROWS)
+            moves.append((norms[side].at[tiles], held_norm.at[tiles, side]))
+            moves.append((turned[side].at[tiles], held_turned.at[tiles, :, lanes]))
+            moves.append((raws[side].at[tiles, 1], held_value.at[tiles, side]))
+        return [
+            pltpu.make_async_copy(source, target, in_sem.at[step, index])
+            for index, (source, target) in enumerate(moves)
+        ]
+
+    for step in range(DEPTH // PAIRS):
+        for copy in loads(step):
+            copy.start()
     dk_ref[...] = jnp.zeros_like(dk_ref)
     dv_ref[...] = jnp.zeros_like(dv_ref)
     gain_grad_ref[...] = jnp.zeros_like(gain_grad_ref)
-    for copy in loads:
-        copy.wait()
 
     def block_body(block, carry):
+        @pl.when(lax.rem(block, PAIRS) == 0)
+        def _():
+            for copy in loads(block // PAIRS):
+                copy.wait()
+
         unit_rows, inverse = unit_norm(held_query[block, 0])
         query = (unit_rows * gain_ref[...]).astype(jnp.bfloat16)
         grad = held_query[block, 1]
         pos = pos_ref[pl.ds(block, 1), :]
         low = low_ref[pl.ds(block, 1), :]
+        row = lax.broadcasted_iota(jnp.int32, (ROWS, LANES), 0)
         first, inner, diagonal, last = (bounds_ref[block, i] for i in range(4))
 
         def scores_body(masked, step, sums):
@@ -234,38 +249,36 @@
             for pair in range(PAIRS):
                 tile = step * PAIRS + pair
                 for side in range(2):
-                    scores = nt_dot(held_norm[side, tile], query)
-                    mask = None
+                    scores = nt_dot(held_norm[tile, side], query)
                     if masked:
                         which = half if side == 0 else 1 - half
-                        key_pos = (2 * tile + which) * ROWS + lax.broadcasted_iota(
-                            jnp.int32, (ROWS, LANES), 0
-                        )
-                        mask = (key_pos >= low) & (key_pos <= pos)
+                        base = (2 * tile + which) * ROWS
+                        mask = row >= low - base
+                        if masked > 1:
+                            mask = mask & (row <= pos - base)
                         scores = jnp.where(mask, scores, MASKED_SCORE)
-                    parts.append((tile, side, scores, mask))
+                    parts.append((tile, side, scores))
                     peak = jnp.maximum(peak, jnp.max(fold(scores), axis=0))
             new_best = jnp.maximum(best, jnp.max(peak, axis=0, keepdims=True) * EXP2_FACTOR)
             scale = jnp.exp2(best - new_best)
             total, weighted = total * scale, weighted * scale
-            for tile, side, scores, mask in parts:
+            for index, (tile, side, scores) in enumerate(parts):
                 shifted = jnp.exp2(scores * EXP2_FACTOR - new_best)
-                if masked:
-                    shifted = jnp.where(mask, shifted, 0.0)
-                dots = nt_dot(held_value[side, tile], grad)
-                chance_ref[tile, side * ROWS : (side + 1) * ROWS] = shifted
-                dot_ref[tile, side * ROWS : (side + 1) * ROWS] = dots
+                dots = nt_dot(held_value[tile, side], grad)
+                rows = slice(index * ROWS, (index + 1) * ROWS)
+                chance_ref[step, rows] = shifted
+                dot_ref[step, rows] = dots
                 total = total + jnp.sum(fold(shifted), axis=0)
                 weighted = weighted + jnp.sum(fold(shifted * dots), axis=0)
             peak_ref[pl.ds(step, 1), :] = new_best
             return new_best, total, weighted
 
         empty = jnp.zeros((8, LANES), jnp.float32)
-        sums = (jnp.full((1, LANES), MASKED_SCORE, jnp.float32), empty, empty)
-        sums = lax.fori_loop(first, inner, functools.partial(scores_body, True), sums)
-        sums = lax.fori_loop(inner, diagonal, functools.partial(scores_body, False), sums)
+        sums = (jnp.full((1, LANES), LEAST_PEAK, jnp.float32), empty, empty)
+        sums = lax.fori_loop(first, inner, functools.partial(scores_body, 1), sums)
+        sums = lax.fori_loop(inner, diagonal, functools.partial(scores_body, 0), sums)
         best, total, weighted = lax.fori_loop(
-            diagonal, last, functools.partial(scores_body, True), sums
+            diagonal, last, functools.partial(scores_body, 2), sums
         )
         share = 1.0 / jnp.sum(total, axis=0, keepdims=True)
         delta = jnp.sum(weighted, axis=0, keepdims=True) * share
@@ -273,74 +286,90 @@
 
         def grads_body(step, carry):
             step_share = share * jnp.exp2(peak_ref[pl.ds(step, 1), :] - best)
-            score_grads, norms_t = [], []
+            score_grads, keys_t = [], []
             for pair in range(PAIRS):
-                tile = step * PAIRS + pair
-                chance = chance_ref[tile] * step_share
-                score_grad = (chance * (dot_ref[tile] - delta)).astype(jnp.bfloat16)
-                dv_ref[tile] += nn_dot(chance.astype(jnp.bfloat16), grad)
-                dk_ref[tile] += nn_dot(score_grad, query)
+                rows = slice(pair * 2 * ROWS, (pair + 1) * 2 * ROWS)
+                chance = chance_ref[step, rows] * step_share
+                score_grad = (chance * (dot_ref[step, rows] - delta)).astype(jnp.bfloat16)
+                dv_ref[step, rows] += nn_dot(chance.astype(jnp.bfloat16), grad)
+                dk_ref[step, rows] += nn_dot(score_grad, query)
                 score_grads.append(score_grad)
-                norms_t += [held_turned[0, tile], held_turned[1, tile]]
-            dqt_ref[...] += nn_dot(
-                jnp.concatenate(norms_t, axis=1), jnp.concatenate(score_grads, axis=0)
-            )
+                keys_t.append(held_turned[step * PAIRS + pair])
+            dqt_ref[...] += nn_dot(jnp.concatenate(keys_t, axis=1), jnp.concatenate(score_grads, axis=0))
             return carry
 
         lax.fori_loop(first, last, grads_body, 0)
         query_grad = dqt_ref[...].T * FACTOR
-        held_dq[block] = unit_norm_backward(
+        held_dq[block, :ROWS] = unit_norm_backward(
             query_grad, unit_rows, inverse, gain_ref[...]
         ).astype(jnp.bfloat16)
         gain_grad_ref[...] += jnp.sum(query_grad * unit_rows, axis=0, keepdims=True)
         return carry
 
     lax.fori_loop(0, DEPTH, block_body, 0)
-    cast_ref[:, 0] = dv_ref[:, ROWS:].astype(jnp.bfloat16)
-    cast_ref[:, 1] = dk_ref[:, ROWS:].astype(jnp.bfloat16)
-    moves = [
-        (held_dq, dq_ref),
-        (cast_ref, other_ref),
-        (dv_ref.at[:, :ROWS], own_ref.at[0]),
-        (dk_ref.at[:, :ROWS], own_ref.at[1]),
-    ]
-    copies = [
-        pltpu.make_async_copy(source, target, out_sem.at[index])
-        for index, (source, target) in enumerate(moves)
-    ]
-    for copy in copies:
-        copy.start()
+    key_total = jnp.zeros((ROWS, HD), jnp.float32)
+    for tile in range(DEPTH):
+        for side in range(2):
+            start = (tile % PAIRS * 2 + side) * ROWS
+            key_grad = dk_ref[tile // PAIRS, start : start + ROWS]
+            key_total += key_grad * held_norm[tile, side].astype(jnp.float32)
+    key_total = jnp.sum(key_total, axis=0, keepdims=True) * FACTOR / key_gain_ref[...]
+    row = lax.broadcasted_iota(jnp.int32, (EXTRA, HD), 0)
+    extra = jnp.zeros((EXTRA, HD), jnp.float32)
+    for which, rest in enumerate((gain_grad_ref[...], key_total)):
+        for index in range(3):
+            term = rest.astype(jnp.bfloat16).astype(jnp.float32)
+            extra = jnp.where(row == 3 * which + index, term, extra)
+            rest = rest - term
+    for tile in range(DEPTH):
+        held_dq[tile, ROWS:] = extra.astype(jnp.bfloat16)
+    copies = [pltpu.make_async_copy(held_dq, dq_ref, dq_sem.at[0])]
+    copies[0].start()
+    for tile in range(DEPTH):
+        step, base = tile // PAIRS, tile % PAIRS * 2 * ROWS
+        for side, out_ref in enumerate((own_ref, other_ref)):
+            rows = slice(base + side * ROWS, base + (side + 1) * ROWS)
+            cast_ref[side, tile, 0] = dv_ref[step, rows].astype(jnp.bfloat16)
+            cast_ref[side, tile, 1] = dk_ref[step, rows].astype(jnp.bfloat16)
+            copies.append(
+                pltpu.make_async_copy(
+                    cast_ref.at[side, tile], out_ref.at[tile], out_sem.at[side, tile]
+                )
+            )
+            copies[-1].start()
     for copy in copies:
         copy.wait()
 
 
-def attention(bounds, half, pos, low, gain, queries_grads, keys, raws):
-    tiles = DEPTH
-    pairs = DEPTH * tiles * ROWS * 2 * ROWS
-    wide = pltpu.VMEM((tiles, 2 * ROWS, LANES), jnp.float32)
-    total = pltpu.VMEM((tiles, 2 * ROWS, HD), jnp.float32)
-    rows = pltpu.VMEM((tiles, ROWS, HD), jnp.bfloat16)
-    outs = [
-        jax.ShapeDtypeStruct((DEPTH, ROWS, HD), jnp.bfloat16),
-        jax.ShapeDtypeStruct((1, HD), jnp.float32),
-        jax.ShapeDtypeStruct((2, DEPTH, ROWS, HD), jnp.float32),
-        jax.ShapeDtypeStruct((DEPTH, 2, ROWS, HD), jnp.bfloat16),
-    ]
+def attention(bounds, half, pos, low, gain, key_gain, queries_grads, keys, raws):
+    steps = DEPTH // PAIRS
+    pairs = DEPTH * DEPTH * ROWS * 2 * ROWS
+    scores = pltpu.VMEM((steps, WIDE, LANES), jnp.float32)
+    total = pltpu.VMEM((steps, WIDE, HD), jnp.float32)
+    both = pltpu.VMEM((DEPTH, 2, ROWS, HD), jnp.bfloat16)
+    sums = jax.ShapeDtypeStruct((DEPTH, 2, ROWS, HD), jnp.bfloat16)
     return pl.pallas_call(
         attention_kernel,
-        in_specs=[SMEM_SPEC, SMEM_SPEC, VMEM_SPEC, VMEM_SPEC, VMEM_SPEC] + [ANY_SPEC] * 7,
-        out_specs=[ANY_SPEC, VMEM_SPEC, ANY_SPEC, ANY_SPEC],
-        out_shape=outs,
+        in_specs=[SMEM_SPEC, SMEM_SPEC] + [VMEM_SPEC] * 4 + [ANY_SPEC] * 7,
+        out_specs=[ANY_SPEC, ANY_SPEC, ANY_SPEC],
+        out_shape=[
+            jax.ShapeDtypeStruct((DEPTH, ROWS + EXTRA, HD), jnp.bfloat16),
+            sums,
+            sums,
+        ],
         scratch_shapes=[
-            wide, wide, pltpu.VMEM((tiles, LANES), jnp.float32), total, total,
+            scores, scores, pltpu.VMEM((DEPTH, LANES), jnp.float32), total, total,
             pltpu.VMEM((HD, LANES), jnp.float32),
-            pltpu.VMEM((2, tiles, ROWS, HD), jnp.bfloat16),
-            pltpu.VMEM((2, tiles, HD, ROWS), jnp.bfloat16),
-            pltpu.VMEM((2, tiles, ROWS, HD), jnp.bfloat16),
-            pltpu.VMEM((DEPTH, 2, ROWS, HD), jnp.bfloat16),
-            rows, pltpu.VMEM((DEPTH, 2, ROWS, HD), jnp.bfloat16),
-            pltpu.SemaphoreType.DMA((7,)),
-            pltpu.SemaphoreType.DMA((4,)),
+            both,
+            pltpu.VMEM((DEPTH, HD, 2 * ROWS), jnp.bfloat16),
+            both,
+            both,
+            pltpu.VMEM((DEPTH, ROWS + EXTRA, HD), jnp.bfloat16),
+            pltpu.VMEM((2, DEPTH, 2, ROWS, HD), jnp.bfloat16),
+            pltpu.VMEM((1, HD), jnp.float32),
+            pltpu.SemaphoreType.DMA((steps, 7)),
+            pltpu.SemaphoreType.DMA((1,)),
+            pltpu.SemaphoreType.DMA((2, DEPTH)),
         ],
         compiler_params=pltpu.CompilerParams(vmem_limit_bytes=VMEM_LIMIT),
         cost_estimate=pl.CostEstimate(
@@ -348,47 +377,23 @@
         ),
         name="attention",
     )(
-        bounds, half, pos, low, gain, queries_grads,
+        bounds, half, pos, low, gain, key_gain, queries_grads,
         *[key[0] for key in keys], *[key[1] for key in keys], *raws,
     )
 
 
-def key_gain_kernel(own_ref, other_ref, raw_own, raw_other, out_ref):
-    total = jnp.zeros((ROWS, HD), jnp.float32)
-    for tile in range(DEPTH):
-        for grad, raw_ref in ((own_ref[0, tile], raw_own), (other_ref[tile, 0], raw_other)):
-            total += grad.astype(jnp.float32) * unit_norm(raw_ref[tile, 0])[0]
-    out_ref[...] = jnp.sum(total, axis=0, keepdims=True) * FACTOR
-
-
 def keys_of_pair():
     return pl.BlockSpec((DEPTH, 1, ROWS, HD), lambda i: (0, 0, 0, 0))
-
-
-def key_gain(own, other, raws):
-    return pl.pallas_call(
-        key_gain_kernel,
-        grid=(1,),
-        in_specs=[
-            pl.BlockSpec((1, DEPTH, ROWS, HD), lambda i: (1, 0, 0, 0)),
-            pl.BlockSpec((DEPTH, 1, ROWS, HD), lambda i: (0, 1, 0, 0)),
-            keys_of_pair(),
-            keys_of_pair(),
-        ],
-        out_specs=whole(1, HD),
-        out_shape=jax.ShapeDtypeStruct((1, HD), jnp.float32),
-        cost_estimate=pl.CostEstimate(flops=0, bytes_accessed=5 * 2**19, transcendentals=0),
-        name="key_gain",
-    )(own, other, *raws)
 
 
 def finish_kernel(
     own_ref, other_ref, raw_ref, gain_ref, out_ref
 ):
     for tile in range(DEPTH):
-        value_sum = own_ref[0, tile] + other_ref[tile, 0].astype(jnp.float32)
+        value_sum = own_ref[tile, 0].astype(jnp.float32) + other_ref[tile, 0].astype(jnp.float32)
         out_ref[tile, :ROWS] = value_sum.astype(jnp.bfloat16)
-        grad_norm = (own_ref[1, tile] + other_ref[tile, 1].astype(jnp.float32)) * FACTOR
+        grad_norm = own_ref[tile, 1].astype(jnp.float32) + other_ref[tile, 1].astype(jnp.float32)
+        grad_norm = grad_norm * FACTOR
         unit_rows, inverse = unit_norm(raw_ref[tile, 0])
         out_ref[tile, ROWS : 2 * ROWS] = unit_norm_backward(
             grad_norm, unit_rows, inverse, gain_ref[...]
@@ -400,20 +405,26 @@
     return pl.pallas_call(
         finish_kernel,
         grid=(1,),
-        in_specs=[whole(2, DEPTH, ROWS, HD), whole(DEPTH, 2, ROWS, HD)]
+        in_specs=[whole(DEPTH, 2, ROWS, HD), whole(DEPTH, 2, ROWS, HD)]
         + [keys_of_pair(), whole(1, HD)],
         out_specs=whole(DEPTH, rows, HD),
         out_shape=jax.ShapeDtypeStruct((DEPTH, rows, HD), jnp.bfloat16),
         cost_estimate=pl.CostEstimate(flops=0, bytes_accessed=2**23, transcendentals=0),
+        compiler_params=pltpu.CompilerParams(vmem_limit_bytes=16 * 1024 * 1024),
         name="finish",
     )(own, other, raw, gain)
 
 
 def project_kernel(part_ref, rows_ref, weight_ref, *refs):
-    outs, joined_ref = refs[:-1], refs[-1]
+    outs, (gains_ref, joined_ref) = refs[:-2], refs[-2:]
     width = outs[0].shape[1]
     for head in range(rows_ref.shape[0]):
-        joined_ref[:, head * HD : (head + 1) * HD] = rows_ref[head]
+        joined_ref[:, head * HD : (head + 1) * HD] = rows_ref[head, :ROWS]
+        terms = rows_ref[head, ROWS:].astype(jnp.float32)
+        for which in range(2):
+            first, second, third = (terms[3 * which + i : 3 * which + i + 1] for i in range(3))
+            place = which * HEADS_LOCAL + head
+            gains_ref[place : place + 1, :] = (third + second) + first
     for step, out_ref in enumerate(outs):
         base = lax.rem(part_ref[0] + step, len(outs)) * width
         for start in range(0, width, LANES):
@@ -424,17 +435,17 @@
 
 
 def project(part, weight, rows, parts):
-    heads, count, _ = rows.shape
     model, inner = weight.shape
+    out = jax.ShapeDtypeStruct((ROWS, model // parts), jnp.bfloat16)
     return pl.pallas_call(
         project_kernel,
         in_specs=[SMEM_SPEC, VMEM_SPEC, VMEM_SPEC],
-        out_specs=[VMEM_SPEC] * parts,
-        out_shape=[jax.ShapeDtypeStruct((count, model // parts), jnp.bfloat16)] * parts,
-        scratch_shapes=[pltpu.VMEM((count, inner), jnp.bfloat16)],
+        out_specs=[VMEM_SPEC] * (parts + 1),
+        out_shape=[out] * parts + [jax.ShapeDtypeStruct((2 * HEADS_LOCAL, HD), jnp.float32)],
+        scratch_shapes=[pltpu.VMEM((ROWS, inner), jnp.bfloat16)],
         compiler_params=pltpu.CompilerParams(vmem_limit_bytes=20 * 1024 * 1024),
         cost_estimate=pl.CostEstimate(
-            flops=2 * count * model * inner, bytes_accessed=2 * model * inner, transcendentals=0
+            flops=2 * ROWS * model * inner, bytes_accessed=2 * model * inner, transcendentals=0
         ),
         name="project",
     )(part, rows, weight)
@@ -457,16 +468,12 @@
     return total.astype(jnp.bfloat16)
 
 
-def spread_gains(gains, z):
+def sum_gains(gains):
     moved = [
         lax.ppermute(gains, "dp", [(i, (i + step) % 4) for i in range(4)]) for step in (1, 2, 3)
     ]
     total = (gains + moved[1]) + (moved[0] + moved[2])
-    mine = jnp.arange(HEADS_LOCAL, dtype=jnp.int32)[:, None, None] == z
-    total = jnp.where(mine, total[None], 0.0)
-    for distance in (1, 2, 4, 8):
-        total = total + lax.ppermute(total, "ctx", [(i, i ^ distance) for i in range(16)])
-    return total
+    return total + swap_half(total)
 
 
 def local(q_raw, k_raw, values, d_out, q_gain, k_gain, q_weight, doc_lengths):
@@ -487,8 +494,8 @@
     wide = 2 * ROWS * PAIRS
     first = low[:, 0] // wide
     last = pos[:, -1] // wide + 1
-    inner = jnp.clip((low[:, -1] + wide - 1) // wide, first, last)
-    diagonal = jnp.clip(pos[:, 0] // wide, inner, last)
+    diagonal = jnp.clip(pos[:, 0] // wide, first, last)
+    inner = jnp.clip((low[:, -1] + wide - 1) // wide, first, diagonal)
     bounds = jnp.stack([first, inner, diagonal, last], axis=1).astype(jnp.int32)
 
     own = along_z(pack(k_raw[0], values[0]))
@@ -499,12 +506,13 @@
         key_prep(k_gain_row, own),
         key_prep(k_gain_row, other),
     )
-    dq, query_gain_sum, sums, other_sums = attention(
+    dq, sums, other_sums = attention(
         bounds,
         half.reshape(1),
         pos,
         low,
         q_gain_row,
+        k_gain_row,
         queries_grads,
         ((norm_own, turned_own), (norm_other, turned_other)),
         (own, other),
@@ -512,15 +520,14 @@
 
     returned = along_z(dq)
     moved = swap_half(other_sums)
-    key_gain_sum = key_gain(sums, other_sums, (own, other))
-    gains = spread_gains(jnp.concatenate([query_gain_sum, key_gain_sum], axis=0), z)
-    key_gain_sum, returned = lax.optimization_barrier((key_gain_sum, returned))
-    parts = project(lax.axis_index("tp").reshape(1), q_weight, returned, 4)
+    *parts, gains = project(lax.axis_index("tp").reshape(1), q_weight, returned, 4)
     moved, *parts = lax.optimization_barrier((moved, *parts))
     input_grad = sum_tp(parts)
-    pieces_back = along_z(finish(sums, moved, own, k_gain_row))
-    value_grad, key_grad = unpack(pieces_back)
-    return (input_grad[None], key_grad[None], value_grad[None], gains[:, 0], gains[:, 1])
+    finished = finish(sums, moved, own, k_gain_row)
+    gains, finished = lax.optimization_barrier((gains, finished))
+    gains = sum_gains(gains)
+    value_grad, key_grad = unpack(along_z(finished))
+    return (input_grad[None], key_grad[None], value_grad[None], gains[:HEADS_LOCAL], gains[HEADS_LOCAL:])
 
 
 def solution(mesh):

time: 193 us -> 180 us (0.933)
  starting transfers between devices: 56.6 us -> 45 us
  Pallas kernels: 59.6 us -> 51.2 us
  waiting for transfers between devices: 65.8 us -> 70.6 us
    ppermute x7 -> x3, starting transfers between devices: 16.4 us -> 2 us  [sum_gains(): lax.ppermute(gains, 'dp', [(i, (i + step) % 4) for i in range(4)])]
    pallas_call x3 -> x2, Pallas kernels: 41.7 us -> 33.1 us  [the longest x1 30.4 us: attention(): pl.pallas_call(attention_kernel, in_specs=[SMEM_SPEC, SMEM_SPEC] + [VMEM_...]
    ppermute x7 -> x3, waiting for transfers between devices: 10.4 us -> 3.02 us  [sum_gains(): lax.ppermute(gains, 'dp', [(i, (i + step) % 4) for i in range(4)])]
    ppermute x3, waiting for transfers between devices: 1.88 us -> 7.92 us  [sum_tp(): total = total + lax.ppermute(parts[step], 'tp', pairs).astype(jnp.float32)]
    all_to_all x4, waiting for transfers between devices: 32.8 us -> 37.8 us  [along_z(): return lax.all_to_all(pieces, 'ctx', 0, 0, axis_index_groups=Z_GROUPS)]
    ppermute x2 -> x3, starting transfers between devices: 6.36 us -> 9.09 us  [swap_half(): return lax.ppermute(piece, 'ctx', HALF_SWAP)]
    ppermute x2 -> x3, waiting for transfers between devices: 20.7 us -> 21.8 us  [swap_half(): return lax.ppermute(piece, 'ctx', HALF_SWAP)]
    unnamed x18 -> x28, local copies, waits for them, and re-layouts: 5.33 us -> 6.33 us
  transfers between devices with their start and end apart: 16 -> 13, of which waited for: 9 -> 9; matrix products, arithmetic and copies ran while one was open for 2% -> 2% of each run, Pallas kernels for 9% -> 8%
where the time goes in v3:
time: 180 us; the launch traced here: 178 us
  waiting for transfers between devices  70.6 us (39%)
  Pallas kernels  51.2 us (28%)
  starting transfers between devices  45 us (25%)
  local copies, waits for them, and re-layouts  8.21 us (5%)
  other arithmetic  2.27 us (1%)
    all_to_all x4, waiting for transfers between devices, along_z(): return lax.all_to_all(pieces, 'ctx', 0, 0, axis_index_groups=Z_GROUPS)  37.8 us
    pallas_call x1, Pallas kernels, attention(): pl.pallas_call(attention_kernel, in_specs=[SMEM_SPEC, SMEM_SPEC] + [VMEM_...  30.4 us
    all_to_all x4, starting transfers between devices, along_z(): return lax.all_to_all(pieces, 'ctx', 0, 0, axis_index_groups=Z_GROUPS)  28.1 us
    ppermute x3, waiting for transfers between devices, swap_half(): return lax.ppermute(piece, 'ctx', HALF_SWAP)  21.8 us
    pallas_call x2, Pallas kernels, key_prep(): pl.pallas_call(key_prep_kernel, in_specs=[VMEM_SPEC, ANY_SPEC], out_specs...  9.29 us
    ppermute x3, starting transfers between devices, swap_half(): return lax.ppermute(piece, 'ctx', HALF_SWAP)  9.09 us
    ppermute x3, waiting for transfers between devices, sum_tp(): total = total + lax.ppermute(parts[step], 'tp', pairs).astype(jnp.float32)  7.92 us
    unnamed x28, local copies, waits for them, and re-layouts  6.33 us
  transfers between devices with their start and end apart: 13, of which 9 were waited for; matrix products, arithmetic and copies ran while one was open for 2% of the time, Pallas kernels for 8%

profile of v3, /device:TPU:32, one launch (start us, length us, event | category | flops | bytes accessed | tf_op | source)
XLA Modules:
  0.0 178.3 jit_solution(6620783888311876515)
XLA Ops:
  0.6 2.2 %pack.3 = bf16[8,2,256,128]{3,2,1,0:T(8,128)(2,1)} custom-call(bf16[256,1024]{1,0:T(8,128)(2,1)} %bitcast.15, bf16[256,1024]{1,0:T(8,128)(2,1)} %bitcast.16), custom_call_target="tpu_custom_call" | custom-call | bytes 4194304 | tf_op jit(solution)/shard_map/pack/pallas_call | solution.py:80
  2.8 8.6 %all-to-all-start = ((bf16[8,2,256,128]{3,2,1,0:T(8,128)(2,1)}), bf16[8,2,256,128]{3,2,1,0:T(8,128)(2,1)S(1)}, u32[]{:S(2)}, u32[]{:S(2)}) async-start(bf16[8,2,256,128]{3,2,1,0:T(8,128)(2,1)} %pack.3), calls=%async_computation | async-start | bytes 2097152 | tf_op jit(solution)/shard_map/all_to_all | solution.py:455
  11.4 2.1 %pack.2 = bf16[8,2,256,128]{3,2,1,0:T(8,128)(2,1)} custom-call(bf16[256,1024]{1,0:T(8,128)(2,1)} %bitcast.17, bf16[256,1024]{1,0:T(8,128)(2,1)} %bitcast.18), custom_call_target="tpu_custom_call" | custom-call | bytes 4194304 | tf_op jit(solution)/shard_map/pack/pallas_call | solution.py:80
  13.5 25.1 %all-to-all-done.raw_ref.refs_5_ = bf16[8,2,256,128]{3,2,1,0:T(8,128)(2,1)S(1)} async-done(((bf16[8,2,256,128]{3,2,1,0:T(8,128)(2,1)}), bf16[8,2,256,128]{3,2,1,0:T(8,128)(2,1)S(1)}, u32[]{:S(2)}, u32[]{:S(2)}) %all-to-all-start) | async-done | bytes 1048608 | tf_op jit(solution)/shard_map/all_to_all | solution.py:455
  38.7 4.9 %all-to-all-start.1 = ((bf16[8,2,256,128]{3,2,1,0:T(8,128)(2,1)}), bf16[8,2,256,128]{3,2,1,0:T(8,128)(2,1)S(1)}, u32[]{:S(2)}, u32[]{:S(2)}) async-start(bf16[8,2,256,128]{3,2,1,0:T(8,128)(2,1)} %pack.2), calls=%async_computation.1 | async-start | bytes 2097152 | tf_op jit(solution)/shard_map/all_to_all | solution.py:455
  43.6 3.0 %collective-permute-start = (bf16[8,2,256,128]{3,2,1,0:T(8,128)(2,1)S(1)}, bf16[8,2,256,128]{3,2,1,0:T(8,128)(2,1)S(1)}, u32[]{:S(2)}, u32[]{:S(2)}) collective-permute-start(bf16[8,2,256,128]{3,2,1,0:T(8,128)(2,1)S(1)} %all-to-all-done.raw_ref.refs_5_), channel_id=1, source_target_pairs={{0,16},{16,0},{32,48},{48,32},{64,80},{80,64},{96,112},{112,96},{1... | collective-permute-start | bytes 3145736 | tf_op jit(solution)/shard_map/ppermute | solution.py:459
  46.8 1.3 constant_dynamic-slice_fusion
  49.0 4.6 %key_prep.2 = (bf16[8,256,128]{2,1,0:T(8,128)(2,1)}, bf16[8,128,256]{2,1,0:T(8,128)(2,1)}) custom-call(f32[1,128]{1,0:T(1,128)} %get-tuple-element.57.gain_ref.key_gain_ref, bf16[8,2,256,128]{3,2,1,0:T(8,128)(2,1)} %copy-done), custom_call_target="tpu_custom_call" | custom-call | bytes 4194304 | tf_op jit(solution)/shard_map/key_prep/pallas_call | solution.py:165
  53.7 16.2 %collective-permute-done.raw_ref.refs_6_ = bf16[8,2,256,128]{3,2,1,0:T(8,128)(2,1)S(1)} collective-permute-done((bf16[8,2,256,128]{3,2,1,0:T(8,128)(2,1)S(1)}, bf16[8,2,256,128]{3,2,1,0:T(8,128)(2,1)S(1)}, u32[]{:S(2)}, u32[]{:S(2)}) %collective-permute-start) | collective-permute-done | bytes 1048608 | tf_op jit(solution)/shard_map/ppermute | solution.py:459
  69.9 1.0 copy-done.10
  70.9 4.6 %key_prep.3 = (bf16[8,256,128]{2,1,0:T(8,128)(2,1)}, bf16[8,128,256]{2,1,0:T(8,128)(2,1)}) custom-call(f32[1,128]{1,0:T(1,128)} %get-tuple-element.57.gain_ref.key_gain_ref, bf16[8,2,256,128]{3,2,1,0:T(8,128)(2,1)} %copy-done.10), custom_call_target="tpu_custom_call" | custom-call | bytes 4194304 | tf_op jit(solution)/shard_map/key_prep/pallas_call | solution.py:165
  75.6 0.9 copy-done.9
  76.5 30.4 %attention.1 = (bf16[8,272,128]{2,1,0:T(8,128)(2,1)}, bf16[8,2,256,128]{3,2,1,0:T(8,128)(2,1)}, bf16[8,2,256,128]{3,2,1,0:T(8,128)(2,1)}) custom-call(s32[8,4]{1,0:T(8,128)} %pad_add_fusion.bounds_ref, s32[1]{0:T(128)} %bitcast.3.half_ref, s32[8,256]{1,0:T(8,128)} %copy-done.11, s32[8,256]{1,0:T(8,128)} %copy-done.12, f32[1,128]{1,0:T(1,128)} %get-tuple-element.58.gain_ref, ...), custom_call_target="tpu_custom_call" | custom-call | flops 12884901888 | bytes 8388608 | tf_op jit(solution)/shard_map/attention/pallas_call | solution.py:351
  106.9 7.4 %all-to-all-start.2 = ((bf16[8,272,128]{2,1,0:T(8,128)(2,1)}), bf16[8,272,128]{2,1,0:T(8,128)(2,1)S(1)}, u32[]{:S(2)}, u32[]{:S(2)}) async-start(bf16[8,272,128]{2,1,0:T(8,128)(2,1)} %get-tuple-element.35), calls=%async_computation.2 | async-start | bytes 1114112 | tf_op jit(solution)/shard_map/all_to_all | solution.py:455
  114.3 3.0 %collective-permute-start.1 = (bf16[8,2,256,128]{3,2,1,0:T(8,128)(2,1)}, bf16[8,2,256,128]{3,2,1,0:T(8,128)(2,1)S(1)}, u32[]{:S(2)}, u32[]{:S(2)}) collective-permute-start(bf16[8,2,256,128]{3,2,1,0:T(8,128)(2,1)} %get-tuple-element.34), channel_id=1, source_target_pairs={{0,16},{16,0},{32,48},{48,32},{64,80},{80,64},{96,112},{112,96},{1... | collective-permute-start | bytes 3145736 | tf_op jit(solution)/shard_map/ppermute | solution.py:459
  117.3 12.7 %all-to-all-done.2.rows_ref = bf16[8,272,128]{2,1,0:T(8,128)(2,1)S(1)} async-done(((bf16[8,272,128]{2,1,0:T(8,128)(2,1)}), bf16[8,272,128]{2,1,0:T(8,128)(2,1)S(1)}, u32[]{:S(2)}, u32[]{:S(2)}) %all-to-all-start.2) | async-done | bytes 557088 | tf_op jit(solution)/shard_map/all_to_all | solution.py:455
  130.0 3.4 %copy-done.2 = bf16[4096,1024]{1,0:T(8,128)(2,1)S(1)} copy-done((bf16[4096,1024]{1,0:T(8,128)(2,1)S(1)}, bf16[4096,1024]{1,0:T(8,128)(2,1)}, u32[]{:S(2)}) %copy-start.2) | copy-done | bytes 8388632
  133.4 2.4 %project.1 = (bf16[256,1024]{1,0:T(8,128)(2,1)S(1)}, bf16[256,1024]{1,0:T(8,128)(2,1)S(1)}, bf16[256,1024]{1,0:T(8,128)(2,1)S(1)}, bf16[256,1024]{1,0:T(8,128)(2,1)S(1)}, f32[16,128]{1,0:T(8,128)S(1)}) custom-call(s32[1]{0:T(128)} %bitcast.8.part_ref, bf16[8,272,128]{2,1,0:T(8,128)(2,1)S(1)} %all-to-all-done.2.rows_ref, bf16[4096,1024]{1,0:T(8,128)(2,1)S(1)} %copy-done.2), custom_call_target="tpu_custom_call" | custom-call | flops 2147483648 | bytes 8388608 | tf_op jit(solution)/shard_map/project/pallas_call | solution.py:440
  135.9 3.5 %collective-permute-done.1.other_ref = bf16[8,2,256,128]{3,2,1,0:T(8,128)(2,1)S(1)} collective-permute-done((bf16[8,2,256,128]{3,2,1,0:T(8,128)(2,1)}, bf16[8,2,256,128]{3,2,1,0:T(8,128)(2,1)S(1)}, u32[]{:S(2)}, u32[]{:S(2)}) %collective-permute-start.1) | collective-permute-done | bytes 1048608 | tf_op jit(solution)/shard_map/ppermute | solution.py:459
  139.4 2.7 %finish.1 = bf16[8,512,128]{2,1,0:T(8,128)(2,1)} custom-call(bf16[8,2,256,128]{3,2,1,0:T(8,128)(2,1)S(1)} %copy-done.3, bf16[8,2,256,128]{3,2,1,0:T(8,128)(2,1)S(1)} %collective-permute-done.1.other_ref, bf16[8,2,256,128]{3,2,1,0:T(8,128)(2,1)S(1)} %copy-done.1, f32[1,128]{1,0:T(1,128)S(1)} %copy-done.4), custom_call_target="tpu_custom_call" | custom-call | bytes 8388608 | tf_op jit(solution)/shard_map/finish/pallas_call | solution.py:405
  142.1 7.2 %all-to-all-start.3 = ((bf16[8,512,128]{2,1,0:T(8,128)(2,1)}), bf16[8,512,128]{2,1,0:T(8,128)(2,1)S(1)}, u32[]{:S(2)}, u32[]{:S(2)}) async-start(bf16[8,512,128]{2,1,0:T(8,128)(2,1)} %finish.1), calls=%async_computation.3 | async-start | bytes 2097152 | tf_op jit(solution)/shard_map/all_to_all | solution.py:455
  149.3 1.6 collective-permute-start.2
  150.9 2.9 %collective-permute-start.3 = (bf16[256,1024]{1,0:T(8,128)(2,1)}, bf16[256,1024]{1,0:T(8,128)(2,1)S(1)}, u32[]{:S(2)}, u32[]{:S(2)}) collective-permute-start(bf16[256,1024]{1,0:T(8,128)(2,1)} %copy-done.6), channel_id=1, source_target_pairs={{0,8},{4,12},{8,0},{12,4},{1,9},{5,13},{9,1},{13,5},{2,10},{6,14},... | collective-permute-start | bytes 1572872 | tf_op jit(solution)/shard_map/ppermute | solution.py:467
  153.8 1.3 collective-permute-start.4
  156.5 1.5 collective-permute-start.5
  158.2 1.9 %collective-permute-done.5 = f32[16,128]{1,0:T(8,128)S(1)} collective-permute-done((f32[16,128]{1,0:T(8,128)S(1)}, f32[16,128]{1,0:T(8,128)S(1)}, u32[]{:S(2)}, u32[]{:S(2)}) %collective-permute-start.5) | collective-permute-done | bytes 8224 | tf_op jit(solution)/shard_map/ppermute | solution.py:473
  160.1 3.0 %collective-permute-start.8 = (f32[16,128]{1,0:T(8,128)S(1)}, f32[16,128]{1,0:T(8,128)S(1)}, u32[]{:S(2)}, u32[]{:S(2)}) collective-permute-start(f32[16,128]{1,0:T(8,128)S(1)} %add_add_fusion), channel_id=1, source_target_pairs={{0,16},{16,0},{32,48},{48,32},{64,80},{80,64},{96,112},{112,96},{1... | collective-permute-start | bytes 24584 | tf_op jit(solution)/shard_map/ppermute | solution.py:459
  163.2 2.1 %collective-permute-done.8 = f32[16,128]{1,0:T(8,128)S(1)} collective-permute-done((f32[16,128]{1,0:T(8,128)S(1)}, f32[16,128]{1,0:T(8,128)S(1)}, u32[]{:S(2)}, u32[]{:S(2)}) %collective-permute-start.8) | collective-permute-done | bytes 8224 | tf_op jit(solution)/shard_map/ppermute | solution.py:459
  165.9 7.9 %collective-permute-done.3 = bf16[256,1024]{1,0:T(8,128)(2,1)S(1)} collective-permute-done((bf16[256,1024]{1,0:T(8,128)(2,1)}, bf16[256,1024]{1,0:T(8,128)(2,1)S(1)}, u32[]{:S(2)}, u32[]{:S(2)}) %collective-permute-start.3) | collective-permute-done | bytes 524320 | tf_op jit(solution)/shard_map/ppermute | solution.py:467
  173.8 1.1 fusion
  175.0 1.0 copy-done.8
  175.9 2.1 %unpack.1 = (bf16[256,1024]{1,0:T(8,128)(2,1)}, bf16[256,1024]{1,0:T(8,128)(2,1)}) custom-call(bf16[8,512,128]{2,1,0:T(8,128)(2,1)} %copy-done.8), custom_call_target="tpu_custom_call" | custom-call | bytes 4194304 | tf_op jit(solution)/shard_map/unpack/pallas_call | solution.py:121
  (42 shorter events, 3.4 us)
Async XLA Ops:
  0.6 46.0 %copy-start.13 = (s32[1,8]{1,0:T(1,128)S(1)}, s32[1,8]{1,0:T(1,128)}, u32[]{:S(2)}) copy-start(s32[1,8]{1,0:T(1,128)} %param.15) | copy-start | bytes 100
  2.8 35.9 %all-to-all-start = ((bf16[8,2,256,128]{3,2,1,0:T(8,128)(2,1)}), bf16[8,2,256,128]{3,2,1,0:T(8,128)(2,1)S(1)}, u32[]{:S(2)}, u32[]{:S(2)}) async-start(bf16[8,2,256,128]{3,2,1,0:T(8,128)(2,1)} %pack.3), calls=%async_computation | async-start | bytes 2097152 | tf_op jit(solution)/shard_map/all_to_all | solution.py:455
  38.7 10.4 %copy-start = (bf16[8,2,256,128]{3,2,1,0:T(8,128)(2,1)}, bf16[8,2,256,128]{3,2,1,0:T(8,128)(2,1)S(1)}, u32[]{:S(2)}) copy-start(bf16[8,2,256,128]{3,2,1,0:T(8,128)(2,1)S(1)} %all-to-all-done.raw_ref.refs_5_) | copy-start | bytes 3145732
  38.7 36.9 %all-to-all-start.1 = ((bf16[8,2,256,128]{3,2,1,0:T(8,128)(2,1)}), bf16[8,2,256,128]{3,2,1,0:T(8,128)(2,1)S(1)}, u32[]{:S(2)}, u32[]{:S(2)}) async-start(bf16[8,2,256,128]{3,2,1,0:T(8,128)(2,1)} %pack.2), calls=%async_computation.1 | async-start | bytes 2097152 | tf_op jit(solution)/shard_map/all_to_all | solution.py:455
  43.6 26.3 %collective-permute-start = (bf16[8,2,256,128]{3,2,1,0:T(8,128)(2,1)S(1)}, bf16[8,2,256,128]{3,2,1,0:T(8,128)(2,1)S(1)}, u32[]{:S(2)}, u32[]{:S(2)}) collective-permute-start(bf16[8,2,256,128]{3,2,1,0:T(8,128)(2,1)S(1)} %all-to-all-done.raw_ref.refs_5_), channel_id=1, source_target_pairs={{0,16},{16,0},{32,48},{48,32},{64,80},{80,64},{96,112},{112,96},{1... | collective-permute-start | bytes 3145736 | tf_op jit(solution)/shard_map/ppermute | solution.py:459
  48.2 27.4 %copy-start.11 = (s32[8,256]{1,0:T(8,128)}, s32[8,256]{1,0:T(8,128)S(1)}, u32[]{:S(2)}) copy-start(s32[8,256]{1,0:T(8,128)S(1)} %iota_add_fusion.pos_ref) | copy-start | bytes 24580
  48.3 27.3 %copy-start.12 = (s32[8,256]{1,0:T(8,128)}, s32[8,256]{1,0:T(8,128)S(1)}, u32[]{:S(2)}) copy-start(s32[8,256]{1,0:T(8,128)S(1)} %select_reduce_fusion.low_ref) | copy-start | bytes 24580
  69.9 1.0 copy-start.10
  75.5 1.0 copy-start.9
  106.9 32.5 %copy-start.1 = (bf16[8,2,256,128]{3,2,1,0:T(8,128)(2,1)S(1)}, bf16[8,2,256,128]{3,2,1,0:T(8,128)(2,1)}, u32[]{:S(2)}) copy-start(bf16[8,2,256,128]{3,2,1,0:T(8,128)(2,1)} %copy-done) | copy-start | bytes 3145732
  106.9 32.5 %copy-start.4 = (f32[1,128]{1,0:T(1,128)S(1)}, f32[1,128]{1,0:T(1,128)}, u32[]{:S(2)}) copy-start(f32[1,128]{1,0:T(1,128)} %get-tuple-element.57.gain_ref.key_gain_ref) | copy-start | bytes 1540
  106.9 23.1 %all-to-all-start.2 = ((bf16[8,272,128]{2,1,0:T(8,128)(2,1)}), bf16[8,272,128]{2,1,0:T(8,128)(2,1)S(1)}, u32[]{:S(2)}, u32[]{:S(2)}) async-start(bf16[8,272,128]{2,1,0:T(8,128)(2,1)} %get-tuple-element.35), calls=%async_computation.2 | async-start | bytes 1114112 | tf_op jit(solution)/shard_map/all_to_all | solution.py:455
  114.3 25.1 %collective-permute-start.1 = (bf16[8,2,256,128]{3,2,1,0:T(8,128)(2,1)}, bf16[8,2,256,128]{3,2,1,0:T(8,128)(2,1)S(1)}, u32[]{:S(2)}, u32[]{:S(2)}) collective-permute-start(bf16[8,2,256,128]{3,2,1,0:T(8,128)(2,1)} %get-tuple-element.34), channel_id=1, source_target_pairs={{0,16},{16,0},{32,48},{48,32},{64,80},{80,64},{96,112},{112,96},{1... | collective-permute-start | bytes 3145736 | tf_op jit(solution)/shard_map/ppermute | solution.py:459
  130.0 3.4 %copy-start.2 = (bf16[4096,1024]{1,0:T(8,128)(2,1)S(1)}, bf16[4096,1024]{1,0:T(8,128)(2,1)}, u32[]{:S(2)}) copy-start(bf16[4096,1024]{1,0:T(8,128)(2,1)} %weight_ref.1) | copy-start | bytes 25165828
  133.4 5.9 %copy-start.3 = (bf16[8,2,256,128]{3,2,1,0:T(8,128)(2,1)S(1)}, bf16[8,2,256,128]{3,2,1,0:T(8,128)(2,1)}, u32[]{:S(2)}) copy-start(bf16[8,2,256,128]{3,2,1,0:T(8,128)(2,1)} %get-tuple-element.45.own_ref) | copy-start | bytes 3145732
  135.8 6.2 %copy-start.5 = (bf16[256,1024]{1,0:T(8,128)(2,1)}, bf16[256,1024]{1,0:T(8,128)(2,1)S(1)}, u32[]{:S(2)}) copy-start(bf16[256,1024]{1,0:T(8,128)(2,1)S(1)} %get-tuple-element.43) | copy-start | bytes 1572868
  135.8 6.2 %copy-start.6 = (bf16[256,1024]{1,0:T(8,128)(2,1)}, bf16[256,1024]{1,0:T(8,128)(2,1)S(1)}, u32[]{:S(2)}) copy-start(bf16[256,1024]{1,0:T(8,128)(2,1)S(1)} %get-tuple-element.42) | copy-start | bytes 1572868
  135.8 6.2 %copy-start.7 = (bf16[256,1024]{1,0:T(8,128)(2,1)}, bf16[256,1024]{1,0:T(8,128)(2,1)S(1)}, u32[]{:S(2)}) copy-start(bf16[256,1024]{1,0:T(8,128)(2,1)S(1)} %get-tuple-element.41) | copy-start | bytes 1572868
  142.1 32.9 %all-to-all-start.3 = ((bf16[8,512,128]{2,1,0:T(8,128)(2,1)}), bf16[8,512,128]{2,1,0:T(8,128)(2,1)S(1)}, u32[]{:S(2)}, u32[]{:S(2)}) async-start(bf16[8,512,128]{2,1,0:T(8,128)(2,1)} %finish.1), calls=%async_computation.3 | async-start | bytes 2097152 | tf_op jit(solution)/shard_map/all_to_all | solution.py:455
  149.3 16.6 %collective-permute-start.2 = (bf16[256,1024]{1,0:T(8,128)(2,1)}, bf16[256,1024]{1,0:T(8,128)(2,1)S(1)}, u32[]{:S(2)}, u32[]{:S(2)}) collective-permute-start(bf16[256,1024]{1,0:T(8,128)(2,1)} %copy-done.7), channel_id=1, source_target_pairs={{0,4},{4,8},{8,12},{12,0},{1,5},{5,9},{9,13},{13,1},{2,6},{6,10},{... | collective-permute-start | bytes 1572872 | tf_op jit(solution)/shard_map/ppermute | solution.py:467
  150.9 23.0 %collective-permute-start.3 = (bf16[256,1024]{1,0:T(8,128)(2,1)}, bf16[256,1024]{1,0:T(8,128)(2,1)S(1)}, u32[]{:S(2)}, u32[]{:S(2)}) collective-permute-start(bf16[256,1024]{1,0:T(8,128)(2,1)} %copy-done.6), channel_id=1, source_target_pairs={{0,8},{4,12},{8,0},{12,4},{1,9},{5,13},{9,1},{13,5},{2,10},{6,14},... | collective-permute-start | bytes 1572872 | tf_op jit(solution)/shard_map/ppermute | solution.py:467
  153.8 20.1 %collective-permute-start.4 = (bf16[256,1024]{1,0:T(8,128)(2,1)}, bf16[256,1024]{1,0:T(8,128)(2,1)S(1)}, u32[]{:S(2)}, u32[]{:S(2)}) collective-permute-start(bf16[256,1024]{1,0:T(8,128)(2,1)} %copy-done.5), channel_id=1, source_target_pairs={{0,12},{4,0},{8,4},{12,8},{1,13},{5,1},{9,5},{13,9},{2,14},{6,2},{... | collective-permute-start | bytes 1572872 | tf_op jit(solution)/shard_map/ppermute | solution.py:467
  155.1 1.4 collective-permute-start.7
  155.1 3.1 %collective-permute-start.6 = (f32[16,128]{1,0:T(8,128)S(1)}, f32[16,128]{1,0:T(8,128)S(1)}, u32[]{:S(2)}, u32[]{:S(2)}) collective-permute-start(f32[16,128]{1,0:T(8,128)S(1)} %get-tuple-element.50), channel_id=1, source_target_pairs={{0,1},{1,2},{2,3},{3,0},{4,5},{5,6},{6,7},{7,4},{8,9},{9,10},{10,1... | collective-permute-start | bytes 24584 | tf_op jit(solution)/shard_map/ppermute | solution.py:473
  156.5 3.7 %collective-permute-start.5 = (f32[16,128]{1,0:T(8,128)S(1)}, f32[16,128]{1,0:T(8,128)S(1)}, u32[]{:S(2)}, u32[]{:S(2)}) collective-permute-start(f32[16,128]{1,0:T(8,128)S(1)} %get-tuple-element.50), channel_id=1, source_target_pairs={{0,2},{1,3},{2,0},{3,1},{4,6},{5,7},{6,4},{7,5},{8,10},{9,11},{10,... | collective-permute-start | bytes 24584 | tf_op jit(solution)/shard_map/ppermute | solution.py:473
  160.1 5.2 %collective-permute-start.8 = (f32[16,128]{1,0:T(8,128)S(1)}, f32[16,128]{1,0:T(8,128)S(1)}, u32[]{:S(2)}, u32[]{:S(2)}) collective-permute-start(f32[16,128]{1,0:T(8,128)S(1)} %add_add_fusion), channel_id=1, source_target_pairs={{0,16},{16,0},{32,48},{48,32},{64,80},{80,64},{96,112},{112,96},{1... | collective-permute-start | bytes 24584 | tf_op jit(solution)/shard_map/ppermute | solution.py:459
  175.0 1.0 copy-start.8

commit v4 on v3

--- a/solution.py
+++ b/solution.py
@@ -13,7 +13,8 @@
 HEADS_LOCAL = 8
 HD = 128
 ROWS = 256
-LANES = 256
+LANES = 512
+COLUMNS = 256
 PAIRS = 2
 WIDE = 2 * PAIRS * ROWS
 EXTRA = 16
@@ -120,7 +121,7 @@
     rows = jax.ShapeDtypeStruct((ROWS, HEADS_LOCAL * HD), jnp.bfloat16)
     return pl.pallas_call(
         unpack_kernel,
-        in_specs=[ANY_SPEC],
+        in_specs=[pl.BlockSpec(memory_space=pl.ANY)],
         out_specs=[ANY_SPEC, ANY_SPEC],
         out_shape=[rows, rows],
         scratch_shapes=[
@@ -129,6 +130,7 @@
             pltpu.SemaphoreType.DMA((HEADS_LOCAL, 2)),
         ],
         cost_estimate=pl.CostEstimate(flops=0, bytes_accessed=2**22, transcendentals=0),
+        compiler_params=pltpu.CompilerParams(vmem_limit_bytes=16 * 1024 * 1024),
         name="unpack",
     )(pieces)
 
@@ -229,14 +231,14 @@
     gain_grad_ref[...] = jnp.zeros_like(gain_grad_ref)
 
     def block_body(block, carry):
-        @pl.when(lax.rem(block, PAIRS) == 0)
-        def _():
-            for copy in loads(block // PAIRS):
-                copy.wait()
-
-        unit_rows, inverse = unit_norm(held_query[block, 0])
+        for copy in loads(block):
+            copy.wait()
+        shards = [block * PAIRS + pair for pair in range(PAIRS)]
+        unit_rows, inverse = unit_norm(
+            jnp.concatenate([held_query[shard, 0] for shard in shards], axis=0)
+        )
         query = (unit_rows * gain_ref[...]).astype(jnp.bfloat16)
-        grad = held_query[block, 1]
+        grad = jnp.concatenate([held_query[shard, 1] for shard in shards], axis=0)
         pos = pos_ref[pl.ds(block, 1), :]
         low = low_ref[pl.ds(block, 1), :]
         row = lax.broadcasted_iota(jnp.int32, (ROWS, LANES), 0)
@@ -300,13 +302,14 @@
 
         lax.fori_loop(first, last, grads_body, 0)
         query_grad = dqt_ref[...].T * FACTOR
-        held_dq[block, :ROWS] = unit_norm_backward(
-            query_grad, unit_rows, inverse, gain_ref[...]
-        ).astype(jnp.bfloat16)
+        raw_grad = unit_norm_backward(query_grad, unit_rows, inverse, gain_ref[...])
+        for pair, shard in enumerate(shards):
+            rows = slice(pair * ROWS, (pair + 1) * ROWS)
+            held_dq[shard, :ROWS] = raw_grad[rows].astype(jnp.bfloat16)
         gain_grad_ref[...] += jnp.sum(query_grad * unit_rows, axis=0, keepdims=True)
         return carry
 
-    lax.fori_loop(0, DEPTH, block_body, 0)
+    lax.fori_loop(0, DEPTH // PAIRS, block_body, 0)
     key_total = jnp.zeros((ROWS, HD), jnp.float32)
     for tile in range(DEPTH):
         for side in range(2):
@@ -427,9 +430,9 @@
             gains_ref[place : place + 1, :] = (third + second) + first
     for step, out_ref in enumerate(outs):
         base = lax.rem(part_ref[0] + step, len(outs)) * width
-        for start in range(0, width, LANES):
-            rows = pl.ds(pl.multiple_of(base + start, LANES), LANES)
-            out_ref[:, start : start + LANES] = nt_dot(
+        for start in range(0, width, COLUMNS):
+            rows = pl.ds(pl.multiple_of(base + start, COLUMNS), COLUMNS)
+            out_ref[:, start : start + COLUMNS] = nt_dot(
                 joined_ref[...], weight_ref[rows, :]
             ).astype(jnp.bfloat16)
 
@@ -488,6 +491,7 @@
     pos = (2 * jnp.arange(8, dtype=jnp.int32)[:, None] + half) * ROWS + jnp.arange(
         ROWS, dtype=jnp.int32
     )
+    pos = pos.reshape(DEPTH // PAIRS, LANES)
     low = jnp.max(
         jnp.where(starts[None, None, :] <= pos[:, :, None], starts[None, None, :], 0), axis=2
     )

time: 180 us -> 174 us (0.967)
  Pallas kernels: 51.2 us -> 46.1 us
    pallas_call x1, Pallas kernels: 30.4 us -> 25 us  [attention(): pl.pallas_call(attention_kernel, in_specs=[SMEM_SPEC, SMEM_SPEC] + [VMEM_...]
    unnamed x28 -> x32, local copies, waits for them, and re-layouts: 6.33 us -> 5.44 us
where the time goes in v4:
time: 174 us; the launch traced here: 172 us
  waiting for transfers between devices  70.6 us (41%)
  Pallas kernels  46.1 us (26%)
  starting transfers between devices  45 us (26%)
  local copies, waits for them, and re-layouts  7.33 us (4%)
  other arithmetic  2.2 us (1%)
    all_to_all x4, waiting for transfers between devices, along_z(): return lax.all_to_all(pieces, 'ctx', 0, 0, axis_index_groups=Z_GROUPS)  37.9 us
    all_to_all x4, starting transfers between devices, along_z(): return lax.all_to_all(pieces, 'ctx', 0, 0, axis_index_groups=Z_GROUPS)  28.1 us
    pallas_call x1, Pallas kernels, attention(): pl.pallas_call(attention_kernel, in_specs=[SMEM_SPEC, SMEM_SPEC] + [VMEM_...  25 us
    ppermute x3, waiting for transfers between devices, swap_half(): return lax.ppermute(piece, 'ctx', HALF_SWAP)  21.9 us
    pallas_call x2, Pallas kernels, key_prep(): pl.pallas_call(key_prep_kernel, in_specs=[VMEM_SPEC, ANY_SPEC], out_specs...  9.29 us
    ppermute x3, starting transfers between devices, swap_half(): return lax.ppermute(piece, 'ctx', HALF_SWAP)  9.07 us
    ppermute x3, waiting for transfers between devices, sum_tp(): total = total + lax.ppermute(parts[step], 'tp', pairs).astype(jnp.float32)  7.89 us
    ppermute x3, starting transfers between devices, sum_tp(): total = total + lax.ppermute(parts[step], 'tp', pairs).astype(jnp.float32)  5.83 us
  transfers between devices with their start and end apart: 13, of which 9 were waited for; matrix products, arithmetic and copies ran while one was open for 2% of the time, Pallas kernels for 8%

profile of v4, /device:TPU:32, one launch (start us, length us, event | category | flops | bytes accessed | tf_op | source)
XLA Modules:
  0.0 172.3 jit_solution(8743079533204226429)
XLA Ops:
  0.6 2.2 %pack.3 = bf16[8,2,256,128]{3,2,1,0:T(8,128)(2,1)} custom-call(bf16[256,1024]{1,0:T(8,128)(2,1)} %bitcast.25, bf16[256,1024]{1,0:T(8,128)(2,1)} %bitcast.26), custom_call_target="tpu_custom_call" | custom-call | bytes 4194304 | tf_op jit(solution)/shard_map/pack/pallas_call | solution.py:81
  2.8 8.6 %all-to-all-start = ((bf16[8,2,256,128]{3,2,1,0:T(8,128)(2,1)}), bf16[8,2,256,128]{3,2,1,0:T(8,128)(2,1)S(1)}, u32[]{:S(2)}, u32[]{:S(2)}) async-start(bf16[8,2,256,128]{3,2,1,0:T(8,128)(2,1)} %pack.3), calls=%async_computation | async-start | bytes 2097152 | tf_op jit(solution)/shard_map/all_to_all | solution.py:458
  11.4 2.1 %pack.2 = bf16[8,2,256,128]{3,2,1,0:T(8,128)(2,1)} custom-call(bf16[256,1024]{1,0:T(8,128)(2,1)} %bitcast.27, bf16[256,1024]{1,0:T(8,128)(2,1)} %bitcast.28), custom_call_target="tpu_custom_call" | custom-call | bytes 4194304 | tf_op jit(solution)/shard_map/pack/pallas_call | solution.py:81
  13.5 25.1 %all-to-all-done.raw_ref.refs_5_ = bf16[8,2,256,128]{3,2,1,0:T(8,128)(2,1)S(1)} async-done(((bf16[8,2,256,128]{3,2,1,0:T(8,128)(2,1)}), bf16[8,2,256,128]{3,2,1,0:T(8,128)(2,1)S(1)}, u32[]{:S(2)}, u32[]{:S(2)}) %all-to-all-start) | async-done | bytes 1048608 | tf_op jit(solution)/shard_map/all_to_all | solution.py:458
  38.7 4.9 %all-to-all-start.1 = ((bf16[8,2,256,128]{3,2,1,0:T(8,128)(2,1)}), bf16[8,2,256,128]{3,2,1,0:T(8,128)(2,1)S(1)}, u32[]{:S(2)}, u32[]{:S(2)}) async-start(bf16[8,2,256,128]{3,2,1,0:T(8,128)(2,1)} %pack.2), calls=%async_computation.1 | async-start | bytes 2097152 | tf_op jit(solution)/shard_map/all_to_all | solution.py:458
  43.7 3.0 %collective-permute-start = (bf16[8,2,256,128]{3,2,1,0:T(8,128)(2,1)S(1)}, bf16[8,2,256,128]{3,2,1,0:T(8,128)(2,1)S(1)}, u32[]{:S(2)}, u32[]{:S(2)}) collective-permute-start(bf16[8,2,256,128]{3,2,1,0:T(8,128)(2,1)S(1)} %all-to-all-done.raw_ref.refs_5_), channel_id=1, source_target_pairs={{0,16},{16,0},{32,48},{48,32},{64,80},{80,64},{96,112},{112,96},{1... | collective-permute-start | bytes 3145736 | tf_op jit(solution)/shard_map/ppermute | solution.py:462
  46.9 1.3 constant_dynamic-slice_fusion
  49.1 4.6 %key_prep.2 = (bf16[8,256,128]{2,1,0:T(8,128)(2,1)}, bf16[8,128,256]{2,1,0:T(8,128)(2,1)}) custom-call(f32[1,128]{1,0:T(1,128)} %get-tuple-element.59.gain_ref.key_gain_ref, bf16[8,2,256,128]{3,2,1,0:T(8,128)(2,1)} %copy-done), custom_call_target="tpu_custom_call" | custom-call | bytes 4194304 | tf_op jit(solution)/shard_map/key_prep/pallas_call | solution.py:167
  53.7 16.3 %collective-permute-done.raw_ref.refs_6_ = bf16[8,2,256,128]{3,2,1,0:T(8,128)(2,1)S(1)} collective-permute-done((bf16[8,2,256,128]{3,2,1,0:T(8,128)(2,1)S(1)}, bf16[8,2,256,128]{3,2,1,0:T(8,128)(2,1)S(1)}, u32[]{:S(2)}, u32[]{:S(2)}) %collective-permute-start) | collective-permute-done | bytes 1048608 | tf_op jit(solution)/shard_map/ppermute | solution.py:462
  70.0 1.0 copy-done.9
  71.0 4.6 %key_prep.3 = (bf16[8,256,128]{2,1,0:T(8,128)(2,1)}, bf16[8,128,256]{2,1,0:T(8,128)(2,1)}) custom-call(f32[1,128]{1,0:T(1,128)} %get-tuple-element.59.gain_ref.key_gain_ref, bf16[8,2,256,128]{3,2,1,0:T(8,128)(2,1)} %copy-done.9), custom_call_target="tpu_custom_call" | custom-call | bytes 4194304 | tf_op jit(solution)/shard_map/key_prep/pallas_call | solution.py:167
  75.7 0.9 copy-done.8
  76.6 25.0 %attention.1 = (bf16[8,272,128]{2,1,0:T(8,128)(2,1)}, bf16[8,2,256,128]{3,2,1,0:T(8,128)(2,1)}, bf16[8,2,256,128]{3,2,1,0:T(8,128)(2,1)}) custom-call(s32[4,4]{1,0:T(4,128)} %pad_add_fusion.bounds_ref, s32[1]{0:T(128)} %bitcast.3.half_ref, s32[4,512]{1,0:T(4,128)} %copy-done.10, s32[4,512]{1,0:T(4,128)} %copy-done.11, f32[1,128]{1,0:T(1,128)} %get-tuple-element.60.gain_ref, ...), custom_call_target="tpu_custom_call" | custom-call | flops 12884901888 | bytes 8388608 | tf_op jit(solution)/shard_map/attention/pallas_call | solution.py:354
  101.6 7.4 %all-to-all-start.2 = ((bf16[8,272,128]{2,1,0:T(8,128)(2,1)}), bf16[8,272,128]{2,1,0:T(8,128)(2,1)S(1)}, u32[]{:S(2)}, u32[]{:S(2)}) async-start(bf16[8,272,128]{2,1,0:T(8,128)(2,1)} %get-tuple-element.35), calls=%async_computation.2 | async-start | bytes 1114112 | tf_op jit(solution)/shard_map/all_to_all | solution.py:458
  109.0 3.0 %collective-permute-start.1 = (bf16[8,2,256,128]{3,2,1,0:T(8,128)(2,1)}, bf16[8,2,256,128]{3,2,1,0:T(8,128)(2,1)S(1)}, u32[]{:S(2)}, u32[]{:S(2)}) collective-permute-start(bf16[8,2,256,128]{3,2,1,0:T(8,128)(2,1)} %get-tuple-element.34), channel_id=1, source_target_pairs={{0,16},{16,0},{32,48},{48,32},{64,80},{80,64},{96,112},{112,96},{1... | collective-permute-start | bytes 3145736 | tf_op jit(solution)/shard_map/ppermute | solution.py:462
  112.0 12.7 %all-to-all-done.2.rows_ref = bf16[8,272,128]{2,1,0:T(8,128)(2,1)S(1)} async-done(((bf16[8,272,128]{2,1,0:T(8,128)(2,1)}), bf16[8,272,128]{2,1,0:T(8,128)(2,1)S(1)}, u32[]{:S(2)}, u32[]{:S(2)}) %all-to-all-start.2) | async-done | bytes 557088 | tf_op jit(solution)/shard_map/all_to_all | solution.py:458
  124.7 3.4 %copy-done.2 = bf16[4096,1024]{1,0:T(8,128)(2,1)S(1)} copy-done((bf16[4096,1024]{1,0:T(8,128)(2,1)S(1)}, bf16[4096,1024]{1,0:T(8,128)(2,1)}, u32[]{:S(2)}) %copy-start.2) | copy-done | bytes 8388632
  128.1 2.4 %project.1 = (bf16[256,1024]{1,0:T(8,128)(2,1)S(1)}, bf16[256,1024]{1,0:T(8,128)(2,1)S(1)}, bf16[256,1024]{1,0:T(8,128)(2,1)S(1)}, bf16[256,1024]{1,0:T(8,128)(2,1)S(1)}, f32[16,128]{1,0:T(8,128)S(1)}) custom-call(s32[1]{0:T(128)} %bitcast.8.part_ref, bf16[8,272,128]{2,1,0:T(8,128)(2,1)S(1)} %all-to-all-done.2.rows_ref, bf16[4096,1024]{1,0:T(8,128)(2,1)S(1)} %copy-done.2), custom_call_target="tpu_custom_call" | custom-call | flops 2147483648 | bytes 8388608 | tf_op jit(solution)/shard_map/project/pallas_call | solution.py:443
  130.6 3.5 %collective-permute-done.1.other_ref = bf16[8,2,256,128]{3,2,1,0:T(8,128)(2,1)S(1)} collective-permute-done((bf16[8,2,256,128]{3,2,1,0:T(8,128)(2,1)}, bf16[8,2,256,128]{3,2,1,0:T(8,128)(2,1)S(1)}, u32[]{:S(2)}, u32[]{:S(2)}) %collective-permute-start.1) | collective-permute-done | bytes 1048608 | tf_op jit(solution)/shard_map/ppermute | solution.py:462
  134.1 2.7 %finish.1 = bf16[8,512,128]{2,1,0:T(8,128)(2,1)} custom-call(bf16[8,2,256,128]{3,2,1,0:T(8,128)(2,1)S(1)} %copy-done.3, bf16[8,2,256,128]{3,2,1,0:T(8,128)(2,1)S(1)} %collective-permute-done.1.other_ref, bf16[8,2,256,128]{3,2,1,0:T(8,128)(2,1)S(1)} %copy-done.1, f32[1,128]{1,0:T(1,128)S(1)} %copy-done.4), custom_call_target="tpu_custom_call" | custom-call | bytes 8388608 | tf_op jit(solution)/shard_map/finish/pallas_call | solution.py:408
  136.8 7.2 %all-to-all-start.3 = ((bf16[8,512,128]{2,1,0:T(8,128)(2,1)}), bf16[8,512,128]{2,1,0:T(8,128)(2,1)S(1)}, u32[]{:S(2)}, u32[]{:S(2)}) async-start(bf16[8,512,128]{2,1,0:T(8,128)(2,1)} %finish.1), calls=%async_computation.3 | async-start | bytes 2097152 | tf_op jit(solution)/shard_map/all_to_all | solution.py:458
  144.0 1.6 collective-permute-start.2
  145.6 2.9 %collective-permute-start.3 = (bf16[256,1024]{1,0:T(8,128)(2,1)}, bf16[256,1024]{1,0:T(8,128)(2,1)S(1)}, u32[]{:S(2)}, u32[]{:S(2)}) collective-permute-start(bf16[256,1024]{1,0:T(8,128)(2,1)} %copy-done.6), channel_id=1, source_target_pairs={{0,8},{4,12},{8,0},{12,4},{1,9},{5,13},{9,1},{13,5},{2,10},{6,14},... | collective-permute-start | bytes 1572872 | tf_op jit(solution)/shard_map/ppermute | solution.py:470
  148.5 1.3 collective-permute-start.4
  150.3 0.9 collective-permute-done.7
  151.2 1.5 collective-permute-start.5
  152.9 1.9 %collective-permute-done.5 = f32[16,128]{1,0:T(8,128)S(1)} collective-permute-done((f32[16,128]{1,0:T(8,128)S(1)}, f32[16,128]{1,0:T(8,128)S(1)}, u32[]{:S(2)}, u32[]{:S(2)}) %collective-permute-start.5) | collective-permute-done | bytes 8224 | tf_op jit(solution)/shard_map/ppermute | solution.py:476
  154.8 3.0 %collective-permute-start.8 = (f32[16,128]{1,0:T(8,128)S(1)}, f32[16,128]{1,0:T(8,128)S(1)}, u32[]{:S(2)}, u32[]{:S(2)}) collective-permute-start(f32[16,128]{1,0:T(8,128)S(1)} %add_add_fusion), channel_id=1, source_target_pairs={{0,16},{16,0},{32,48},{48,32},{64,80},{80,64},{96,112},{112,96},{1... | collective-permute-start | bytes 24584 | tf_op jit(solution)/shard_map/ppermute | solution.py:462
  157.9 2.1 %collective-permute-done.8 = f32[16,128]{1,0:T(8,128)S(1)} collective-permute-done((f32[16,128]{1,0:T(8,128)S(1)}, f32[16,128]{1,0:T(8,128)S(1)}, u32[]{:S(2)}, u32[]{:S(2)}) %collective-permute-start.8) | collective-permute-done | bytes 8224 | tf_op jit(solution)/shard_map/ppermute | solution.py:462
  160.6 7.9 %collective-permute-done.3 = bf16[256,1024]{1,0:T(8,128)(2,1)S(1)} collective-permute-done((bf16[256,1024]{1,0:T(8,128)(2,1)}, bf16[256,1024]{1,0:T(8,128)(2,1)S(1)}, u32[]{:S(2)}, u32[]{:S(2)}) %collective-permute-start.3) | collective-permute-done | bytes 524320 | tf_op jit(solution)/shard_map/ppermute | solution.py:470
  168.5 1.1 fusion
  169.6 2.5 %unpack.1 = (bf16[256,1024]{1,0:T(8,128)(2,1)}, bf16[256,1024]{1,0:T(8,128)(2,1)}) custom-call(bf16[8,512,128]{2,1,0:T(8,128)(2,1)S(1)} %all-to-all-done.3.pieces_ref), custom_call_target="tpu_custom_call" | custom-call | bytes 4194304 | tf_op jit(solution)/shard_map/unpack/pallas_call | solution.py:122
  (46 shorter events, 2.6 us)
Async XLA Ops:
  0.6 46.1 %copy-start.12 = (s32[1,8]{1,0:T(1,128)S(1)}, s32[1,8]{1,0:T(1,128)}, u32[]{:S(2)}) copy-start(s32[1,8]{1,0:T(1,128)} %param.15) | copy-start | bytes 100
  2.8 35.9 %all-to-all-start = ((bf16[8,2,256,128]{3,2,1,0:T(8,128)(2,1)}), bf16[8,2,256,128]{3,2,1,0:T(8,128)(2,1)S(1)}, u32[]{:S(2)}, u32[]{:S(2)}) async-start(bf16[8,2,256,128]{3,2,1,0:T(8,128)(2,1)} %pack.3), calls=%async_computation | async-start | bytes 2097152 | tf_op jit(solution)/shard_map/all_to_all | solution.py:458
  38.7 10.4 %copy-start = (bf16[8,2,256,128]{3,2,1,0:T(8,128)(2,1)}, bf16[8,2,256,128]{3,2,1,0:T(8,128)(2,1)S(1)}, u32[]{:S(2)}) copy-start(bf16[8,2,256,128]{3,2,1,0:T(8,128)(2,1)S(1)} %all-to-all-done.raw_ref.refs_5_) | copy-start | bytes 3145732
  38.7 37.0 %all-to-all-start.1 = ((bf16[8,2,256,128]{3,2,1,0:T(8,128)(2,1)}), bf16[8,2,256,128]{3,2,1,0:T(8,128)(2,1)S(1)}, u32[]{:S(2)}, u32[]{:S(2)}) async-start(bf16[8,2,256,128]{3,2,1,0:T(8,128)(2,1)} %pack.2), calls=%async_computation.1 | async-start | bytes 2097152 | tf_op jit(solution)/shard_map/all_to_all | solution.py:458
  43.7 26.3 %collective-permute-start = (bf16[8,2,256,128]{3,2,1,0:T(8,128)(2,1)S(1)}, bf16[8,2,256,128]{3,2,1,0:T(8,128)(2,1)S(1)}, u32[]{:S(2)}, u32[]{:S(2)}) collective-permute-start(bf16[8,2,256,128]{3,2,1,0:T(8,128)(2,1)S(1)} %all-to-all-done.raw_ref.refs_5_), channel_id=1, source_target_pairs={{0,16},{16,0},{32,48},{48,32},{64,80},{80,64},{96,112},{112,96},{1... | collective-permute-start | bytes 3145736 | tf_op jit(solution)/shard_map/ppermute | solution.py:462
  48.2 27.4 %copy-start.10 = (s32[4,512]{1,0:T(4,128)}, s32[4,512]{1,0:T(4,128)S(1)}, u32[]{:S(2)}) copy-start(s32[4,512]{1,0:T(4,128)S(1)} %get-tuple-element.57.pos_ref) | copy-start | bytes 24580
  48.3 27.3 %copy-start.11 = (s32[4,512]{1,0:T(4,128)}, s32[4,512]{1,0:T(4,128)S(1)}, u32[]{:S(2)}) copy-start(s32[4,512]{1,0:T(4,128)S(1)} %select_reduce_fusion.low_ref) | copy-start | bytes 24580
  70.0 1.0 copy-start.9
  75.7 1.0 copy-start.8
  101.6 32.5 %copy-start.1 = (bf16[8,2,256,128]{3,2,1,0:T(8,128)(2,1)S(1)}, bf16[8,2,256,128]{3,2,1,0:T(8,128)(2,1)}, u32[]{:S(2)}) copy-start(bf16[8,2,256,128]{3,2,1,0:T(8,128)(2,1)} %copy-done) | copy-start | bytes 3145732
  101.6 32.5 %copy-start.4 = (f32[1,128]{1,0:T(1,128)S(1)}, f32[1,128]{1,0:T(1,128)}, u32[]{:S(2)}) copy-start(f32[1,128]{1,0:T(1,128)} %get-tuple-element.59.gain_ref.key_gain_ref) | copy-start | bytes 1540
  101.6 23.1 %all-to-all-start.2 = ((bf16[8,272,128]{2,1,0:T(8,128)(2,1)}), bf16[8,272,128]{2,1,0:T(8,128)(2,1)S(1)}, u32[]{:S(2)}, u32[]{:S(2)}) async-start(bf16[8,272,128]{2,1,0:T(8,128)(2,1)} %get-tuple-element.35), calls=%async_computation.2 | async-start | bytes 1114112 | tf_op jit(solution)/shard_map/all_to_all | solution.py:458
  109.0 25.0 %collective-permute-start.1 = (bf16[8,2,256,128]{3,2,1,0:T(8,128)(2,1)}, bf16[8,2,256,128]{3,2,1,0:T(8,128)(2,1)S(1)}, u32[]{:S(2)}, u32[]{:S(2)}) collective-permute-start(bf16[8,2,256,128]{3,2,1,0:T(8,128)(2,1)} %get-tuple-element.34), channel_id=1, source_target_pairs={{0,16},{16,0},{32,48},{48,32},{64,80},{80,64},{96,112},{112,96},{1... | collective-permute-start | bytes 3145736 | tf_op jit(solution)/shard_map/ppermute | solution.py:462
  124.7 3.4 %copy-start.2 = (bf16[4096,1024]{1,0:T(8,128)(2,1)S(1)}, bf16[4096,1024]{1,0:T(8,128)(2,1)}, u32[]{:S(2)}) copy-start(bf16[4096,1024]{1,0:T(8,128)(2,1)} %weight_ref.1) | copy-start | bytes 25165828
  128.1 5.9 %copy-start.3 = (bf16[8,2,256,128]{3,2,1,0:T(8,128)(2,1)S(1)}, bf16[8,2,256,128]{3,2,1,0:T(8,128)(2,1)}, u32[]{:S(2)}) copy-start(bf16[8,2,256,128]{3,2,1,0:T(8,128)(2,1)} %get-tuple-element.45.own_ref) | copy-start | bytes 3145732
  130.5 6.2 %copy-start.5 = (bf16[256,1024]{1,0:T(8,128)(2,1)}, bf16[256,1024]{1,0:T(8,128)(2,1)S(1)}, u32[]{:S(2)}) copy-start(bf16[256,1024]{1,0:T(8,128)(2,1)S(1)} %get-tuple-element.43) | copy-start | bytes 1572868
  130.5 6.2 %copy-start.6 = (bf16[256,1024]{1,0:T(8,128)(2,1)}, bf16[256,1024]{1,0:T(8,128)(2,1)S(1)}, u32[]{:S(2)}) copy-start(bf16[256,1024]{1,0:T(8,128)(2,1)S(1)} %get-tuple-element.42) | copy-start | bytes 1572868
  130.6 6.2 %copy-start.7 = (bf16[256,1024]{1,0:T(8,128)(2,1)}, bf16[256,1024]{1,0:T(8,128)(2,1)S(1)}, u32[]{:S(2)}) copy-start(bf16[256,1024]{1,0:T(8,128)(2,1)S(1)} %get-tuple-element.41) | copy-start | bytes 1572868
  136.8 32.9 %all-to-all-start.3 = ((bf16[8,512,128]{2,1,0:T(8,128)(2,1)}), bf16[8,512,128]{2,1,0:T(8,128)(2,1)S(1)}, u32[]{:S(2)}, u32[]{:S(2)}) async-start(bf16[8,512,128]{2,1,0:T(8,128)(2,1)} %finish.1), calls=%async_computation.3 | async-start | bytes 2097152 | tf_op jit(solution)/shard_map/all_to_all | solution.py:458
  144.0 16.6 %collective-permute-start.2 = (bf16[256,1024]{1,0:T(8,128)(2,1)}, bf16[256,1024]{1,0:T(8,128)(2,1)S(1)}, u32[]{:S(2)}, u32[]{:S(2)}) collective-permute-start(bf16[256,1024]{1,0:T(8,128)(2,1)} %copy-done.7), channel_id=1, source_target_pairs={{0,4},{4,8},{8,12},{12,0},{1,5},{5,9},{9,13},{13,1},{2,6},{6,10},{... | collective-permute-start | bytes 1572872 | tf_op jit(solution)/shard_map/ppermute | solution.py:470
  145.6 22.9 %collective-permute-start.3 = (bf16[256,1024]{1,0:T(8,128)(2,1)}, bf16[256,1024]{1,0:T(8,128)(2,1)S(1)}, u32[]{:S(2)}, u32[]{:S(2)}) collective-permute-start(bf16[256,1024]{1,0:T(8,128)(2,1)} %copy-done.6), channel_id=1, source_target_pairs={{0,8},{4,12},{8,0},{12,4},{1,9},{5,13},{9,1},{13,5},{2,10},{6,14},... | collective-permute-start | bytes 1572872 | tf_op jit(solution)/shard_map/ppermute | solution.py:470
  148.5 20.0 %collective-permute-start.4 = (bf16[256,1024]{1,0:T(8,128)(2,1)}, bf16[256,1024]{1,0:T(8,128)(2,1)S(1)}, u32[]{:S(2)}, u32[]{:S(2)}) collective-permute-start(bf16[256,1024]{1,0:T(8,128)(2,1)} %copy-done.5), channel_id=1, source_target_pairs={{0,12},{4,0},{8,4},{12,8},{1,13},{5,1},{9,5},{13,9},{2,14},{6,2},{... | collective-permute-start | bytes 1572872 | tf_op jit(solution)/shard_map/ppermute | solution.py:470
  149.8 1.4 collective-permute-start.7
  149.8 3.1 %collective-permute-start.6 = (f32[16,128]{1,0:T(8,128)S(1)}, f32[16,128]{1,0:T(8,128)S(1)}, u32[]{:S(2)}, u32[]{:S(2)}) collective-permute-start(f32[16,128]{1,0:T(8,128)S(1)} %get-tuple-element.50), channel_id=1, source_target_pairs={{0,1},{1,2},{2,3},{3,0},{4,5},{5,6},{6,7},{7,4},{8,9},{9,10},{10,1... | collective-permute-start | bytes 24584 | tf_op jit(solution)/shard_map/ppermute | solution.py:476
  151.2 3.7 %collective-permute-start.5 = (f32[16,128]{1,0:T(8,128)S(1)}, f32[16,128]{1,0:T(8,128)S(1)}, u32[]{:S(2)}, u32[]{:S(2)}) collective-permute-start(f32[16,128]{1,0:T(8,128)S(1)} %get-tuple-element.50), channel_id=1, source_target_pairs={{0,2},{1,3},{2,0},{3,1},{4,6},{5,7},{6,4},{7,5},{8,10},{9,11},{10,... | collective-permute-start | bytes 24584 | tf_op jit(solution)/shard_map/ppermute | solution.py:476
  154.8 5.2 %collective-permute-start.8 = (f32[16,128]{1,0:T(8,128)S(1)}, f32[16,128]{1,0:T(8,128)S(1)}, u32[]{:S(2)}, u32[]{:S(2)}) collective-permute-start(f32[16,128]{1,0:T(8,128)S(1)} %add_add_fusion), channel_id=1, source_target_pairs={{0,16},{16,0},{32,48},{48,32},{64,80},{80,64},{96,112},{112,96},{1... | collective-permute-start | bytes 24584 | tf_op jit(solution)/shard_map/ppermute | solution.py:462

commit v5 on v4

--- a/solution.py
+++ b/solution.py
@@ -139,9 +139,13 @@
     return pl.BlockSpec(shape, lambda i: (0,) * len(shape))
 
 
-def key_prep_kernel(gain_ref, raw_ref, norm_ref, turned_ref, held_raw, held_norm, held_turned, in_sem, out_sem):
+def key_prep_kernel(paired, gain_ref, raw_ref, norm_ref, turned_ref, held_raw, held_norm, held_turned, in_sem, out_sem):
     inward = [
-        pltpu.make_async_copy(raw_ref.at[tile, 0], held_raw.at[tile], in_sem.at[tile])
+        pltpu.make_async_copy(
+            raw_ref.at[tile, 0] if paired else raw_ref.at[tile],
+            held_raw.at[tile],
+            in_sem.at[tile],
+        )
         for tile in range(DEPTH)
     ]
     outward = [
@@ -162,10 +166,11 @@
         copy.wait()
 
 
-def key_prep(gain, keys_values):
+def key_prep(gain, keys):
+    paired = keys.ndim == 4
     shapes = [(DEPTH, ROWS, HD), (DEPTH, HD, ROWS)]
     return pl.pallas_call(
-        key_prep_kernel,
+        functools.partial(key_prep_kernel, paired),
         in_specs=[VMEM_SPEC, ANY_SPEC],
         out_specs=[ANY_SPEC] * 2,
         out_shape=[jax.ShapeDtypeStruct(shape, jnp.bfloat16) for shape in shapes],
@@ -178,7 +183,7 @@
         ],
         cost_estimate=pl.CostEstimate(flops=0, bytes_accessed=2**22, transcendentals=0),
         name="key_prep",
-    )(gain, keys_values)
+    )(gain, keys)
 
 
 def fold(tile):
@@ -217,7 +222,8 @@
             lanes = pl.ds(side * ROWS, ROWS)
             moves.append((norms[side].at[tiles], held_norm.at[tiles, side]))
             moves.append((turned[side].at[tiles], held_turned.at[tiles, :, lanes]))
-            moves.append((raws[side].at[tiles, 1], held_value.at[tiles, side]))
+            value = raws[0].at[tiles, 1] if side == 0 else raws[1].at[tiles]
+            moves.append((value, held_value.at[tiles, side]))
         return [
             pltpu.make_async_copy(source, target, in_sem.at[step, index])
             for index, (source, target) in enumerate(moves)
@@ -505,10 +511,15 @@
     own = along_z(pack(k_raw[0], values[0]))
     sent, own = lax.optimization_barrier((pack(q_raw[0], d_out[0]), own))
     queries_grads = along_z(sent)
-    other = swap_half(own)
+    key_other = swap_half(own[:, 0])
+    keys_own = key_prep(k_gain_row, own)
+    value_own, key_other, *keys_own = lax.optimization_barrier(
+        (own[:, 1], key_other, *keys_own)
+    )
+    value_other = swap_half(value_own)
     (norm_own, turned_own), (norm_other, turned_other) = (
-        key_prep(k_gain_row, own),
-        key_prep(k_gain_row, other),
+        keys_own,
+        key_prep(k_gain_row, key_other),
     )
     dq, sums, other_sums = attention(
         bounds,
@@ -519,7 +530,7 @@
         k_gain_row,
         queries_grads,
         ((norm_own, turned_own), (norm_other, turned_other)),
-        (own, other),
+        (own, value_other),
     )
 
     returned = along_z(dq)

time: 174 us -> 172 us (0.989)
  waiting for transfers between devices: 70.6 us -> 63.2 us
  starting transfers between devices: 45 us -> 48.1 us
    ppermute x3 -> x4, waiting for transfers between devices: 21.9 us -> 17.1 us  [swap_half(): return lax.ppermute(piece, 'ctx', HALF_SWAP)]
    ppermute x3 -> x4, starting transfers between devices: 9.07 us -> 12.2 us  [swap_half(): return lax.ppermute(piece, 'ctx', HALF_SWAP)]
    all_to_all x4, waiting for transfers between devices: 37.9 us -> 36.1 us  [along_z(): return lax.all_to_all(pieces, 'ctx', 0, 0, axis_index_groups=Z_GROUPS)]
    unnamed x32 -> x36, local copies, waits for them, and re-layouts: 5.44 us -> 4.68 us
  transfers between devices with their start and end apart: 13 -> 14, of which waited for: 9 -> 10; matrix products, arithmetic and copies ran while one was open for 2% -> 4% of each run, Pallas kernels for 8% -> 8%
where the time goes in v5:
time: 172 us; the launch traced here: 171 us
  waiting for transfers between devices  63.2 us (37%)
  starting transfers between devices  48.1 us (28%)
  Pallas kernels  47.5 us (28%)
  local copies, waits for them, and re-layouts  7.91 us (5%)
  other arithmetic  2.85 us (2%)
    all_to_all x4, waiting for transfers between devices, along_z(): return lax.all_to_all(pieces, 'ctx', 0, 0, axis_index_groups=Z_GROUPS)  36.1 us
    all_to_all x4, starting transfers between devices, along_z(): return lax.all_to_all(pieces, 'ctx', 0, 0, axis_index_groups=Z_GROUPS)  28.1 us
    pallas_call x1, Pallas kernels, attention(): pl.pallas_call(attention_kernel, in_specs=[SMEM_SPEC, SMEM_SPEC] + [VMEM_...  26.4 us
    ppermute x4, waiting for transfers between devices, swap_half(): return lax.ppermute(piece, 'ctx', HALF_SWAP)  17.1 us
    ppermute x4, starting transfers between devices, swap_half(): return lax.ppermute(piece, 'ctx', HALF_SWAP)  12.2 us
    pallas_call x2, Pallas kernels, key_prep(): pl.pallas_call(functools.partial(key_prep_kernel, paired), in_specs=[VMEM...  9.21 us
    ppermute x3, waiting for transfers between devices, sum_tp(): total = total + lax.ppermute(parts[step], 'tp', pairs).astype(jnp.float32)  6.99 us
    ppermute x3, starting transfers between devices, sum_tp(): total = total + lax.ppermute(parts[step], 'tp', pairs).astype(jnp.float32)  5.83 us
  transfers between devices with their start and end apart: 14, of which 10 were waited for; matrix products, arithmetic and copies ran while one was open for 4% of the time, Pallas kernels for 8%

profile of v5, /device:TPU:32, one launch (start us, length us, event | category | flops | bytes accessed | tf_op | source)
XLA Modules:
  0.0 170.5 jit_solution(937138769698589351)
XLA Ops:
  0.7 2.2 %pack.3 = bf16[8,2,256,128]{3,2,1,0:T(8,128)(2,1)} custom-call(bf16[256,1024]{1,0:T(8,128)(2,1)} %bitcast.29, bf16[256,1024]{1,0:T(8,128)(2,1)} %bitcast.30), custom_call_target="tpu_custom_call" | custom-call | bytes 4194304 | tf_op jit(solution)/shard_map/pack/pallas_call | solution.py:81
  2.8 8.6 %all-to-all-start = ((bf16[8,2,256,128]{3,2,1,0:T(8,128)(2,1)}), bf16[8,2,256,128]{3,2,1,0:T(8,128)(2,1)S(1)}, u32[]{:S(2)}, u32[]{:S(2)}) async-start(bf16[8,2,256,128]{3,2,1,0:T(8,128)(2,1)} %pack.3), calls=%async_computation | async-start | bytes 2097152 | tf_op jit(solution)/shard_map/all_to_all | solution.py:464
  12.2 2.1 %pack.2 = bf16[8,2,256,128]{3,2,1,0:T(8,128)(2,1)} custom-call(bf16[256,1024]{1,0:T(8,128)(2,1)} %bitcast.31, bf16[256,1024]{1,0:T(8,128)(2,1)} %bitcast.32), custom_call_target="tpu_custom_call" | custom-call | bytes 4194304 | tf_op jit(solution)/shard_map/pack/pallas_call | solution.py:81
  14.4 24.3 %all-to-all-done.raw_ref.refs_5_ = bf16[8,2,256,128]{3,2,1,0:T(8,128)(2,1)S(1)} async-done(((bf16[8,2,256,128]{3,2,1,0:T(8,128)(2,1)}), bf16[8,2,256,128]{3,2,1,0:T(8,128)(2,1)S(1)}, u32[]{:S(2)}, u32[]{:S(2)}) %all-to-all-start) | async-done | bytes 1048608 | tf_op jit(solution)/shard_map/all_to_all | solution.py:464
  38.7 4.9 %all-to-all-start.1 = ((bf16[8,2,256,128]{3,2,1,0:T(8,128)(2,1)}), bf16[8,2,256,128]{3,2,1,0:T(8,128)(2,1)S(1)}, u32[]{:S(2)}, u32[]{:S(2)}) async-start(bf16[8,2,256,128]{3,2,1,0:T(8,128)(2,1)} %pack.2), calls=%async_computation.1 | async-start | bytes 2097152 | tf_op jit(solution)/shard_map/all_to_all | solution.py:464
  43.7 0.9 slice_bitcast_fusion
  44.6 3.0 %collective-permute-start = (bf16[8,256,128]{2,1,0:T(8,128)(2,1)}, bf16[8,256,128]{2,1,0:T(8,128)(2,1)S(1)}, u32[]{:S(2)}, u32[]{:S(2)}) collective-permute-start(bf16[8,256,128]{2,1,0:T(8,128)(2,1)} %get-tuple-element.62), channel_id=1, source_target_pairs={{0,16},{16,0},{32,48},{48,32},{64,80},{80,64},{96,112},{112,96},{1... | collective-permute-start | bytes 1572872 | tf_op jit(solution)/shard_map/ppermute | solution.py:468
  48.2 4.6 %key_prep.2 = (bf16[8,256,128]{2,1,0:T(8,128)(2,1)}, bf16[8,128,256]{2,1,0:T(8,128)(2,1)}) custom-call(f32[1,128]{1,0:T(1,128)} %constant_dynamic-slice_fusion.gain_ref.key_gain_ref, bf16[8,2,256,128]{3,2,1,0:T(8,128)(2,1)} %copy-done.1), custom_call_target="tpu_custom_call" | custom-call | bytes 4194304 | tf_op jit(solution)/shard_map/key_prep/pallas_call | solution.py:172
  52.8 7.1 %collective-permute-done.raw_ref = bf16[8,256,128]{2,1,0:T(8,128)(2,1)S(1)} collective-permute-done((bf16[8,256,128]{2,1,0:T(8,128)(2,1)}, bf16[8,256,128]{2,1,0:T(8,128)(2,1)S(1)}, u32[]{:S(2)}, u32[]{:S(2)}) %collective-permute-start) | collective-permute-done | bytes 524320 | tf_op jit(solution)/shard_map/ppermute | solution.py:468
  59.9 3.0 %collective-permute-start.1 = (bf16[8,256,128]{2,1,0:T(8,128)(2,1)S(1)}, bf16[8,256,128]{2,1,0:T(8,128)(2,1)S(1)}, u32[]{:S(2)}, u32[]{:S(2)}) collective-permute-start(bf16[8,256,128]{2,1,0:T(8,128)(2,1)S(1)} %get-tuple-element.41), channel_id=1, source_target_pairs={{0,16},{16,0},{32,48},{48,32},{64,80},{80,64},{96,112},{112,96},{1... | collective-permute-start | bytes 1572872 | tf_op jit(solution)/shard_map/ppermute | solution.py:468
  62.9 1.2 constant_dynamic-slice_fusion.1.gain_ref
  65.0 4.6 %key_prep.3 = (bf16[8,256,128]{2,1,0:T(8,128)(2,1)}, bf16[8,128,256]{2,1,0:T(8,128)(2,1)}) custom-call(f32[1,128]{1,0:T(1,128)} %constant_dynamic-slice_fusion.gain_ref.key_gain_ref, bf16[8,256,128]{2,1,0:T(8,128)(2,1)} %copy-done.10), custom_call_target="tpu_custom_call" | custom-call | bytes 4194304 | tf_op jit(solution)/shard_map/key_prep/pallas_call | solution.py:172
  69.6 4.4 %collective-permute-done.1.refs_6_ = bf16[8,256,128]{2,1,0:T(8,128)(2,1)S(1)} collective-permute-done((bf16[8,256,128]{2,1,0:T(8,128)(2,1)S(1)}, bf16[8,256,128]{2,1,0:T(8,128)(2,1)S(1)}, u32[]{:S(2)}, u32[]{:S(2)}) %collective-permute-start.1) | collective-permute-done | bytes 524320 | tf_op jit(solution)/shard_map/ppermute | solution.py:468
  75.2 26.4 %attention.1 = (bf16[8,272,128]{2,1,0:T(8,128)(2,1)}, bf16[8,2,256,128]{3,2,1,0:T(8,128)(2,1)}, bf16[8,2,256,128]{3,2,1,0:T(8,128)(2,1)}) custom-call(s32[4,4]{1,0:T(4,128)} %pad_add_fusion.bounds_ref, s32[1]{0:T(128)} %bitcast.3.half_ref, s32[4,512]{1,0:T(4,128)} %copy-done.11, s32[4,512]{1,0:T(4,128)} %copy-done.12, ...), custom_call_target="tpu_custom_call" | custom-call | flops 12884901888 | bytes 8388608 | tf_op jit(solution)/shard_map/attention/pallas_call | solution.py:360
  101.6 7.4 %all-to-all-start.2 = ((bf16[8,272,128]{2,1,0:T(8,128)(2,1)}), bf16[8,272,128]{2,1,0:T(8,128)(2,1)S(1)}, u32[]{:S(2)}, u32[]{:S(2)}) async-start(bf16[8,272,128]{2,1,0:T(8,128)(2,1)} %get-tuple-element.43), calls=%async_computation.2 | async-start | bytes 1114112 | tf_op jit(solution)/shard_map/all_to_all | solution.py:464
  109.0 3.1 %collective-permute-start.2 = (bf16[8,2,256,128]{3,2,1,0:T(8,128)(2,1)}, bf16[8,2,256,128]{3,2,1,0:T(8,128)(2,1)S(1)}, u32[]{:S(2)}, u32[]{:S(2)}) collective-permute-start(bf16[8,2,256,128]{3,2,1,0:T(8,128)(2,1)} %get-tuple-element.42), channel_id=1, source_target_pairs={{0,16},{16,0},{32,48},{48,32},{64,80},{80,64},{96,112},{112,96},{1... | collective-permute-start | bytes 3145736 | tf_op jit(solution)/shard_map/ppermute | solution.py:468
  112.1 11.8 %all-to-all-done.2.rows_ref = bf16[8,272,128]{2,1,0:T(8,128)(2,1)S(1)} async-done(((bf16[8,272,128]{2,1,0:T(8,128)(2,1)}), bf16[8,272,128]{2,1,0:T(8,128)(2,1)S(1)}, u32[]{:S(2)}, u32[]{:S(2)}) %all-to-all-start.2) | async-done | bytes 557088 | tf_op jit(solution)/shard_map/all_to_all | solution.py:464
  123.8 3.4 %copy-done.3 = bf16[4096,1024]{1,0:T(8,128)(2,1)S(1)} copy-done((bf16[4096,1024]{1,0:T(8,128)(2,1)S(1)}, bf16[4096,1024]{1,0:T(8,128)(2,1)}, u32[]{:S(2)}) %copy-start.3) | copy-done | bytes 8388632
  127.2 2.4 %project.1 = (bf16[256,1024]{1,0:T(8,128)(2,1)S(1)}, bf16[256,1024]{1,0:T(8,128)(2,1)S(1)}, bf16[256,1024]{1,0:T(8,128)(2,1)S(1)}, bf16[256,1024]{1,0:T(8,128)(2,1)S(1)}, f32[16,128]{1,0:T(8,128)S(1)}) custom-call(s32[1]{0:T(128)} %bitcast.10.part_ref, bf16[8,272,128]{2,1,0:T(8,128)(2,1)S(1)} %all-to-all-done.2.rows_ref, bf16[4096,1024]{1,0:T(8,128)(2,1)S(1)} %copy-done.3), custom_call_target="tpu_custom_call" | custom-call | flops 2147483648 | bytes 8388608 | tf_op jit(solution)/shard_map/project/pallas_call | solution.py:449
  129.7 3.5 %collective-permute-done.2.other_ref = bf16[8,2,256,128]{3,2,1,0:T(8,128)(2,1)S(1)} collective-permute-done((bf16[8,2,256,128]{3,2,1,0:T(8,128)(2,1)}, bf16[8,2,256,128]{3,2,1,0:T(8,128)(2,1)S(1)}, u32[]{:S(2)}, u32[]{:S(2)}) %collective-permute-start.2) | collective-permute-done | bytes 1048608 | tf_op jit(solution)/shard_map/ppermute | solution.py:468
  133.2 2.7 %finish.1 = bf16[8,512,128]{2,1,0:T(8,128)(2,1)} custom-call(bf16[8,2,256,128]{3,2,1,0:T(8,128)(2,1)S(1)} %copy-done.4, bf16[8,2,256,128]{3,2,1,0:T(8,128)(2,1)S(1)} %collective-permute-done.2.other_ref, bf16[8,2,256,128]{3,2,1,0:T(8,128)(2,1)S(1)} %copy-done.2, f32[1,128]{1,0:T(1,128)S(1)} %copy-done.5), custom_call_target="tpu_custom_call" | custom-call | bytes 8388608 | tf_op jit(solution)/shard_map/finish/pallas_call | solution.py:414
  135.9 7.2 %all-to-all-start.3 = ((bf16[8,512,128]{2,1,0:T(8,128)(2,1)}), bf16[8,512,128]{2,1,0:T(8,128)(2,1)S(1)}, u32[]{:S(2)}, u32[]{:S(2)}) async-start(bf16[8,512,128]{2,1,0:T(8,128)(2,1)} %finish.1), calls=%async_computation.3 | async-start | bytes 2097152 | tf_op jit(solution)/shard_map/all_to_all | solution.py:464
  143.1 1.6 collective-permute-start.3
  144.7 2.9 %collective-permute-start.4 = (bf16[256,1024]{1,0:T(8,128)(2,1)}, bf16[256,1024]{1,0:T(8,128)(2,1)S(1)}, u32[]{:S(2)}, u32[]{:S(2)}) collective-permute-start(bf16[256,1024]{1,0:T(8,128)(2,1)} %copy-done.7), channel_id=1, source_target_pairs={{0,8},{4,12},{8,0},{12,4},{1,9},{5,13},{9,1},{13,5},{2,10},{6,14},... | collective-permute-start | bytes 1572872 | tf_op jit(solution)/shard_map/ppermute | solution.py:476
  147.6 1.3 collective-permute-start.5
  150.3 1.5 collective-permute-start.6
  152.0 1.9 %collective-permute-done.6 = f32[16,128]{1,0:T(8,128)S(1)} collective-permute-done((f32[16,128]{1,0:T(8,128)S(1)}, f32[16,128]{1,0:T(8,128)S(1)}, u32[]{:S(2)}, u32[]{:S(2)}) %collective-permute-start.6) | collective-permute-done | bytes 8224 | tf_op jit(solution)/shard_map/ppermute | solution.py:482
  153.9 3.1 %collective-permute-start.9 = (f32[16,128]{1,0:T(8,128)S(1)}, f32[16,128]{1,0:T(8,128)S(1)}, u32[]{:S(2)}, u32[]{:S(2)}) collective-permute-start(f32[16,128]{1,0:T(8,128)S(1)} %add_add_fusion), channel_id=1, source_target_pairs={{0,16},{16,0},{32,48},{48,32},{64,80},{80,64},{96,112},{112,96},{1... | collective-permute-start | bytes 24584 | tf_op jit(solution)/shard_map/ppermute | solution.py:468
  157.0 2.1 %collective-permute-done.9 = f32[16,128]{1,0:T(8,128)S(1)} collective-permute-done((f32[16,128]{1,0:T(8,128)S(1)}, f32[16,128]{1,0:T(8,128)S(1)}, u32[]{:S(2)}, u32[]{:S(2)}) %collective-permute-start.9) | collective-permute-done | bytes 8224 | tf_op jit(solution)/shard_map/ppermute | solution.py:468
  159.7 7.0 %collective-permute-done.4 = bf16[256,1024]{1,0:T(8,128)(2,1)S(1)} collective-permute-done((bf16[256,1024]{1,0:T(8,128)(2,1)}, bf16[256,1024]{1,0:T(8,128)(2,1)S(1)}, u32[]{:S(2)}, u32[]{:S(2)}) %collective-permute-start.4) | collective-permute-done | bytes 524320 | tf_op jit(solution)/shard_map/ppermute | solution.py:476
  166.7 1.2 fusion
  167.9 2.5 %unpack.1 = (bf16[256,1024]{1,0:T(8,128)(2,1)}, bf16[256,1024]{1,0:T(8,128)(2,1)}) custom-call(bf16[8,512,128]{2,1,0:T(8,128)(2,1)S(1)} %all-to-all-done.3.pieces_ref), custom_call_target="tpu_custom_call" | custom-call | bytes 4194304 | tf_op jit(solution)/shard_map/unpack/pallas_call | solution.py:122
  (54 shorter events, 5.8 us)
Async XLA Ops:
  0.6 47.0 %copy-start = (f32[8,128]{1,0:T(8,128)S(1)}, f32[8,128]{1,0:T(8,128)}, u32[]{:S(2)}) copy-start(f32[8,128]{1,0:T(8,128)} %param.13) | copy-start | bytes 12292
  0.6 47.5 %copy-start.14 = (s32[1,8]{1,0:T(1,128)S(1)}, s32[1,8]{1,0:T(1,128)}, u32[]{:S(2)}) copy-start(s32[1,8]{1,0:T(1,128)} %param.15) | copy-start | bytes 100
  2.8 35.9 %all-to-all-start = ((bf16[8,2,256,128]{3,2,1,0:T(8,128)(2,1)}), bf16[8,2,256,128]{3,2,1,0:T(8,128)(2,1)S(1)}, u32[]{:S(2)}, u32[]{:S(2)}) async-start(bf16[8,2,256,128]{3,2,1,0:T(8,128)(2,1)} %pack.3), calls=%async_computation | async-start | bytes 2097152 | tf_op jit(solution)/shard_map/all_to_all | solution.py:464
  38.7 9.5 %copy-start.1 = (bf16[8,2,256,128]{3,2,1,0:T(8,128)(2,1)}, bf16[8,2,256,128]{3,2,1,0:T(8,128)(2,1)S(1)}, u32[]{:S(2)}) copy-start(bf16[8,2,256,128]{3,2,1,0:T(8,128)(2,1)S(1)} %all-to-all-done.raw_ref.refs_5_) | copy-start | bytes 3145732
  38.7 35.4 %all-to-all-start.1 = ((bf16[8,2,256,128]{3,2,1,0:T(8,128)(2,1)}), bf16[8,2,256,128]{3,2,1,0:T(8,128)(2,1)S(1)}, u32[]{:S(2)}, u32[]{:S(2)}) async-start(bf16[8,2,256,128]{3,2,1,0:T(8,128)(2,1)} %pack.2), calls=%async_computation.1 | async-start | bytes 2097152 | tf_op jit(solution)/shard_map/all_to_all | solution.py:464
  44.6 15.3 %collective-permute-start = (bf16[8,256,128]{2,1,0:T(8,128)(2,1)}, bf16[8,256,128]{2,1,0:T(8,128)(2,1)S(1)}, u32[]{:S(2)}, u32[]{:S(2)}) collective-permute-start(bf16[8,256,128]{2,1,0:T(8,128)(2,1)} %get-tuple-element.62), channel_id=1, source_target_pairs={{0,16},{16,0},{32,48},{48,32},{64,80},{80,64},{96,112},{112,96},{1... | collective-permute-start | bytes 1572872 | tf_op jit(solution)/shard_map/ppermute | solution.py:468
  48.2 25.9 %copy-start.11 = (s32[4,512]{1,0:T(4,128)}, s32[4,512]{1,0:T(4,128)S(1)}, u32[]{:S(2)}) copy-start(s32[4,512]{1,0:T(4,128)S(1)} %get-tuple-element.67.pos_ref) | copy-start | bytes 24580
  59.9 5.1 %copy-start.10 = (bf16[8,256,128]{2,1,0:T(8,128)(2,1)}, bf16[8,256,128]{2,1,0:T(8,128)(2,1)S(1)}, u32[]{:S(2)}) copy-start(bf16[8,256,128]{2,1,0:T(8,128)(2,1)S(1)} %collective-permute-done.raw_ref) | copy-start | bytes 1572868
  59.9 14.2 %collective-permute-start.1 = (bf16[8,256,128]{2,1,0:T(8,128)(2,1)S(1)}, bf16[8,256,128]{2,1,0:T(8,128)(2,1)S(1)}, u32[]{:S(2)}, u32[]{:S(2)}) collective-permute-start(bf16[8,256,128]{2,1,0:T(8,128)(2,1)S(1)} %get-tuple-element.41), channel_id=1, source_target_pairs={{0,16},{16,0},{32,48},{48,32},{64,80},{80,64},{96,112},{112,96},{1... | collective-permute-start | bytes 1572872 | tf_op jit(solution)/shard_map/ppermute | solution.py:468
  64.2 9.8 %copy-start.12 = (s32[4,512]{1,0:T(4,128)}, s32[4,512]{1,0:T(4,128)S(1)}, u32[]{:S(2)}) copy-start(s32[4,512]{1,0:T(4,128)S(1)} %select_reduce_fusion.low_ref) | copy-start | bytes 24580
  74.0 0.8 copy-start.13
  74.1 1.2 copy-start.9
  101.6 31.5 %copy-start.2 = (bf16[8,2,256,128]{3,2,1,0:T(8,128)(2,1)S(1)}, bf16[8,2,256,128]{3,2,1,0:T(8,128)(2,1)}, u32[]{:S(2)}) copy-start(bf16[8,2,256,128]{3,2,1,0:T(8,128)(2,1)} %copy-done.1) | copy-start | bytes 3145732
  101.6 31.5 %copy-start.5 = (f32[1,128]{1,0:T(1,128)S(1)}, f32[1,128]{1,0:T(1,128)}, u32[]{:S(2)}) copy-start(f32[1,128]{1,0:T(1,128)} %constant_dynamic-slice_fusion.gain_ref.key_gain_ref) | copy-start | bytes 1540
  101.6 22.2 %all-to-all-start.2 = ((bf16[8,272,128]{2,1,0:T(8,128)(2,1)}), bf16[8,272,128]{2,1,0:T(8,128)(2,1)S(1)}, u32[]{:S(2)}, u32[]{:S(2)}) async-start(bf16[8,272,128]{2,1,0:T(8,128)(2,1)} %get-tuple-element.43), calls=%async_computation.2 | async-start | bytes 1114112 | tf_op jit(solution)/shard_map/all_to_all | solution.py:464
  109.0 24.1 %collective-permute-start.2 = (bf16[8,2,256,128]{3,2,1,0:T(8,128)(2,1)}, bf16[8,2,256,128]{3,2,1,0:T(8,128)(2,1)S(1)}, u32[]{:S(2)}, u32[]{:S(2)}) collective-permute-start(bf16[8,2,256,128]{3,2,1,0:T(8,128)(2,1)} %get-tuple-element.42), channel_id=1, source_target_pairs={{0,16},{16,0},{32,48},{48,32},{64,80},{80,64},{96,112},{112,96},{1... | collective-permute-start | bytes 3145736 | tf_op jit(solution)/shard_map/ppermute | solution.py:468
  123.8 3.4 %copy-start.3 = (bf16[4096,1024]{1,0:T(8,128)(2,1)S(1)}, bf16[4096,1024]{1,0:T(8,128)(2,1)}, u32[]{:S(2)}) copy-start(bf16[4096,1024]{1,0:T(8,128)(2,1)} %weight_ref.1) | copy-start | bytes 25165828
  127.2 5.9 %copy-start.4 = (bf16[8,2,256,128]{3,2,1,0:T(8,128)(2,1)S(1)}, bf16[8,2,256,128]{3,2,1,0:T(8,128)(2,1)}, u32[]{:S(2)}) copy-start(bf16[8,2,256,128]{3,2,1,0:T(8,128)(2,1)} %get-tuple-element.53.own_ref) | copy-start | bytes 3145732
  129.6 6.2 %copy-start.6 = (bf16[256,1024]{1,0:T(8,128)(2,1)}, bf16[256,1024]{1,0:T(8,128)(2,1)S(1)}, u32[]{:S(2)}) copy-start(bf16[256,1024]{1,0:T(8,128)(2,1)S(1)} %get-tuple-element.51) | copy-start | bytes 1572868
  129.6 6.2 %copy-start.7 = (bf16[256,1024]{1,0:T(8,128)(2,1)}, bf16[256,1024]{1,0:T(8,128)(2,1)S(1)}, u32[]{:S(2)}) copy-start(bf16[256,1024]{1,0:T(8,128)(2,1)S(1)} %get-tuple-element.50) | copy-start | bytes 1572868
  129.7 6.2 %copy-start.8 = (bf16[256,1024]{1,0:T(8,128)(2,1)}, bf16[256,1024]{1,0:T(8,128)(2,1)S(1)}, u32[]{:S(2)}) copy-start(bf16[256,1024]{1,0:T(8,128)(2,1)S(1)} %get-tuple-element.49) | copy-start | bytes 1572868
  135.9 32.0 %all-to-all-start.3 = ((bf16[8,512,128]{2,1,0:T(8,128)(2,1)}), bf16[8,512,128]{2,1,0:T(8,128)(2,1)S(1)}, u32[]{:S(2)}, u32[]{:S(2)}) async-start(bf16[8,512,128]{2,1,0:T(8,128)(2,1)} %finish.1), calls=%async_computation.3 | async-start | bytes 2097152 | tf_op jit(solution)/shard_map/all_to_all | solution.py:464
  143.1 16.6 %collective-permute-start.3 = (bf16[256,1024]{1,0:T(8,128)(2,1)}, bf16[256,1024]{1,0:T(8,128)(2,1)S(1)}, u32[]{:S(2)}, u32[]{:S(2)}) collective-permute-start(bf16[256,1024]{1,0:T(8,128)(2,1)} %copy-done.8), channel_id=1, source_target_pairs={{0,4},{4,8},{8,12},{12,0},{1,5},{5,9},{9,13},{13,1},{2,6},{6,10},{... | collective-permute-start | bytes 1572872 | tf_op jit(solution)/shard_map/ppermute | solution.py:476
  144.7 22.0 %collective-permute-start.4 = (bf16[256,1024]{1,0:T(8,128)(2,1)}, bf16[256,1024]{1,0:T(8,128)(2,1)S(1)}, u32[]{:S(2)}, u32[]{:S(2)}) collective-permute-start(bf16[256,1024]{1,0:T(8,128)(2,1)} %copy-done.7), channel_id=1, source_target_pairs={{0,8},{4,12},{8,0},{12,4},{1,9},{5,13},{9,1},{13,5},{2,10},{6,14},... | collective-permute-start | bytes 1572872 | tf_op jit(solution)/shard_map/ppermute | solution.py:476
  147.6 19.1 %collective-permute-start.5 = (bf16[256,1024]{1,0:T(8,128)(2,1)}, bf16[256,1024]{1,0:T(8,128)(2,1)S(1)}, u32[]{:S(2)}, u32[]{:S(2)}) collective-permute-start(bf16[256,1024]{1,0:T(8,128)(2,1)} %copy-done.6), channel_id=1, source_target_pairs={{0,12},{4,0},{8,4},{12,8},{1,13},{5,1},{9,5},{13,9},{2,14},{6,2},{... | collective-permute-start | bytes 1572872 | tf_op jit(solution)/shard_map/ppermute | solution.py:476
  148.9 1.4 collective-permute-start.8
  148.9 3.1 %collective-permute-start.7 = (f32[16,128]{1,0:T(8,128)S(1)}, f32[16,128]{1,0:T(8,128)S(1)}, u32[]{:S(2)}, u32[]{:S(2)}) collective-permute-start(f32[16,128]{1,0:T(8,128)S(1)} %get-tuple-element.58), channel_id=1, source_target_pairs={{0,1},{1,2},{2,3},{3,0},{4,5},{5,6},{6,7},{7,4},{8,9},{9,10},{10,1... | collective-permute-start | bytes 24584 | tf_op jit(solution)/shard_map/ppermute | solution.py:482
  150.3 3.7 %collective-permute-start.6 = (f32[16,128]{1,0:T(8,128)S(1)}, f32[16,128]{1,0:T(8,128)S(1)}, u32[]{:S(2)}, u32[]{:S(2)}) collective-permute-start(f32[16,128]{1,0:T(8,128)S(1)} %get-tuple-element.58), channel_id=1, source_target_pairs={{0,2},{1,3},{2,0},{3,1},{4,6},{5,7},{6,4},{7,5},{8,10},{9,11},{10,... | collective-permute-start | bytes 24584 | tf_op jit(solution)/shard_map/ppermute | solution.py:482
  153.9 5.2 %collective-permute-start.9 = (f32[16,128]{1,0:T(8,128)S(1)}, f32[16,128]{1,0:T(8,128)S(1)}, u32[]{:S(2)}, u32[]{:S(2)}) collective-permute-start(f32[16,128]{1,0:T(8,128)S(1)} %add_add_fusion), channel_id=1, source_target_pairs={{0,16},{16,0},{32,48},{48,32},{64,80},{80,64},{96,112},{112,96},{1... | collective-permute-start | bytes 24584 | tf_op jit(solution)/shard_map/ppermute | solution.py:468

commit v6 on v5

--- a/solution.py
+++ b/solution.py
@@ -228,6 +228,12 @@
             pltpu.make_async_copy(source, target, in_sem.at[step, index])
             for index, (source, target) in enumerate(moves)
         ]
+
+    def dq_copy(block):
+        shards = pl.ds(block * PAIRS, PAIRS)
+        return pltpu.make_async_copy(
+            held_dq.at[shards, :ROWS], dq_ref.at[shards, :ROWS], dq_sem.at[block]
+        )
 
     for step in range(DEPTH // PAIRS):
         for copy in loads(step):
@@ -312,10 +318,24 @@
         for pair, shard in enumerate(shards):
             rows = slice(pair * ROWS, (pair + 1) * ROWS)
             held_dq[shard, :ROWS] = raw_grad[rows].astype(jnp.bfloat16)
+        dq_copy(block).start()
         gain_grad_ref[...] += jnp.sum(query_grad * unit_rows, axis=0, keepdims=True)
         return carry
 
     lax.fori_loop(0, DEPTH // PAIRS, block_body, 0)
+    copies = []
+    for tile in range(DEPTH):
+        step, base = tile // PAIRS, tile % PAIRS * 2 * ROWS
+        for side, out_ref in enumerate((own_ref, other_ref)):
+            rows = slice(base + side * ROWS, base + (side + 1) * ROWS)
+            cast_ref[side, tile, 0] = dv_ref[step, rows].astype(jnp.bfloat16)
+            cast_ref[side, tile, 1] = dk_ref[step, rows].astype(jnp.bfloat16)
+            copies.append(
+                pltpu.make_async_copy(
+                    cast_ref.at[side, tile], out_ref.at[tile], out_sem.at[side, tile]
+                )
+            )
+            copies[-1].start()
     key_total = jnp.zeros((ROWS, HD), jnp.float32)
     for tile in range(DEPTH):
         for side in range(2):
@@ -332,20 +352,14 @@
             rest = rest - term
     for tile in range(DEPTH):
         held_dq[tile, ROWS:] = extra.astype(jnp.bfloat16)
-    copies = [pltpu.make_async_copy(held_dq, dq_ref, dq_sem.at[0])]
-    copies[0].start()
-    for tile in range(DEPTH):
-        step, base = tile // PAIRS, tile % PAIRS * 2 * ROWS
-        for side, out_ref in enumerate((own_ref, other_ref)):
-            rows = slice(base + side * ROWS, base + (side + 1) * ROWS)
-            cast_ref[side, tile, 0] = dv_ref[step, rows].astype(jnp.bfloat16)
-            cast_ref[side, tile, 1] = dk_ref[step, rows].astype(jnp.bfloat16)
-            copies.append(
-                pltpu.make_async_copy(
-                    cast_ref.at[side, tile], out_ref.at[tile], out_sem.at[side, tile]
-                )
-            )
-            copies[-1].start()
+    copies.append(
+        pltpu.make_async_copy(
+            held_dq.at[:, ROWS:], dq_ref.at[:, ROWS:], dq_sem.at[DEPTH // PAIRS]
+        )
+    )
+    copies[-1].start()
+    for block in range(DEPTH // PAIRS):
+        dq_copy(block).wait()
     for copy in copies:
         copy.wait()
 
@@ -377,7 +391,7 @@
             pltpu.VMEM((2, DEPTH, 2, ROWS, HD), jnp.bfloat16),
             pltpu.VMEM((1, HD), jnp.float32),
             pltpu.SemaphoreType.DMA((steps, 7)),
-            pltpu.SemaphoreType.DMA((1,)),
+            pltpu.SemaphoreType.DMA((DEPTH // PAIRS + 1,)),
             pltpu.SemaphoreType.DMA((2, DEPTH)),
         ],
         compiler_params=pltpu.CompilerParams(vmem_limit_bytes=VMEM_LIMIT),

time: 172 us -> 171 us (level)
  no operation moved by 1% of the time
where the time goes in v6:
time: 171 us; the launch traced here: 170 us
  waiting for transfers between devices  63.3 us (37%)
  starting transfers between devices  48 us (28%)
  Pallas kernels  47.2 us (28%)
  local copies, waits for them, and re-layouts  7.91 us (5%)
  other arithmetic  2.85 us (2%)
    all_to_all x4, waiting for transfers between devices, along_z(): return lax.all_to_all(pieces, 'ctx', 0, 0, axis_index_groups=Z_GROUPS)  36.1 us
    all_to_all x4, starting transfers between devices, along_z(): return lax.all_to_all(pieces, 'ctx', 0, 0, axis_index_groups=Z_GROUPS)  28.1 us
    pallas_call x1, Pallas kernels, attention(): pl.pallas_call(attention_kernel, in_specs=[SMEM_SPEC, SMEM_SPEC] + [VMEM_...  26.1 us
    ppermute x4, waiting for transfers between devices, swap_half(): return lax.ppermute(piece, 'ctx', HALF_SWAP)  17.2 us
    ppermute x4, starting transfers between devices, swap_half(): return lax.ppermute(piece, 'ctx', HALF_SWAP)  12.1 us
    pallas_call x2, Pallas kernels, key_prep(): pl.pallas_call(functools.partial(key_prep_kernel, paired), in_specs=[VMEM...  9.21 us
    ppermute x3, waiting for transfers between devices, sum_tp(): total = total + lax.ppermute(parts[step], 'tp', pairs).astype(jnp.float32)  6.99 us
    ppermute x3, starting transfers between devices, sum_tp(): total = total + lax.ppermute(parts[step], 'tp', pairs).astype(jnp.float32)  5.83 us
  transfers between devices with their start and end apart: 14, of which 10 were waited for; matrix products, arithmetic and copies ran while one was open for 4% of the time, Pallas kernels for 8%

profile of v6, /device:TPU:32, one launch (start us, length us, event | category | flops | bytes accessed | tf_op | source)
XLA Modules:
  0.0 170.2 jit_solution(3604101464585661334)
XLA Ops:
  0.7 2.2 %pack.3 = bf16[8,2,256,128]{3,2,1,0:T(8,128)(2,1)} custom-call(bf16[256,1024]{1,0:T(8,128)(2,1)} %bitcast.29, bf16[256,1024]{1,0:T(8,128)(2,1)} %bitcast.30), custom_call_target="tpu_custom_call" | custom-call | bytes 4194304 | tf_op jit(solution)/shard_map/pack/pallas_call | solution.py:81
  2.8 8.6 %all-to-all-start = ((bf16[8,2,256,128]{3,2,1,0:T(8,128)(2,1)}), bf16[8,2,256,128]{3,2,1,0:T(8,128)(2,1)S(1)}, u32[]{:S(2)}, u32[]{:S(2)}) async-start(bf16[8,2,256,128]{3,2,1,0:T(8,128)(2,1)} %pack.3), calls=%async_computation | async-start | bytes 2097152 | tf_op jit(solution)/shard_map/all_to_all | solution.py:478
  12.2 2.1 %pack.2 = bf16[8,2,256,128]{3,2,1,0:T(8,128)(2,1)} custom-call(bf16[256,1024]{1,0:T(8,128)(2,1)} %bitcast.31, bf16[256,1024]{1,0:T(8,128)(2,1)} %bitcast.32), custom_call_target="tpu_custom_call" | custom-call | bytes 4194304 | tf_op jit(solution)/shard_map/pack/pallas_call | solution.py:81
  14.4 24.3 %all-to-all-done.raw_ref.refs_5_ = bf16[8,2,256,128]{3,2,1,0:T(8,128)(2,1)S(1)} async-done(((bf16[8,2,256,128]{3,2,1,0:T(8,128)(2,1)}), bf16[8,2,256,128]{3,2,1,0:T(8,128)(2,1)S(1)}, u32[]{:S(2)}, u32[]{:S(2)}) %all-to-all-start) | async-done | bytes 1048608 | tf_op jit(solution)/shard_map/all_to_all | solution.py:478
  38.7 4.9 %all-to-all-start.1 = ((bf16[8,2,256,128]{3,2,1,0:T(8,128)(2,1)}), bf16[8,2,256,128]{3,2,1,0:T(8,128)(2,1)S(1)}, u32[]{:S(2)}, u32[]{:S(2)}) async-start(bf16[8,2,256,128]{3,2,1,0:T(8,128)(2,1)} %pack.2), calls=%async_computation.1 | async-start | bytes 2097152 | tf_op jit(solution)/shard_map/all_to_all | solution.py:478
  43.7 0.9 slice_bitcast_fusion
  44.6 3.0 %collective-permute-start = (bf16[8,256,128]{2,1,0:T(8,128)(2,1)}, bf16[8,256,128]{2,1,0:T(8,128)(2,1)S(1)}, u32[]{:S(2)}, u32[]{:S(2)}) collective-permute-start(bf16[8,256,128]{2,1,0:T(8,128)(2,1)} %get-tuple-element.62), channel_id=1, source_target_pairs={{0,16},{16,0},{32,48},{48,32},{64,80},{80,64},{96,112},{112,96},{1... | collective-permute-start | bytes 1572872 | tf_op jit(solution)/shard_map/ppermute | solution.py:482
  48.2 4.6 %key_prep.2 = (bf16[8,256,128]{2,1,0:T(8,128)(2,1)}, bf16[8,128,256]{2,1,0:T(8,128)(2,1)}) custom-call(f32[1,128]{1,0:T(1,128)} %constant_dynamic-slice_fusion.gain_ref.key_gain_ref, bf16[8,2,256,128]{3,2,1,0:T(8,128)(2,1)} %copy-done.1), custom_call_target="tpu_custom_call" | custom-call | bytes 4194304 | tf_op jit(solution)/shard_map/key_prep/pallas_call | solution.py:172
  52.8 7.1 %collective-permute-done.raw_ref = bf16[8,256,128]{2,1,0:T(8,128)(2,1)S(1)} collective-permute-done((bf16[8,256,128]{2,1,0:T(8,128)(2,1)}, bf16[8,256,128]{2,1,0:T(8,128)(2,1)S(1)}, u32[]{:S(2)}, u32[]{:S(2)}) %collective-permute-start) | collective-permute-done | bytes 524320 | tf_op jit(solution)/shard_map/ppermute | solution.py:482
  59.9 3.0 %collective-permute-start.1 = (bf16[8,256,128]{2,1,0:T(8,128)(2,1)S(1)}, bf16[8,256,128]{2,1,0:T(8,128)(2,1)S(1)}, u32[]{:S(2)}, u32[]{:S(2)}) collective-permute-start(bf16[8,256,128]{2,1,0:T(8,128)(2,1)S(1)} %get-tuple-element.41), channel_id=1, source_target_pairs={{0,16},{16,0},{32,48},{48,32},{64,80},{80,64},{96,112},{112,96},{1... | collective-permute-start | bytes 1572872 | tf_op jit(solution)/shard_map/ppermute | solution.py:482
  62.9 1.2 constant_dynamic-slice_fusion.1.gain_ref
  65.0 4.6 %key_prep.3 = (bf16[8,256,128]{2,1,0:T(8,128)(2,1)}, bf16[8,128,256]{2,1,0:T(8,128)(2,1)}) custom-call(f32[1,128]{1,0:T(1,128)} %constant_dynamic-slice_fusion.gain_ref.key_gain_ref, bf16[8,256,128]{2,1,0:T(8,128)(2,1)} %copy-done.10), custom_call_target="tpu_custom_call" | custom-call | bytes 4194304 | tf_op jit(solution)/shard_map/key_prep/pallas_call | solution.py:172
  69.6 4.4 %collective-permute-done.1.refs_6_ = bf16[8,256,128]{2,1,0:T(8,128)(2,1)S(1)} collective-permute-done((bf16[8,256,128]{2,1,0:T(8,128)(2,1)S(1)}, bf16[8,256,128]{2,1,0:T(8,128)(2,1)S(1)}, u32[]{:S(2)}, u32[]{:S(2)}) %collective-permute-start.1) | collective-permute-done | bytes 524320 | tf_op jit(solution)/shard_map/ppermute | solution.py:482
  75.2 26.1 %attention.1 = (bf16[8,272,128]{2,1,0:T(8,128)(2,1)}, bf16[8,2,256,128]{3,2,1,0:T(8,128)(2,1)}, bf16[8,2,256,128]{3,2,1,0:T(8,128)(2,1)}) custom-call(s32[4,4]{1,0:T(4,128)} %pad_add_fusion.bounds_ref, s32[1]{0:T(128)} %bitcast.3.half_ref, s32[4,512]{1,0:T(4,128)} %copy-done.11, s32[4,512]{1,0:T(4,128)} %copy-done.12, ...), custom_call_target="tpu_custom_call" | custom-call | flops 12884901888 | bytes 8388608 | tf_op jit(solution)/shard_map/attention/pallas_call | solution.py:374
  101.3 7.4 %all-to-all-start.2 = ((bf16[8,272,128]{2,1,0:T(8,128)(2,1)}), bf16[8,272,128]{2,1,0:T(8,128)(2,1)S(1)}, u32[]{:S(2)}, u32[]{:S(2)}) async-start(bf16[8,272,128]{2,1,0:T(8,128)(2,1)} %get-tuple-element.43), calls=%async_computation.2 | async-start | bytes 1114112 | tf_op jit(solution)/shard_map/all_to_all | solution.py:478
  108.7 3.0 %collective-permute-start.2 = (bf16[8,2,256,128]{3,2,1,0:T(8,128)(2,1)}, bf16[8,2,256,128]{3,2,1,0:T(8,128)(2,1)S(1)}, u32[]{:S(2)}, u32[]{:S(2)}) collective-permute-start(bf16[8,2,256,128]{3,2,1,0:T(8,128)(2,1)} %get-tuple-element.42), channel_id=1, source_target_pairs={{0,16},{16,0},{32,48},{48,32},{64,80},{80,64},{96,112},{112,96},{1... | collective-permute-start | bytes 3145736 | tf_op jit(solution)/shard_map/ppermute | solution.py:482
  111.7 11.8 %all-to-all-done.2.rows_ref = bf16[8,272,128]{2,1,0:T(8,128)(2,1)S(1)} async-done(((bf16[8,272,128]{2,1,0:T(8,128)(2,1)}), bf16[8,272,128]{2,1,0:T(8,128)(2,1)S(1)}, u32[]{:S(2)}, u32[]{:S(2)}) %all-to-all-start.2) | async-done | bytes 557088 | tf_op jit(solution)/shard_map/all_to_all | solution.py:478
  123.5 3.4 %copy-done.3 = bf16[4096,1024]{1,0:T(8,128)(2,1)S(1)} copy-done((bf16[4096,1024]{1,0:T(8,128)(2,1)S(1)}, bf16[4096,1024]{1,0:T(8,128)(2,1)}, u32[]{:S(2)}) %copy-start.3) | copy-done | bytes 8388632
  126.9 2.4 %project.1 = (bf16[256,1024]{1,0:T(8,128)(2,1)S(1)}, bf16[256,1024]{1,0:T(8,128)(2,1)S(1)}, bf16[256,1024]{1,0:T(8,128)(2,1)S(1)}, bf16[256,1024]{1,0:T(8,128)(2,1)S(1)}, f32[16,128]{1,0:T(8,128)S(1)}) custom-call(s32[1]{0:T(128)} %bitcast.10.part_ref, bf16[8,272,128]{2,1,0:T(8,128)(2,1)S(1)} %all-to-all-done.2.rows_ref, bf16[4096,1024]{1,0:T(8,128)(2,1)S(1)} %copy-done.3), custom_call_target="tpu_custom_call" | custom-call | flops 2147483648 | bytes 8388608 | tf_op jit(solution)/shard_map/project/pallas_call | solution.py:463
  129.4 3.5 %collective-permute-done.2.other_ref = bf16[8,2,256,128]{3,2,1,0:T(8,128)(2,1)S(1)} collective-permute-done((bf16[8,2,256,128]{3,2,1,0:T(8,128)(2,1)}, bf16[8,2,256,128]{3,2,1,0:T(8,128)(2,1)S(1)}, u32[]{:S(2)}, u32[]{:S(2)}) %collective-permute-start.2) | collective-permute-done | bytes 1048608 | tf_op jit(solution)/shard_map/ppermute | solution.py:482
  132.9 2.7 %finish.1 = bf16[8,512,128]{2,1,0:T(8,128)(2,1)} custom-call(bf16[8,2,256,128]{3,2,1,0:T(8,128)(2,1)S(1)} %copy-done.4, bf16[8,2,256,128]{3,2,1,0:T(8,128)(2,1)S(1)} %collective-permute-done.2.other_ref, bf16[8,2,256,128]{3,2,1,0:T(8,128)(2,1)S(1)} %copy-done.2, f32[1,128]{1,0:T(1,128)S(1)} %copy-done.5), custom_call_target="tpu_custom_call" | custom-call | bytes 8388608 | tf_op jit(solution)/shard_map/finish/pallas_call | solution.py:428
  135.6 7.2 %all-to-all-start.3 = ((bf16[8,512,128]{2,1,0:T(8,128)(2,1)}), bf16[8,512,128]{2,1,0:T(8,128)(2,1)S(1)}, u32[]{:S(2)}, u32[]{:S(2)}) async-start(bf16[8,512,128]{2,1,0:T(8,128)(2,1)} %finish.1), calls=%async_computation.3 | async-start | bytes 2097152 | tf_op jit(solution)/shard_map/all_to_all | solution.py:478
  142.8 1.6 collective-permute-start.3
  144.4 2.9 %collective-permute-start.4 = (bf16[256,1024]{1,0:T(8,128)(2,1)}, bf16[256,1024]{1,0:T(8,128)(2,1)S(1)}, u32[]{:S(2)}, u32[]{:S(2)}) collective-permute-start(bf16[256,1024]{1,0:T(8,128)(2,1)} %copy-done.7), channel_id=1, source_target_pairs={{0,8},{4,12},{8,0},{12,4},{1,9},{5,13},{9,1},{13,5},{2,10},{6,14},... | collective-permute-start | bytes 1572872 | tf_op jit(solution)/shard_map/ppermute | solution.py:490
  147.3 1.3 collective-permute-start.5
  150.0 1.5 collective-permute-start.6
  151.7 1.9 %collective-permute-done.6 = f32[16,128]{1,0:T(8,128)S(1)} collective-permute-done((f32[16,128]{1,0:T(8,128)S(1)}, f32[16,128]{1,0:T(8,128)S(1)}, u32[]{:S(2)}, u32[]{:S(2)}) %collective-permute-start.6) | collective-permute-done | bytes 8224 | tf_op jit(solution)/shard_map/ppermute | solution.py:496
  153.6 3.0 %collective-permute-start.9 = (f32[16,128]{1,0:T(8,128)S(1)}, f32[16,128]{1,0:T(8,128)S(1)}, u32[]{:S(2)}, u32[]{:S(2)}) collective-permute-start(f32[16,128]{1,0:T(8,128)S(1)} %add_add_fusion), channel_id=1, source_target_pairs={{0,16},{16,0},{32,48},{48,32},{64,80},{80,64},{96,112},{112,96},{1... | collective-permute-start | bytes 24584 | tf_op jit(solution)/shard_map/ppermute | solution.py:482
  156.7 2.1 %collective-permute-done.9 = f32[16,128]{1,0:T(8,128)S(1)} collective-permute-done((f32[16,128]{1,0:T(8,128)S(1)}, f32[16,128]{1,0:T(8,128)S(1)}, u32[]{:S(2)}, u32[]{:S(2)}) %collective-permute-start.9) | collective-permute-done | bytes 8224 | tf_op jit(solution)/shard_map/ppermute | solution.py:482
  159.4 7.0 %collective-permute-done.4 = bf16[256,1024]{1,0:T(8,128)(2,1)S(1)} collective-permute-done((bf16[256,1024]{1,0:T(8,128)(2,1)}, bf16[256,1024]{1,0:T(8,128)(2,1)S(1)}, u32[]{:S(2)}, u32[]{:S(2)}) %collective-permute-start.4) | collective-permute-done | bytes 524320 | tf_op jit(solution)/shard_map/ppermute | solution.py:490
  166.4 1.2 fusion
  167.6 2.5 %unpack.1 = (bf16[256,1024]{1,0:T(8,128)(2,1)}, bf16[256,1024]{1,0:T(8,128)(2,1)}) custom-call(bf16[8,512,128]{2,1,0:T(8,128)(2,1)S(1)} %all-to-all-done.3.pieces_ref), custom_call_target="tpu_custom_call" | custom-call | bytes 4194304 | tf_op jit(solution)/shard_map/unpack/pallas_call | solution.py:122
  (54 shorter events, 5.8 us)
Async XLA Ops:
  0.6 47.0 %copy-start = (f32[8,128]{1,0:T(8,128)S(1)}, f32[8,128]{1,0:T(8,128)}, u32[]{:S(2)}) copy-start(f32[8,128]{1,0:T(8,128)} %param.13) | copy-start | bytes 12292
  0.6 47.5 %copy-start.14 = (s32[1,8]{1,0:T(1,128)S(1)}, s32[1,8]{1,0:T(1,128)}, u32[]{:S(2)}) copy-start(s32[1,8]{1,0:T(1,128)} %param.15) | copy-start | bytes 100
  2.8 35.9 %all-to-all-start = ((bf16[8,2,256,128]{3,2,1,0:T(8,128)(2,1)}), bf16[8,2,256,128]{3,2,1,0:T(8,128)(2,1)S(1)}, u32[]{:S(2)}, u32[]{:S(2)}) async-start(bf16[8,2,256,128]{3,2,1,0:T(8,128)(2,1)} %pack.3), calls=%async_computation | async-start | bytes 2097152 | tf_op jit(solution)/shard_map/all_to_all | solution.py:478
  38.7 9.5 %copy-start.1 = (bf16[8,2,256,128]{3,2,1,0:T(8,128)(2,1)}, bf16[8,2,256,128]{3,2,1,0:T(8,128)(2,1)S(1)}, u32[]{:S(2)}) copy-start(bf16[8,2,256,128]{3,2,1,0:T(8,128)(2,1)S(1)} %all-to-all-done.raw_ref.refs_5_) | copy-start | bytes 3145732
  38.7 35.4 %all-to-all-start.1 = ((bf16[8,2,256,128]{3,2,1,0:T(8,128)(2,1)}), bf16[8,2,256,128]{3,2,1,0:T(8,128)(2,1)S(1)}, u32[]{:S(2)}, u32[]{:S(2)}) async-start(bf16[8,2,256,128]{3,2,1,0:T(8,128)(2,1)} %pack.2), calls=%async_computation.1 | async-start | bytes 2097152 | tf_op jit(solution)/shard_map/all_to_all | solution.py:478
  44.6 15.3 %collective-permute-start = (bf16[8,256,128]{2,1,0:T(8,128)(2,1)}, bf16[8,256,128]{2,1,0:T(8,128)(2,1)S(1)}, u32[]{:S(2)}, u32[]{:S(2)}) collective-permute-start(bf16[8,256,128]{2,1,0:T(8,128)(2,1)} %get-tuple-element.62), channel_id=1, source_target_pairs={{0,16},{16,0},{32,48},{48,32},{64,80},{80,64},{96,112},{112,96},{1... | collective-permute-start | bytes 1572872 | tf_op jit(solution)/shard_map/ppermute | solution.py:482
  48.2 25.9 %copy-start.11 = (s32[4,512]{1,0:T(4,128)}, s32[4,512]{1,0:T(4,128)S(1)}, u32[]{:S(2)}) copy-start(s32[4,512]{1,0:T(4,128)S(1)} %get-tuple-element.67.pos_ref) | copy-start | bytes 24580
  59.9 5.1 %copy-start.10 = (bf16[8,256,128]{2,1,0:T(8,128)(2,1)}, bf16[8,256,128]{2,1,0:T(8,128)(2,1)S(1)}, u32[]{:S(2)}) copy-start(bf16[8,256,128]{2,1,0:T(8,128)(2,1)S(1)} %collective-permute-done.raw_ref) | copy-start | bytes 1572868
  59.9 14.2 %collective-permute-start.1 = (bf16[8,256,128]{2,1,0:T(8,128)(2,1)S(1)}, bf16[8,256,128]{2,1,0:T(8,128)(2,1)S(1)}, u32[]{:S(2)}, u32[]{:S(2)}) collective-permute-start(bf16[8,256,128]{2,1,0:T(8,128)(2,1)S(1)} %get-tuple-element.41), channel_id=1, source_target_pairs={{0,16},{16,0},{32,48},{48,32},{64,80},{80,64},{96,112},{112,96},{1... | collective-permute-start | bytes 1572872 | tf_op jit(solution)/shard_map/ppermute | solution.py:482
  64.2 9.8 %copy-start.12 = (s32[4,512]{1,0:T(4,128)}, s32[4,512]{1,0:T(4,128)S(1)}, u32[]{:S(2)}) copy-start(s32[4,512]{1,0:T(4,128)S(1)} %select_reduce_fusion.low_ref) | copy-start | bytes 24580
  74.0 0.8 copy-start.13
  74.1 1.2 copy-start.9
  101.3 31.5 %copy-start.2 = (bf16[8,2,256,128]{3,2,1,0:T(8,128)(2,1)S(1)}, bf16[8,2,256,128]{3,2,1,0:T(8,128)(2,1)}, u32[]{:S(2)}) copy-start(bf16[8,2,256,128]{3,2,1,0:T(8,128)(2,1)} %copy-done.1) | copy-start | bytes 3145732
  101.3 31.5 %copy-start.5 = (f32[1,128]{1,0:T(1,128)S(1)}, f32[1,128]{1,0:T(1,128)}, u32[]{:S(2)}) copy-start(f32[1,128]{1,0:T(1,128)} %constant_dynamic-slice_fusion.gain_ref.key_gain_ref) | copy-start | bytes 1540
  101.3 22.2 %all-to-all-start.2 = ((bf16[8,272,128]{2,1,0:T(8,128)(2,1)}), bf16[8,272,128]{2,1,0:T(8,128)(2,1)S(1)}, u32[]{:S(2)}, u32[]{:S(2)}) async-start(bf16[8,272,128]{2,1,0:T(8,128)(2,1)} %get-tuple-element.43), calls=%async_computation.2 | async-start | bytes 1114112 | tf_op jit(solution)/shard_map/all_to_all | solution.py:478
  108.7 24.1 %collective-permute-start.2 = (bf16[8,2,256,128]{3,2,1,0:T(8,128)(2,1)}, bf16[8,2,256,128]{3,2,1,0:T(8,128)(2,1)S(1)}, u32[]{:S(2)}, u32[]{:S(2)}) collective-permute-start(bf16[8,2,256,128]{3,2,1,0:T(8,128)(2,1)} %get-tuple-element.42), channel_id=1, source_target_pairs={{0,16},{16,0},{32,48},{48,32},{64,80},{80,64},{96,112},{112,96},{1... | collective-permute-start | bytes 3145736 | tf_op jit(solution)/shard_map/ppermute | solution.py:482
  123.5 3.4 %copy-start.3 = (bf16[4096,1024]{1,0:T(8,128)(2,1)S(1)}, bf16[4096,1024]{1,0:T(8,128)(2,1)}, u32[]{:S(2)}) copy-start(bf16[4096,1024]{1,0:T(8,128)(2,1)} %weight_ref.1) | copy-start | bytes 25165828
  126.9 5.9 %copy-start.4 = (bf16[8,2,256,128]{3,2,1,0:T(8,128)(2,1)S(1)}, bf16[8,2,256,128]{3,2,1,0:T(8,128)(2,1)}, u32[]{:S(2)}) copy-start(bf16[8,2,256,128]{3,2,1,0:T(8,128)(2,1)} %get-tuple-element.53.own_ref) | copy-start | bytes 3145732
  129.3 6.2 %copy-start.6 = (bf16[256,1024]{1,0:T(8,128)(2,1)}, bf16[256,1024]{1,0:T(8,128)(2,1)S(1)}, u32[]{:S(2)}) copy-start(bf16[256,1024]{1,0:T(8,128)(2,1)S(1)} %get-tuple-element.51) | copy-start | bytes 1572868
  129.3 6.2 %copy-start.7 = (bf16[256,1024]{1,0:T(8,128)(2,1)}, bf16[256,1024]{1,0:T(8,128)(2,1)S(1)}, u32[]{:S(2)}) copy-start(bf16[256,1024]{1,0:T(8,128)(2,1)S(1)} %get-tuple-element.50) | copy-start | bytes 1572868
  129.4 6.2 %copy-start.8 = (bf16[256,1024]{1,0:T(8,128)(2,1)}, bf16[256,1024]{1,0:T(8,128)(2,1)S(1)}, u32[]{:S(2)}) copy-start(bf16[256,1024]{1,0:T(8,128)(2,1)S(1)} %get-tuple-element.49) | copy-start | bytes 1572868
  135.6 32.0 %all-to-all-start.3 = ((bf16[8,512,128]{2,1,0:T(8,128)(2,1)}), bf16[8,512,128]{2,1,0:T(8,128)(2,1)S(1)}, u32[]{:S(2)}, u32[]{:S(2)}) async-start(bf16[8,512,128]{2,1,0:T(8,128)(2,1)} %finish.1), calls=%async_computation.3 | async-start | bytes 2097152 | tf_op jit(solution)/shard_map/all_to_all | solution.py:478
  142.8 16.6 %collective-permute-start.3 = (bf16[256,1024]{1,0:T(8,128)(2,1)}, bf16[256,1024]{1,0:T(8,128)(2,1)S(1)}, u32[]{:S(2)}, u32[]{:S(2)}) collective-permute-start(bf16[256,1024]{1,0:T(8,128)(2,1)} %copy-done.8), channel_id=1, source_target_pairs={{0,4},{4,8},{8,12},{12,0},{1,5},{5,9},{9,13},{13,1},{2,6},{6,10},{... | collective-permute-start | bytes 1572872 | tf_op jit(solution)/shard_map/ppermute | solution.py:490
  144.4 22.0 %collective-permute-start.4 = (bf16[256,1024]{1,0:T(8,128)(2,1)}, bf16[256,1024]{1,0:T(8,128)(2,1)S(1)}, u32[]{:S(2)}, u32[]{:S(2)}) collective-permute-start(bf16[256,1024]{1,0:T(8,128)(2,1)} %copy-done.7), channel_id=1, source_target_pairs={{0,8},{4,12},{8,0},{12,4},{1,9},{5,13},{9,1},{13,5},{2,10},{6,14},... | collective-permute-start | bytes 1572872 | tf_op jit(solution)/shard_map/ppermute | solution.py:490
  147.3 19.1 %collective-permute-start.5 = (bf16[256,1024]{1,0:T(8,128)(2,1)}, bf16[256,1024]{1,0:T(8,128)(2,1)S(1)}, u32[]{:S(2)}, u32[]{:S(2)}) collective-permute-start(bf16[256,1024]{1,0:T(8,128)(2,1)} %copy-done.6), channel_id=1, source_target_pairs={{0,12},{4,0},{8,4},{12,8},{1,13},{5,1},{9,5},{13,9},{2,14},{6,2},{... | collective-permute-start | bytes 1572872 | tf_op jit(solution)/shard_map/ppermute | solution.py:490
  148.6 1.4 collective-permute-start.8
  148.6 3.1 %collective-permute-start.7 = (f32[16,128]{1,0:T(8,128)S(1)}, f32[16,128]{1,0:T(8,128)S(1)}, u32[]{:S(2)}, u32[]{:S(2)}) collective-permute-start(f32[16,128]{1,0:T(8,128)S(1)} %get-tuple-element.58), channel_id=1, source_target_pairs={{0,1},{1,2},{2,3},{3,0},{4,5},{5,6},{6,7},{7,4},{8,9},{9,10},{10,1... | collective-permute-start | bytes 24584 | tf_op jit(solution)/shard_map/ppermute | solution.py:496
  150.0 3.7 %collective-permute-start.6 = (f32[16,128]{1,0:T(8,128)S(1)}, f32[16,128]{1,0:T(8,128)S(1)}, u32[]{:S(2)}, u32[]{:S(2)}) collective-permute-start(f32[16,128]{1,0:T(8,128)S(1)} %get-tuple-element.58), channel_id=1, source_target_pairs={{0,2},{1,3},{2,0},{3,1},{4,6},{5,7},{6,4},{7,5},{8,10},{9,11},{10,... | collective-permute-start | bytes 24584 | tf_op jit(solution)/shard_map/ppermute | solution.py:496
  153.6 5.2 %collective-permute-start.9 = (f32[16,128]{1,0:T(8,128)S(1)}, f32[16,128]{1,0:T(8,128)S(1)}, u32[]{:S(2)}, u32[]{:S(2)}) collective-permute-start(f32[16,128]{1,0:T(8,128)S(1)} %add_add_fusion), channel_id=1, source_target_pairs={{0,16},{16,0},{32,48},{48,32},{64,80},{80,64},{96,112},{112,96},{1... | collective-permute-start | bytes 24584 | tf_op jit(solution)/shard_map/ppermute | solution.py:482
